TPU v7x, 256 devices: a whole 4x4x8 slice. The times are simulated.
256 devices in a mesh: depth: 8 (over z), row: 4 (over y), col: 8 (over x, core).
Axes of the slice: x: 4, y: 4, z: 8, core: 2. Of those that a mesh axis runs over, the one named last changes fastest.
Arguments:
- a_tiles: bfloat16 [128, 40, 128, 128], P('row', 'depth', 'col'), may hold values from -6 to 6
- a_kcol: int32 [128, 40], P('row', 'depth'), may hold values from 0 to 15, as said below
- b_tiles: bfloat16 [128, 64, 128, 128], P('depth', 'col', 'row'), may hold values from -0.125 to 0.125
- b_jcol: int32 [128, 64], P('depth', 'col'), may hold values from 0 to 15, as said below
- c_jcol: int32 [128, 64], P('row', 'col'), may hold values from 0 to 15, as said below
- c_place: int32 [128, 64], P('row', 'col'), may hold values from 0 to 255, as said below
Outputs:
- c_owned: float32 [8192, 128, 128], P(('depth', 'row', 'col'))
Inputs may be any that keep to these rules, and one draw needn't show every extreme that they name: Within one block row and one layer, the 5 entries a_kcol[i, d * 5 + s] are distinct. Within one block row and one column group, the 8 entries b_jcol[k, g * 8 + u] are distinct. Within one block row and one column group, the 8 entries c_jcol[i, g * 8 + v] are distinct. Over the kept blocks that share i // 32 and t // 8, c_place takes each value from 0 to 255 once.
All inputs are finite; a program needn't handle non-finite values.
Results may differ from a plain program's by a relative error of at most 0.0003.
Values may be sent and summed in bfloat16 or wider, within the bound.
No kernel may reach another device: no remote copies, remote signals or barrier semaphores. Data moves between devices by JAX's collectives and lax.ppermute only.
A program may use at most 128 MiB of HBM per device.

v0:
```python
import jax
import jax.numpy as jnp
from jax import lax
from jax.sharding import PartitionSpec as P


def select_blocks(a_kcol, b_jcol, c_jcol):
    k_rows, b_count = b_jcol.shape
    k_ids = jnp.arange(k_rows, dtype=jnp.int32)
    onehot_k = (a_kcol[:, :, None] == k_ids[None, None, :]).astype(jnp.int32)
    tile_cols = jnp.sum(onehot_k[:, :, :, None] * b_jcol[None, None, :, :], axis=2)
    matches = tile_cols[:, None, :, :] == c_jcol[:, :, None, None]
    slot_ids = jnp.arange(b_count, dtype=jnp.int32)
    chosen = jnp.sum(jnp.where(matches, slot_ids[None, None, None, :], 0), axis=3)
    located = jnp.any(matches, axis=3)
    flat_index = a_kcol[:, None, :] * b_count + chosen
    return jnp.where(located, flat_index, k_rows * b_count)


def tile_products(a_part, b_part, b_pick):
    k_rows, b_count, piece_rows, tile_width = b_part.shape
    padded = jnp.concatenate(
        [
            b_part.reshape(k_rows * b_count, piece_rows, tile_width),
            jnp.zeros((1, piece_rows, tile_width), b_part.dtype),
        ],
        axis=0,
    )
    row_count = a_part.shape[0]
    block_count = row_count // 4
    a_blocks = a_part.reshape((block_count, 4) + a_part.shape[1:])
    pick_blocks = b_pick.reshape((block_count, 4) + b_pick.shape[1:])

    def one_block(blk_pair):
        a_block, pick_block = blk_pair
        stacked = padded[pick_block]
        return jnp.einsum("iaxy,itayz->itxz", a_block, stacked, preferred_element_type=jnp.float32)

    products = lax.map(one_block, (a_blocks, pick_blocks))
    return products.reshape((row_count,) + products.shape[2:])


def per_device(a_tiles, a_kcol, b_tiles, b_jcol, c_jcol, c_place):
    a_whole = lax.all_gather(a_tiles, "col", axis=2, tiled=True)
    b_pick = select_blocks(a_kcol, b_jcol, c_jcol)
    row_count, c_count = c_jcol.shape
    tile_width = a_whole.shape[3]
    b_whole = lax.all_gather(b_tiles, "row", axis=2, tiled=True)
    tile_sum = tile_products(a_whole, b_whole, b_pick)
    tile_count = row_count * c_count
    place_flat = c_place.reshape(tile_count)
    targets = jnp.arange(tile_count, dtype=jnp.int32)
    send_order = jnp.sum(
        jnp.where(place_flat[None, :] == targets[:, None], targets[None, :], 0), axis=1
    )
    outgoing = tile_sum.reshape(tile_count, tile_width, tile_width)[send_order]
    depth_size = lax.axis_size("depth")
    col_size = lax.axis_size("col")
    capacity = tile_count // (depth_size * col_size)
    grouped = outgoing.reshape(depth_size * col_size, capacity, tile_width, tile_width)
    arrived = lax.all_to_all(grouped, ("depth", "col"), split_axis=0, concat_axis=0, tiled=True)
    return jnp.sum(arrived.reshape(depth_size, col_size * capacity, tile_width, tile_width), axis=0)


def solution(mesh):
    return jax.shard_map(
        per_device,
        mesh=mesh,
        in_specs=(
            P("row", "depth", "col", None),
            P("row", "depth"),
            P("depth", "col", "row", None),
            P("depth", "col"),
            P("row", "col"),
            P("row", "col"),
        ),
        out_specs=P(("depth", "row", "col"), None, None),
        check_vma=False,
    )
```

profile of v0, /device:TPU:1, one launch (start us, length us, event | category | flops | bytes accessed | tf_op | source)
XLA Modules:
  0.0 644.4 jit_solution(17048221391989696653)
XLA Ops:
  6.5 0.7 all-gather.3.cloned.1.call-update
  7.3 0.7 all-gather.5.cloned.1.call-update
  8.0 0.8 copy.26
  8.8 0.7 fusion.4
  9.6 0.7 fusion.3
  10.4 0.8 compare_reduce_fusion
  11.2 0.1 copy.27
  11.3 0.7 broadcast_multiply_fusion
  12.1 0.8 copy.30
  12.9 0.1 select_reduce_fusion
  13.1 0.1 add_select_fusion
  13.2 50.6 %all-gather.3.cloned.1.call-done = bf16[16,8,128,128]{3,2,1,0:T(8,128)(2,1)} async-done(((bf16[16,8,32,128]{3,2,1,0:T(8,128)(2,1)}), bf16[16,8,128,128]{3,2,1,0:T(8,128)(2,1)}) %all-gather.3.cloned.1.call-update) | async-done | bytes 4194320 | tf_op jit(solution)/shard_map/all_gather | solution.py:48
  63.8 5.8 concatenate.3
  69.7 39.8 %all-gather.5.cloned.1.call-done = bf16[32,5,128,128]{3,2,1,0:T(8,128)(2,1)} async-done(((bf16[32,5,16,128]{3,2,1,0:T(8,128)(2,1)}), bf16[32,5,128,128]{3,2,1,0:T(8,128)(2,1)}) %all-gather.5.cloned.1.call-update) | async-done | bytes 5242896 | tf_op jit(solution)/shard_map/all_gather | solution.py:44
  109.5 126.4 %while.10 = (s32[]{:T(128)}, f32[8,4,8,128,128]{3,4,2,1,0:T(8,128)}, s32[8,4,8,5]{2,1,0,3:T(4,128)S(1)}, bf16[129,128,128]{2,1,0:T(8,128)(2,1)}, bf16[8,4,5,128,128]{4,3,2,1,0:T(8,128)(2,1)}, /*index=5*/s32[]{:T(128)}) while((s32[]{:T(128)}, f32[8,4,8,128,128]{3,4,2,1,0:T(8,128)}, s32[8,4,8,5]{2,1,0,3:T(4,128)S(1)}, ...), condition=%wide.region_4.5_spmd, body=%wide.region_3.4_spmd.sunk | while | flops 671090176 | bytes 18492744 | solution.py:39
  109.5 0.1 copy.37
  109.6 0.1 reshape.97
  109.7 9.8 %gather_fusion = bf16[160,128,128]{2,1,0:T(8,128)(2,1)} fusion(bf16[129,128,128]{2,1,0:T(8,128)(2,1)} %get-tuple-element.104, s32[1024]{0:T(1024)S(1)} %pad_clamp_fusion.3), kind=kCustom, calls=%fused_computation.clone.1 | custom fusion | bytes 10486400 | tf_op jit(solution)/shard_map/while/body/eval_jaxpr/gather | solution.py:36
  119.5 5.8 bitcast_dynamic-update-slice_fusion.2
  125.3 0.1 copy.37
  125.4 0.1 reshape.97
  125.6 9.8 %gather_fusion = bf16[160,128,128]{2,1,0:T(8,128)(2,1)} fusion(bf16[129,128,128]{2,1,0:T(8,128)(2,1)} %get-tuple-element.104, s32[1024]{0:T(1024)S(1)} %pad_clamp_fusion.3), kind=kCustom, calls=%fused_computation.clone.1 | custom fusion | bytes 10486400 | tf_op jit(solution)/shard_map/while/body/eval_jaxpr/gather | solution.py:36
  135.3 5.8 bitcast_dynamic-update-slice_fusion.2
  141.1 0.1 copy.37
  141.2 0.1 reshape.97
  141.3 9.8 %gather_fusion = bf16[160,128,128]{2,1,0:T(8,128)(2,1)} fusion(bf16[129,128,128]{2,1,0:T(8,128)(2,1)} %get-tuple-element.104, s32[1024]{0:T(1024)S(1)} %pad_clamp_fusion.3), kind=kCustom, calls=%fused_computation.clone.1 | custom fusion | bytes 10486400 | tf_op jit(solution)/shard_map/while/body/eval_jaxpr/gather | solution.py:36
  151.1 5.8 bitcast_dynamic-update-slice_fusion.2
  156.9 0.1 copy.37
  157.0 0.1 reshape.97
  157.1 9.8 %gather_fusion = bf16[160,128,128]{2,1,0:T(8,128)(2,1)} fusion(bf16[129,128,128]{2,1,0:T(8,128)(2,1)} %get-tuple-element.104, s32[1024]{0:T(1024)S(1)} %pad_clamp_fusion.3), kind=kCustom, calls=%fused_computation.clone.1 | custom fusion | bytes 10486400 | tf_op jit(solution)/shard_map/while/body/eval_jaxpr/gather | solution.py:36
  166.9 5.8 bitcast_dynamic-update-slice_fusion.2
  172.7 0.1 copy.37
  172.8 0.1 reshape.97
  173.0 9.8 %gather_fusion = bf16[160,128,128]{2,1,0:T(8,128)(2,1)} fusion(bf16[129,128,128]{2,1,0:T(8,128)(2,1)} %get-tuple-element.104, s32[1024]{0:T(1024)S(1)} %pad_clamp_fusion.3), kind=kCustom, calls=%fused_computation.clone.1 | custom fusion | bytes 10486400 | tf_op jit(solution)/shard_map/while/body/eval_jaxpr/gather | solution.py:36
  182.7 5.9 bitcast_dynamic-update-slice_fusion.2
  188.7 0.1 reshape.97
  188.8 9.8 %gather_fusion = bf16[160,128,128]{2,1,0:T(8,128)(2,1)} fusion(bf16[129,128,128]{2,1,0:T(8,128)(2,1)} %get-tuple-element.104, s32[1024]{0:T(1024)S(1)} %pad_clamp_fusion.3), kind=kCustom, calls=%fused_computation.clone.1 | custom fusion | bytes 10486400 | tf_op jit(solution)/shard_map/while/body/eval_jaxpr/gather | solution.py:36
  198.6 5.8 bitcast_dynamic-update-slice_fusion.2
  204.4 0.1 reshape.97
  204.6 9.8 %gather_fusion = bf16[160,128,128]{2,1,0:T(8,128)(2,1)} fusion(bf16[129,128,128]{2,1,0:T(8,128)(2,1)} %get-tuple-element.104, s32[1024]{0:T(1024)S(1)} %pad_clamp_fusion.3), kind=kCustom, calls=%fused_computation.clone.1 | custom fusion | bytes 10486400 | tf_op jit(solution)/shard_map/while/body/eval_jaxpr/gather | solution.py:36
  214.3 5.8 bitcast_dynamic-update-slice_fusion.2
  220.3 0.1 reshape.97
  220.4 9.8 %gather_fusion = bf16[160,128,128]{2,1,0:T(8,128)(2,1)} fusion(bf16[129,128,128]{2,1,0:T(8,128)(2,1)} %get-tuple-element.104, s32[1024]{0:T(1024)S(1)} %pad_clamp_fusion.3), kind=kCustom, calls=%fused_computation.clone.1 | custom fusion | bytes 10486400 | tf_op jit(solution)/shard_map/while/body/eval_jaxpr/gather | solution.py:36
  230.1 5.8 bitcast_dynamic-update-slice_fusion.2
  235.9 17.7 %gather_fusion.1 = f32[256,128,128]{1,2,0:T(8,128)} fusion(f32[256,128,128]{1,2,0:T(8,128)} %bitcast.47, s32[1024]{0:T(1024)S(1)} %pad_clamp_fusion.1), kind=kCustom, calls=%fused_computation.1 | custom fusion | bytes 33555456 | tf_op jit(solution)/shard_map/gather | solution.py:56
  253.6 374.4 %all_to_all.5 = f32[64,4,128,128]{2,3,1,0:T(8,128)} all-to-all(f32[64,4,128,128]{2,3,1,0:T(8,128)} %bitcast.45), channel_id=1, replica_groups=mesh['depth'=8,'row'=4,'col'=8] {'depth','col'}, dimensions={0} | all-to-all | bytes 33554432 | tf_op jit(solution)/shard_map/all_to_all | solution.py:61
  628.0 7.8 %bitcast_reduce_fusion = f32[32,128,128]{1,2,0:T(8,128)S(1)} fusion(f32[8,32,128,128]{2,3,1,0:T(8,128)} %bitcast.46), kind=kLoop, calls=%fused_computation.9 | loop fusion | flops 3670016 | bytes 18874368 | tf_op jit(solution)/shard_map/reduce_sum | solution.py:62
  635.8 1.8 copy.31
  (36 shorter events, 0.8 us)
Async XLA Ops:
  6.5 57.3 %all-gather.3.cloned.1.call-start = ((), (), s32[]{:S(2)}) async-start(), calls=%async_computation.1 | async-start | bytes 5242880 | tf_op jit(solution)/shard_map/all_gather | solution.py:48
  7.3 102.2 %all-gather.5.cloned.1.call-start = ((), (), s32[]{:S(2)}) async-start(), calls=%async_computation.2 | async-start | bytes 5898240 | tf_op jit(solution)/shard_map/all_gather | solution.py:44
Sparse Core Ops, SparseCore 0:
  9.2 54.5 all-gather.2
  65.6 43.8 all-gather.4
where the time goes:
time: 646 us; the launch traced here: 644 us
  blocking collectives  374 us (58%)
  local copies, waits for them, and re-layouts  107 us (17%)
  waiting for transfers between devices  91.9 us (14%)
  matrix products  46.4 us (7%)
  between operations  13.5 us (2%)
  other arithmetic  11.1 us (2%)
    all_to_all x1, blocking collectives, per_device(): lax.all_to_all(grouped, ('depth', 'col'), split_axis=0, concat_axis=0, ti...  374 us
    gather x8, local copies, waits for them, and re-layouts, one_block(): stacked = padded[pick_block]  78.1 us
    all_gather x1, waiting for transfers between devices, per_device(): b_whole = lax.all_gather(b_tiles, 'row', axis=2, tiled=True)  50.6 us
    dot_general x8, matrix products, one_block(): jnp.einsum('iaxy,itayz->itxz', a_block, stacked, preferred_element_type=j...  46.4 us
    all_gather x1, waiting for transfers between devices, per_device(): a_whole = lax.all_gather(a_tiles, 'col', axis=2, tiled=True)  39.8 us
    gather x1, local copies, waits for them, and re-layouts, per_device(): outgoing = tile_sum.reshape(tile_count, tile_width, tile_width)[send_order]  17.7 us
  transfers between devices with their start and end apart: 2, of which 2 were waited for; matrix products, arithmetic and copies ran while one was open for 2% of the time, Pallas kernels for 0%

commit v1 on v0

v1 whole, which is shorter than its diff:
```python
import functools

import jax
import jax.numpy as jnp
from jax import lax
from jax.experimental import pallas as pl
from jax.experimental.pallas import tpu as pltpu
from jax.sharding import PartitionSpec as P

F32 = jnp.float32
I16 = jnp.int16
BF16 = jnp.bfloat16
VM = pltpu.VMEM
TOP = 32767.0
FINE = 128.0
TINY = 2.0**-110
TILE = 128
PART = 8
SUB = 16
ROWS = SUB * TILE
HALF_ROWS = PART * TILE
CODE_ROWS = 16


def select_blocks(a_kcol, b_jcol, c_jcol):
    k_rows, b_count = b_jcol.shape
    k_ids = jnp.arange(k_rows, dtype=jnp.int32)
    onehot_k = (a_kcol[:, :, None] == k_ids[None, None, :]).astype(jnp.int32)
    tile_cols = jnp.sum(onehot_k[:, :, :, None] * b_jcol[None, None, :, :], axis=2)
    matches = tile_cols[:, None, :, :] == c_jcol[:, :, None, None]
    slot_ids = jnp.arange(b_count, dtype=jnp.int32)
    chosen = jnp.sum(jnp.where(matches, slot_ids[None, None, None, :], 0), axis=3)
    located = jnp.any(matches, axis=3)
    flat_index = a_kcol[:, None, :] * b_count + chosen
    return jnp.where(located, flat_index, k_rows * b_count)


def make_table(a_kcol, b_jcol, c_jcol, c_place):
    picks = select_blocks(a_kcol, b_jcol, c_jcol)
    rows, kept, slots = picks.shape
    row_ids = jnp.broadcast_to(jnp.arange(rows, dtype=jnp.int32)[:, None, None], (rows, kept, 1))
    fields = jnp.concatenate([row_ids, picks], axis=2).reshape(rows * kept, slots + 1)
    q = jnp.arange(rows * kept, dtype=jnp.int32)
    target = q // 32 * 32 + q % 8 * 4 + q // 8 % 4
    hit = c_place.reshape(1, rows * kept) == target[:, None]
    table = jnp.sum(jnp.where(hit[:, :, None], fields[None], 0), axis=1)
    return table.reshape(rows * kept * (slots + 1))


def assemble_kernel(pos, a0, ap, al, ar, alp, arp, a2, a3, a2p, a3p, b0, bl, br, b2, b3, a_out, b_out, sem):
    row = pos[1]
    col = pos[2]
    other = col + 1 - 2 * (col % 2)
    half_a = a2.shape[0]
    half_b = b2.shape[0]
    count_a, count_b = a0.shape[0], b0.shape[0]

    def a_rows(c, lo, n):
        return a_out.at[pl.ds(lo, n), pl.ds(pl.multiple_of(c % 8 * 16, 16), 16), :]

    def b_rows(r, lo, n):
        return b_out.at[pl.ds(lo, n), pl.ds(pl.multiple_of(r % 4 * 32, 16), 32), :]

    copies = [
        (a0, a_rows(col, 0, count_a)),
        (ap, a_rows(other, 0, count_a)),
        (al, a_rows(col + 6, 0, count_a)),
        (ar, a_rows(col + 2, 0, count_a)),
        (alp, a_rows(other + 6, 0, count_a)),
        (arp, a_rows(other + 2, 0, count_a)),
        (a2, a_rows(col + 4, 0, half_a)),
        (a3, a_rows(col + 4, half_a, half_a)),
        (a2p, a_rows(other + 4, 0, half_a)),
        (a3p, a_rows(other + 4, half_a, half_a)),
        (b0, b_rows(row, 0, count_b)),
        (bl, b_rows(row + 3, 0, count_b)),
        (br, b_rows(row + 1, 0, count_b)),
        (b2, b_rows(row + 2, 0, half_b)),
        (b3, b_rows(row + 2, half_b, half_b)),
    ]
    started = [pltpu.make_async_copy(src, dst, sem.at[n]) for n, (src, dst) in enumerate(copies)]
    for one in started:
        one.start()
    b_out[count_b] = jnp.zeros(b_out.shape[1:], BF16)
    for one in started:
        one.wait()


def own_sum(tab, a, b, q):
    base = q * 6
    i = tab[base]
    left = jnp.concatenate([a[i * 5 + s] for s in range(5)], axis=1)
    right = jnp.concatenate([b[tab[base + 1 + s]] for s in range(5)], axis=0)
    return jnp.dot(left, right, preferred_element_type=F32)


def read_codes(ref, row, scale):
    codes = ref[pl.ds(row, CODE_ROWS), :].astype(jnp.int32).astype(F32)
    scale[...] = jnp.exp2(codes * (1.0 / FINE)) * (1.0 / TOP)


def decoded(ref, scale, t):
    rows = ref[pl.ds(pl.multiple_of(t * TILE, TILE), TILE), :]
    return rows.astype(jnp.int32).astype(F32) * scale[pl.ds(t, 1), :]


def encode(acc, out, row, codes, t):
    top = jnp.maximum(jnp.max(jnp.abs(acc), axis=0, keepdims=True), TINY)
    code = jnp.ceil(jnp.log2(top) * FINE) + 1.0
    codes[pl.ds(t, 1), :] = code
    quant = jnp.round(acc * (jnp.exp2(code * (-1.0 / FINE)) * TOP))
    out[pl.ds(row, TILE), :] = quant.astype(jnp.int32).astype(I16)


def write_codes(codes, out, row):
    out[pl.ds(row, CODE_ROWS), :] = codes[...].astype(jnp.int32).astype(I16)


def first_kernel(h, pos, tab, a, b, out_r, out_l, code_r, code_l):
    base = (pos[0] + 4) % 8 * 32 + h * SUB
    code_r[...] = jnp.zeros_like(code_r)
    code_l[...] = jnp.zeros_like(code_l)

    def body(g, carry):
        for u in range(2):
            t = g * 2 + u
            row = pl.multiple_of(t * TILE, TILE)
            encode(own_sum(tab, a, b, base + t), out_r, row, code_r, t)
            encode(own_sum(tab, a, b, base + PART + t), out_l, row, code_l, t)
        return carry

    lax.fori_loop(0, PART // 2, body, 0)
    write_codes(code_r, out_r, HALF_ROWS)
    write_codes(code_l, out_l, HALF_ROWS)


def second_kernel(h, pos, tab, a, b, in_r, in_l, out_r, out_l, code_r, code_l, scale_r, scale_l):
    base_r = (pos[0] + 3) % 8 * 32 + h * SUB
    base_l = (pos[0] + 5) % 8 * 32 + h * SUB
    read_codes(in_r, HALF_ROWS, scale_r)
    read_codes(in_l, HALF_ROWS, scale_l)

    def body(t, carry):
        row = pl.multiple_of(t * TILE, TILE)
        late = pl.multiple_of((t + PART) * TILE, TILE)
        encode(own_sum(tab, a, b, base_r + t) + decoded(in_r, scale_r, t), out_r, row, code_r, t)
        encode(own_sum(tab, a, b, base_r + PART + t), out_r, late, code_r, t + PART)
        encode(own_sum(tab, a, b, base_l + t), out_l, row, code_l, t)
        encode(own_sum(tab, a, b, base_l + PART + t) + decoded(in_l, scale_l, t), out_l, late, code_l, t + PART)
        return carry

    lax.fori_loop(0, PART, body, 0)
    write_codes(code_r, out_r, ROWS)
    write_codes(code_l, out_l, ROWS)


def middle_kernel(h, away, pos, tab, a, b, in_r, in_l, out_r, out_l, code_r, code_l, scale_r, scale_l):
    base_r = (pos[0] + away) % 8 * 32 + h * SUB
    base_l = (pos[0] + 8 - away) % 8 * 32 + h * SUB
    read_codes(in_r, ROWS, scale_r)
    read_codes(in_l, ROWS, scale_l)

    def body(g, carry):
        for u in range(2):
            t = g * 2 + u
            row = pl.multiple_of(t * TILE, TILE)
            encode(own_sum(tab, a, b, base_r + t) + decoded(in_r, scale_r, t), out_r, row, code_r, t)
            encode(own_sum(tab, a, b, base_l + t) + decoded(in_l, scale_l, t), out_l, row, code_l, t)
        return carry

    lax.fori_loop(0, SUB // 2, body, 0)
    write_codes(code_r, out_r, ROWS)
    write_codes(code_l, out_l, ROWS)


def last_kernel(h, pos, tab, a, b, in_r, in_l, out, code, scale_r, scale_l):
    base = pos[0] * 32 + h * SUB
    read_codes(in_r, ROWS, scale_r)
    read_codes(in_l, ROWS, scale_l)
    code[...] = jnp.zeros_like(code)

    def body(oc, carry):
        for ab in range(2):
            t = ab * PART + oc
            acc = own_sum(tab, a, b, base + t) + decoded(in_r, scale_r, t) + decoded(in_l, scale_l, t)
            encode(acc, out.at[oc], ab * TILE, code, ab)
        write_codes(code, out.at[oc], 2 * TILE)
        return carry

    lax.fori_loop(0, PART, body, 0)


def deliver_kernel(one, two, out, scale):
    def body(g, carry):
        for h, src in enumerate((one, two)):
            read_codes(src.at[g], 2 * TILE, scale)
            for ab in range(2):
                rows = src[g, pl.ds(ab * TILE, TILE), :].astype(jnp.int32).astype(F32)
                out[g * 4 + 2 * h + ab] = rows * scale[ab : ab + 1, :]
        return carry

    lax.fori_loop(0, out.shape[0] // 4, body, 0)


SMEM_SPEC = pl.BlockSpec(memory_space=pltpu.SMEM)
VMEM_SPEC = pl.BlockSpec(memory_space=pltpu.VMEM)
ANY_SPEC = pl.BlockSpec(memory_space=pl.ANY)


def params(mib):
    return pltpu.CompilerParams(vmem_limit_bytes=mib * 2**20)


def cost(tiles, bytes_accessed):
    return pl.CostEstimate(flops=tiles * 5 * 2 * TILE**3, bytes_accessed=bytes_accessed, transcendentals=0)


def scratch(count):
    return [pltpu.VMEM((CODE_ROWS, TILE), F32)] * count


def message(rows):
    return jax.ShapeDtypeStruct((rows + CODE_ROWS, TILE), I16)


def step(kernel, name, tiles, out_shape, scratches, *args):
    ins = [SMEM_SPEC, SMEM_SPEC] + [VMEM_SPEC] * (len(args) - 2)
    return pl.pallas_call(
        kernel,
        out_shape=out_shape,
        in_specs=ins,
        out_specs=jax.tree.map(lambda _: VMEM_SPEC, out_shape),
        scratch_shapes=scratch(scratches),
        compiler_params=params(16),
        cost_estimate=cost(tiles, 2**22),
        name=name,
    )(*args)


def deliver(one, two, tiles):
    return pl.pallas_call(
        deliver_kernel,
        out_shape=jax.ShapeDtypeStruct((tiles, TILE, TILE), F32),
        in_specs=[VMEM_SPEC] * 2,
        out_specs=VMEM_SPEC,
        scratch_shapes=scratch(1),
        compiler_params=params(16),
        cost_estimate=cost(0, 2**22),
        name="deliver",
    )(one, two)


def per_device(a_tiles, a_kcol, b_tiles, b_jcol, c_jcol, c_place):
    depth, row, col = (lax.axis_size(n) for n in ("depth", "row", "col"))

    def shift(axis, size, by):
        pairs = [(i, (i + by) % size) for i in range(size)]
        return lambda x: lax.ppermute(x, axis, pairs)

    y_up, y_down = shift("row", row, 1), shift("row", row, -1)
    x_up, x_down = shift("col", col, 2), shift("col", col, -2)
    z_up, z_down = shift("depth", depth, 1), shift("depth", depth, -1)

    def swap(x):
        return lax.ppermute(x, "col", [(i, i ^ 1) for i in range(col)])

    pos = jnp.stack([lax.axis_index(n) for n in ("depth", "row", "col")]).astype(jnp.int32)
    b0 = b_tiles.reshape((-1,) + b_tiles.shape[2:])
    a0 = a_tiles.reshape((-1,) + a_tiles.shape[2:])
    half_b, half_a = b0.shape[0] // 2, a0.shape[0] // 2
    bl, br = y_up(b0), y_down(b0)
    al, ar = x_up(a0), x_down(a0)
    ap = swap(a0)
    b2, b3 = y_up(bl[:half_b]), y_down(br[half_b:])
    a2, a3 = x_up(al[:half_a]), x_down(ar[half_a:])
    alp, arp, a2p, a3p = swap(al), swap(ar), swap(a2), swap(a3)
    tab = make_table(a_kcol, b_jcol, c_jcol, c_place)
    a, b = pl.pallas_call(
        assemble_kernel,
        out_shape=(VM((a0.shape[0], TILE, TILE), BF16), VM((b0.shape[0] + 1, TILE, TILE), BF16)),
        in_specs=[SMEM_SPEC] + [ANY_SPEC] * 15,
        out_specs=(VMEM_SPEC, VMEM_SPEC),
        scratch_shapes=[pltpu.SemaphoreType.DMA((15,))],
        compiler_params=params(16),
        cost_estimate=cost(0, 9 * 2**20),
        name="assemble",
    )(pos, a0, ap, al, ar, alp, arp, a2, a3, a2p, a3p, b0, bl, br, b2, b3)

    short = (message(HALF_ROWS),) * 2
    full = (message(ROWS),) * 2
    flying = []
    for h in range(2):
        r, l = step(functools.partial(first_kernel, h), f"first{h}", 16, short, 2, pos, tab, a, b)
        flying.append((z_up(r), z_down(l)))
    for hop in range(3):
        landed, flying = flying, []
        for h in range(2):
            if hop == 0:
                kernel, name = functools.partial(second_kernel, h), f"second{h}"
            else:
                kernel, name = functools.partial(middle_kernel, h, 3 - hop), f"middle{hop}{h}"
            r, l = step(kernel, name, 32, full, 4, pos, tab, a, b, *landed[h])
            flying.append((z_up(r), z_down(l)))
    arrived = []
    for h in range(2):
        out = jax.ShapeDtypeStruct((col, 2 * TILE + CODE_ROWS, TILE), I16)
        mine = step(functools.partial(last_kernel, h), f"last{h}", 16, out, 3, pos, tab, a, b, *flying[h])
        arrived.append(lax.all_to_all(mine, "col", split_axis=0, concat_axis=0, tiled=True))
    return deliver(*arrived, col * 4)


def solution(mesh):
    return jax.shard_map(
        per_device,
        mesh=mesh,
        in_specs=(
            P("row", "depth", "col", None),
            P("row", "depth"),
            P("depth", "col", "row", None),
            P("depth", "col"),
            P("row", "col"),
            P("row", "col"),
        ),
        out_specs=P(("depth", "row", "col"), None, None),
        check_vma=False,
    )
```

time: 646 us -> 182 us (0.28)
  blocking collectives: 374 us -> 13.4 us
  local copies, waits for them, and re-layouts: 107 us -> 14 us
  starting transfers between devices: 0.04 us -> 57.4 us
  matrix products: 46.4 us -> 0 us
  Pallas kernels: 0 us -> 37.7 us
  waiting for transfers between devices: 91.9 us -> 55.1 us
  between operations: 13.5 us -> 0.26 us
  other arithmetic: 11.1 us -> 3.47 us
    all_to_all x1, blocking collectives: 374 us -> 13.4 us  [per_device(): lax.all_to_all(mine, 'col', split_axis=0, concat_axis=0, tiled=True)]
    gather x9 -> x0, local copies, waits for them, and re-layouts: 95.8 us -> none  [the longest x8 78.1 us: one_block(): stacked = padded[pick_block]]
    all_gather x2 -> x0, waiting for transfers between devices: 90.5 us -> none  [the longest x1 50.6 us: per_device(): b_whole = lax.all_gather(b_tiles, 'row', axis=2, tiled=True)]
    ppermute x0 -> x29, waiting for transfers between devices: none -> 52.9 us  [the longest x24 51.9 us: shift(): return lambda x: lax.ppermute(x, axis, pairs)]
    ppermute x0 -> x29, starting transfers between devices: none -> 47.2 us  [the longest x24 38.1 us: shift(): return lambda x: lax.ppermute(x, axis, pairs)]
    dot_general x8 -> x0, matrix products: 46.4 us -> none  [one_block(): jnp.einsum('iaxy,itayz->itxz', a_block, stacked, preferred_element_type=j...]
    pallas_call x0 -> x12, Pallas kernels: none -> 37.7 us  [the longest x10 33 us: step(): pl.pallas_call(kernel, out_shape=out_shape, in_specs=ins, out_specs=jax.t...]
    all_to_all x0 -> x1, starting transfers between devices: none -> 10.2 us  [per_device(): lax.all_to_all(mine, 'col', split_axis=0, concat_axis=0, tiled=True)]
  transfers between devices with their start and end apart: 2 -> 30, of which waited for: 2 -> 11; matrix products, arithmetic and copies ran while one was open for 2% -> 5% of each run, Pallas kernels for 0% -> 15%
where the time goes in v1:
time: 182 us; the launch traced here: 181 us
  starting transfers between devices  57.4 us (32%)
  waiting for transfers between devices  55.1 us (30%)
  Pallas kernels  37.7 us (21%)
  local copies, waits for them, and re-layouts  14 us (8%)
  blocking collectives  13.4 us (7%)
  other arithmetic  3.47 us (2%)
    ppermute x24, waiting for transfers between devices, shift(): return lambda x: lax.ppermute(x, axis, pairs)  51.9 us
    ppermute x24, starting transfers between devices, shift(): return lambda x: lax.ppermute(x, axis, pairs)  38.1 us
    pallas_call x10, Pallas kernels, step(): pl.pallas_call(kernel, out_shape=out_shape, in_specs=ins, out_specs=jax.t...  33 us
    all_to_all x1, blocking collectives, per_device(): lax.all_to_all(mine, 'col', split_axis=0, concat_axis=0, tiled=True)  13.4 us
    unnamed x19, local copies, waits for them, and re-layouts  10.2 us
    all_to_all x1, starting transfers between devices, per_device(): lax.all_to_all(mine, 'col', split_axis=0, concat_axis=0, tiled=True)  10.2 us
    ppermute x5, starting transfers between devices, swap(): return lax.ppermute(x, 'col', [(i, i ^ 1) for i in range(col)])  9.08 us
  transfers between devices with their start and end apart: 30, of which 11 were waited for; matrix products, arithmetic and copies ran while one was open for 5% of the time, Pallas kernels for 15%

profile of v1, /device:TPU:1, one launch (start us, length us, event | category | flops | bytes accessed | tf_op | source)
XLA Modules:
  0.0 181.4 jit_solution(1464111966713844363)
XLA Ops:
  0.0 2.1 %collective-permute-start.9 = (bf16[128,32,128]{2,1,0:T(8,128)(2,1)}, bf16[128,32,128]{2,1,0:T(8,128)(2,1)S(1)}, u32[]{:S(2)}, u32[]{:S(2)}) collective-permute-start(bf16[128,32,128]{2,1,0:T(8,128)(2,1)} %bitcast.11), channel_id=1, source_target_pairs={{0,8},{8,16},{16,24},{24,0},{1,9},{9,17},{17,25},{25,1},{2,10},{10... | collective-permute-start | bytes 3145736 | tf_op jit(solution)/shard_map/ppermute | solution.py:258
  2.1 1.4 collective-permute-start.10
  3.6 1.2 collective-permute-start.1
  4.8 1.5 collective-permute-start.2
  6.2 3.5 %collective-permute-start = (bf16[160,16,128]{2,1,0:T(8,128)(2,1)}, bf16[160,16,128]{2,1,0:T(8,128)(2,1)}, u32[]{:S(2)}, u32[]{:S(2)}) collective-permute-start(bf16[160,16,128]{2,1,0:T(8,128)(2,1)} %bitcast.16), channel_id=1, source_target_pairs={{0,1},{1,0},{2,3},{3,2},{4,5},{5,4},{6,7},{7,6},{8,9},{9,8},{10,11... | collective-permute-start | bytes 1966088 | tf_op jit(solution)/shard_map/ppermute | solution.py:265
  12.7 5.6 %collective-permute-done.1.al = bf16[160,16,128]{2,1,0:T(8,128)(2,1)S(1)} collective-permute-done((bf16[160,16,128]{2,1,0:T(8,128)(2,1)}, bf16[160,16,128]{2,1,0:T(8,128)(2,1)S(1)}, u32[]{:S(2)}, u32[]{:S(2)}) %collective-permute-start.1) | collective-permute-done | bytes 655392 | tf_op jit(solution)/shard_map/ppermute | solution.py:258
  19.0 1.5 collective-permute-start.5
  22.1 1.5 collective-permute-start.6
  24.8 2.2 %collective-permute-done.5.a2 = bf16[80,16,128]{2,1,0:T(8,128)(2,1)} collective-permute-done((bf16[80,16,128]{2,1,0:T(8,128)(2,1)}, bf16[80,16,128]{2,1,0:T(8,128)(2,1)}, u32[]{:S(2)}, u32[]{:S(2)}) %collective-permute-start.5) | collective-permute-done | bytes 327712 | tf_op jit(solution)/shard_map/ppermute | solution.py:258
  27.0 4.5 %collective-permute-start.3 = (bf16[160,16,128]{2,1,0:T(8,128)(2,1)S(1)}, bf16[160,16,128]{2,1,0:T(8,128)(2,1)}, u32[]{:S(2)}, u32[]{:S(2)}) collective-permute-start(bf16[160,16,128]{2,1,0:T(8,128)(2,1)S(1)} %collective-permute-done.1.al), channel_id=1, source_target_pairs={{0,1},{1,0},{2,3},{3,2},{4,5},{5,4},{6,7},{7,6},{8,9},{9,8},{10,11... | collective-permute-start | bytes 1966088 | tf_op jit(solution)/shard_map/ppermute | solution.py:265
  34.5 1.9 %collective-permute-start.12 = (bf16[64,32,128]{2,1,0:T(8,128)(2,1)}, bf16[64,32,128]{2,1,0:T(8,128)(2,1)}, u32[]{:S(2)}, u32[]{:S(2)}) collective-permute-start(bf16[64,32,128]{2,1,0:T(8,128)(2,1)} %slice.19), channel_id=1, source_target_pairs={{0,24},{8,0},{16,8},{24,16},{1,25},{9,1},{17,9},{25,17},{2,26},{10... | collective-permute-start | bytes 1572872 | tf_op jit(solution)/shard_map/ppermute | solution.py:258
  39.5 9.2 %collective-permute-done.11.b2 = bf16[64,32,128]{2,1,0:T(8,128)(2,1)} collective-permute-done((bf16[64,32,128]{2,1,0:T(8,128)(2,1)}, bf16[64,32,128]{2,1,0:T(8,128)(2,1)}, u32[]{:S(2)}, u32[]{:S(2)}) %collective-permute-start.11) | collective-permute-done | bytes 524320 | tf_op jit(solution)/shard_map/ppermute | solution.py:258
  48.7 1.2 copy-done.4
  49.9 1.1 copy-done.5
  51.0 1.0 copy-done.7
  52.0 3.0 %assemble.1 = (bf16[160,128,128]{2,1,0:T(8,128)(2,1)S(1)}, bf16[129,128,128]{2,1,0:T(8,128)(2,1)S(1)}) custom-call(s32[3]{0:T(128)S(1)} %pad_add_fusion.1.pos, bf16[160,16,128]{2,1,0:T(8,128)(2,1)S(1)} %bitcast.17, bf16[160,16,128]{2,1,0:T(8,128)(2,1)} %collective-permute-done.ap, bf16[160,16,128]{2,1,0:T(8,128)(2,1)S(1)} %collective-permute-done.1.al, ...), custom_call_target="tpu_custom_call" | custom-call | bytes 9437184 | tf_op jit(solution)/shard_map/assemble/pallas_call | solution.py:278
  55.1 2.2 %first1.1 = (s16[1040,128]{1,0:T(8,128)(2,1)S(1)}, s16[1040,128]{1,0:T(8,128)(2,1)S(1)}) custom-call(s32[3]{0:T(128)S(1)} %pad_add_fusion.1.pos, s32[1536]{0:T(1024)S(1)} %reshape.130.tab, bf16[160,128,128]{2,1,0:T(8,128)(2,1)S(1)} %get-tuple-element.23.a, bf16[129,128,128]{2,1,0:T(8,128)(2,1)S(1)} %get-tuple-element.24.b), custom_call_target="tpu_custom_call" | custom-call | flops 335544320 | bytes 4194304 | tf_op jit(solution)/shard_map/first1/pallas_call | solution.py:228
  57.2 2.7 %collective-permute-start.21 = (s16[1040,128]{1,0:T(8,128)(2,1)S(1)}, s16[1040,128]{1,0:T(8,128)(2,1)S(1)}, u32[]{:S(2)}, u32[]{:S(2)}) collective-permute-start(s16[1040,128]{1,0:T(8,128)(2,1)S(1)} %get-tuple-element.33), channel_id=1, source_target_pairs={{0,32},{32,64},{64,96},{96,128},{128,160},{160,192},{192,224},{224... | collective-permute-start | bytes 798728 | tf_op jit(solution)/shard_map/ppermute | solution.py:258
  59.9 4.2 %collective-permute-start.22 = (s16[1040,128]{1,0:T(8,128)(2,1)S(1)}, s16[1040,128]{1,0:T(8,128)(2,1)S(1)}, u32[]{:S(2)}, u32[]{:S(2)}) collective-permute-start(s16[1040,128]{1,0:T(8,128)(2,1)S(1)} %get-tuple-element.34), channel_id=1, source_target_pairs={{0,224},{32,0},{64,32},{96,64},{128,96},{160,128},{192,160},{224,1... | collective-permute-start | bytes 798728 | tf_op jit(solution)/shard_map/ppermute | solution.py:258
  64.1 5.6 %collective-permute-done.21.in_r = s16[1040,128]{1,0:T(8,128)(2,1)S(1)} collective-permute-done((s16[1040,128]{1,0:T(8,128)(2,1)S(1)}, s16[1040,128]{1,0:T(8,128)(2,1)S(1)}, u32[]{:S(2)}, u32[]{:S(2)}) %collective-permute-start.21) | collective-permute-done | bytes 266272 | tf_op jit(solution)/shard_map/ppermute | solution.py:258
  69.7 3.7 %second1.1 = (s16[2064,128]{1,0:T(8,128)(2,1)S(1)}, s16[2064,128]{1,0:T(8,128)(2,1)S(1)}) custom-call(s32[3]{0:T(128)S(1)} %pad_add_fusion.1.pos, s32[1536]{0:T(1024)S(1)} %reshape.130.tab, bf16[160,128,128]{2,1,0:T(8,128)(2,1)S(1)} %get-tuple-element.23.a, bf16[129,128,128]{2,1,0:T(8,128)(2,1)S(1)} %get-tuple-element.24.b, ...), custom_call_target="tpu_custom_call" | custom-call | flops 671088640 | bytes 4194304 | tf_op jit(solution)/shard_map/second1/pallas_call | solution.py:228
  73.5 2.7 %collective-permute-start.24 = (s16[2064,128]{1,0:T(8,128)(2,1)S(1)}, s16[2064,128]{1,0:T(8,128)(2,1)S(1)}, u32[]{:S(2)}, u32[]{:S(2)}) collective-permute-start(s16[2064,128]{1,0:T(8,128)(2,1)S(1)} %get-tuple-element.36), channel_id=1, source_target_pairs={{0,224},{32,0},{64,32},{96,64},{128,96},{160,128},{192,160},{224,1... | collective-permute-start | bytes 1585160 | tf_op jit(solution)/shard_map/ppermute | solution.py:258
  76.2 2.2 %first0.1 = (s16[1040,128]{1,0:T(8,128)(2,1)S(1)}, s16[1040,128]{1,0:T(8,128)(2,1)S(1)}) custom-call(s32[3]{0:T(128)S(1)} %pad_add_fusion.1.pos, s32[1536]{0:T(1024)S(1)} %reshape.130.tab, bf16[160,128,128]{2,1,0:T(8,128)(2,1)S(1)} %get-tuple-element.23.a, bf16[129,128,128]{2,1,0:T(8,128)(2,1)S(1)} %get-tuple-element.24.b), custom_call_target="tpu_custom_call" | custom-call | flops 335544320 | bytes 4194304 | tf_op jit(solution)/shard_map/first0/pallas_call | solution.py:228
  78.5 2.7 %collective-permute-start.14 = (s16[1040,128]{1,0:T(8,128)(2,1)S(1)}, s16[1040,128]{1,0:T(8,128)(2,1)S(1)}, u32[]{:S(2)}, u32[]{:S(2)}) collective-permute-start(s16[1040,128]{1,0:T(8,128)(2,1)S(1)} %get-tuple-element.26), channel_id=1, source_target_pairs={{0,224},{32,0},{64,32},{96,64},{128,96},{160,128},{192,160},{224,1... | collective-permute-start | bytes 798728 | tf_op jit(solution)/shard_map/ppermute | solution.py:258
  81.2 11.3 %collective-permute-done.13.in_r = s16[1040,128]{1,0:T(8,128)(2,1)S(1)} collective-permute-done((s16[1040,128]{1,0:T(8,128)(2,1)S(1)}, s16[1040,128]{1,0:T(8,128)(2,1)S(1)}, u32[]{:S(2)}, u32[]{:S(2)}) %collective-permute-start.13) | collective-permute-done | bytes 266272 | tf_op jit(solution)/shard_map/ppermute | solution.py:258
  92.5 3.6 %second0.1 = (s16[2064,128]{1,0:T(8,128)(2,1)S(1)}, s16[2064,128]{1,0:T(8,128)(2,1)S(1)}) custom-call(s32[3]{0:T(128)S(1)} %pad_add_fusion.1.pos, s32[1536]{0:T(1024)S(1)} %reshape.130.tab, bf16[160,128,128]{2,1,0:T(8,128)(2,1)S(1)} %get-tuple-element.23.a, bf16[129,128,128]{2,1,0:T(8,128)(2,1)S(1)} %get-tuple-element.24.b, ...), custom_call_target="tpu_custom_call" | custom-call | flops 671088640 | bytes 4194304 | tf_op jit(solution)/shard_map/second0/pallas_call | solution.py:228
  96.2 1.0 collective-permute-start.15
  97.1 1.8 collective-permute-start.16
  98.9 3.7 %middle11.1 = (s16[2064,128]{1,0:T(8,128)(2,1)S(1)}, s16[2064,128]{1,0:T(8,128)(2,1)S(1)}) custom-call(s32[3]{0:T(128)S(1)} %pad_add_fusion.1.pos, s32[1536]{0:T(1024)S(1)} %reshape.130.tab, bf16[160,128,128]{2,1,0:T(8,128)(2,1)S(1)} %get-tuple-element.23.a, bf16[129,128,128]{2,1,0:T(8,128)(2,1)S(1)} %get-tuple-element.24.b, ...), custom_call_target="tpu_custom_call" | custom-call | flops 671088640 | bytes 4194304 | tf_op jit(solution)/shard_map/middle11/pallas_call | solution.py:228
  102.7 2.7 %collective-permute-start.26 = (s16[2064,128]{1,0:T(8,128)(2,1)S(1)}, s16[2064,128]{1,0:T(8,128)(2,1)S(1)}, u32[]{:S(2)}, u32[]{:S(2)}) collective-permute-start(s16[2064,128]{1,0:T(8,128)(2,1)S(1)} %get-tuple-element.38), channel_id=1, source_target_pairs={{0,224},{32,0},{64,32},{96,64},{128,96},{160,128},{192,160},{224,1... | collective-permute-start | bytes 1585160 | tf_op jit(solution)/shard_map/ppermute | solution.py:258
  105.3 3.2 %collective-permute-done.15.in_r = s16[2064,128]{1,0:T(8,128)(2,1)S(1)} collective-permute-done((s16[2064,128]{1,0:T(8,128)(2,1)S(1)}, s16[2064,128]{1,0:T(8,128)(2,1)S(1)}, u32[]{:S(2)}, u32[]{:S(2)}) %collective-permute-start.15) | collective-permute-done | bytes 528416 | tf_op jit(solution)/shard_map/ppermute | solution.py:258
  108.6 3.7 %middle10.1 = (s16[2064,128]{1,0:T(8,128)(2,1)S(1)}, s16[2064,128]{1,0:T(8,128)(2,1)S(1)}) custom-call(s32[3]{0:T(128)S(1)} %pad_add_fusion.1.pos, s32[1536]{0:T(1024)S(1)} %reshape.130.tab, bf16[160,128,128]{2,1,0:T(8,128)(2,1)S(1)} %get-tuple-element.23.a, bf16[129,128,128]{2,1,0:T(8,128)(2,1)S(1)} %get-tuple-element.24.b, ...), custom_call_target="tpu_custom_call" | custom-call | flops 671088640 | bytes 4194304 | tf_op jit(solution)/shard_map/middle10/pallas_call | solution.py:228
  112.8 2.3 %collective-permute-start.18 = (s16[2064,128]{1,0:T(8,128)(2,1)S(1)}, s16[2064,128]{1,0:T(8,128)(2,1)S(1)}, u32[]{:S(2)}, u32[]{:S(2)}) collective-permute-start(s16[2064,128]{1,0:T(8,128)(2,1)S(1)} %get-tuple-element.30), channel_id=1, source_target_pairs={{0,224},{32,0},{64,32},{96,64},{128,96},{160,128},{192,160},{224,1... | collective-permute-start | bytes 1585160 | tf_op jit(solution)/shard_map/ppermute | solution.py:258
  115.1 4.8 %collective-permute-done.25.in_r = s16[2064,128]{1,0:T(8,128)(2,1)S(1)} collective-permute-done((s16[2064,128]{1,0:T(8,128)(2,1)S(1)}, s16[2064,128]{1,0:T(8,128)(2,1)S(1)}, u32[]{:S(2)}, u32[]{:S(2)}) %collective-permute-start.25) | collective-permute-done | bytes 528416 | tf_op jit(solution)/shard_map/ppermute | solution.py:258
  119.9 3.7 %middle21.1 = (s16[2064,128]{1,0:T(8,128)(2,1)S(1)}, s16[2064,128]{1,0:T(8,128)(2,1)S(1)}) custom-call(s32[3]{0:T(128)S(1)} %pad_add_fusion.1.pos, s32[1536]{0:T(1024)S(1)} %reshape.130.tab, bf16[160,128,128]{2,1,0:T(8,128)(2,1)S(1)} %get-tuple-element.23.a, bf16[129,128,128]{2,1,0:T(8,128)(2,1)S(1)} %get-tuple-element.24.b, ...), custom_call_target="tpu_custom_call" | custom-call | flops 671088640 | bytes 4194304 | tf_op jit(solution)/shard_map/middle21/pallas_call | solution.py:228
  124.1 2.2 %collective-permute-start.28 = (s16[2064,128]{1,0:T(8,128)(2,1)S(1)}, s16[2064,128]{1,0:T(8,128)(2,1)S(1)}, u32[]{:S(2)}, u32[]{:S(2)}) collective-permute-start(s16[2064,128]{1,0:T(8,128)(2,1)S(1)} %get-tuple-element.40), channel_id=1, source_target_pairs={{0,224},{32,0},{64,32},{96,64},{128,96},{160,128},{192,160},{224,1... | collective-permute-start | bytes 1585160 | tf_op jit(solution)/shard_map/ppermute | solution.py:258
  126.3 4.9 %collective-permute-done.17.in_r = s16[2064,128]{1,0:T(8,128)(2,1)S(1)} collective-permute-done((s16[2064,128]{1,0:T(8,128)(2,1)S(1)}, s16[2064,128]{1,0:T(8,128)(2,1)S(1)}, u32[]{:S(2)}, u32[]{:S(2)}) %collective-permute-start.17) | collective-permute-done | bytes 528416 | tf_op jit(solution)/shard_map/ppermute | solution.py:258
  131.2 3.7 %middle20.1 = (s16[2064,128]{1,0:T(8,128)(2,1)S(1)}, s16[2064,128]{1,0:T(8,128)(2,1)S(1)}) custom-call(s32[3]{0:T(128)S(1)} %pad_add_fusion.1.pos, s32[1536]{0:T(1024)S(1)} %reshape.130.tab, bf16[160,128,128]{2,1,0:T(8,128)(2,1)S(1)} %get-tuple-element.23.a, bf16[129,128,128]{2,1,0:T(8,128)(2,1)S(1)} %get-tuple-element.24.b, ...), custom_call_target="tpu_custom_call" | custom-call | flops 671088640 | bytes 4194304 | tf_op jit(solution)/shard_map/middle20/pallas_call | solution.py:228
  135.4 2.2 %collective-permute-start.20 = (s16[2064,128]{1,0:T(8,128)(2,1)S(1)}, s16[2064,128]{1,0:T(8,128)(2,1)S(1)}, u32[]{:S(2)}, u32[]{:S(2)}) collective-permute-start(s16[2064,128]{1,0:T(8,128)(2,1)S(1)} %get-tuple-element.32), channel_id=1, source_target_pairs={{0,224},{32,0},{64,32},{96,64},{128,96},{160,128},{192,160},{224,1... | collective-permute-start | bytes 1585160 | tf_op jit(solution)/shard_map/ppermute | solution.py:258
  137.7 4.9 %collective-permute-done.27.in_r = s16[2064,128]{1,0:T(8,128)(2,1)S(1)} collective-permute-done((s16[2064,128]{1,0:T(8,128)(2,1)S(1)}, s16[2064,128]{1,0:T(8,128)(2,1)S(1)}, u32[]{:S(2)}, u32[]{:S(2)}) %collective-permute-start.27) | collective-permute-done | bytes 528416 | tf_op jit(solution)/shard_map/ppermute | solution.py:258
  142.6 3.7 %last1.1 = s16[8,272,128]{2,1,0:T(8,128)(2,1)} custom-call(s32[3]{0:T(128)S(1)} %pad_add_fusion.1.pos, s32[1536]{0:T(1024)S(1)} %reshape.130.tab, bf16[160,128,128]{2,1,0:T(8,128)(2,1)S(1)} %get-tuple-element.23.a, bf16[129,128,128]{2,1,0:T(8,128)(2,1)S(1)} %get-tuple-element.24.b, s16[2064,128]{1,0:T(8,128)(2,1)S(1)} %collective-permute-done.27.in_r, ...), custom_call_target="tpu_custom_call" | custom-call | flops 335544320 | bytes 4194304 | tf_op jit(solution)/shard_map/last1/pallas_call | solution.py:228
  146.3 10.2 %all-to-all-start.1 = ((s16[8,272,128]{2,1,0:T(8,128)(2,1)}), s16[8,272,128]{2,1,0:T(8,128)(2,1)S(1)}, u32[]{:S(2)}, u32[]{:S(2)}) async-start(s16[8,272,128]{2,1,0:T(8,128)(2,1)} %last1.1), calls=%async_computation.1 | async-start | bytes 1114112 | tf_op jit(solution)/shard_map/all_to_all | solution.py:308
  156.5 2.5 %copy-done.1 = bf16[160,128,128]{2,1,0:T(8,128)(2,1)S(1)} copy-done((bf16[160,128,128]{2,1,0:T(8,128)(2,1)S(1)}, bf16[160,128,128]{2,1,0:T(8,128)(2,1)}, u32[]{:S(2)}) %copy-start.1) | copy-done | bytes 5242904
  159.0 2.2 %copy-done.3 = bf16[129,128,128]{2,1,0:T(8,128)(2,1)S(1)} copy-done((bf16[129,128,128]{2,1,0:T(8,128)(2,1)S(1)}, bf16[129,128,128]{2,1,0:T(8,128)(2,1)}, u32[]{:S(2)}) %copy-start.3) | copy-done | bytes 4227096
  161.2 2.9 %last0.1 = s16[8,272,128]{2,1,0:T(8,128)(2,1)S(1)} custom-call(s32[3]{0:T(128)S(1)} %pad_add_fusion.1.pos, s32[1536]{0:T(1024)S(1)} %reshape.130.tab, bf16[160,128,128]{2,1,0:T(8,128)(2,1)S(1)} %copy-done.1, bf16[129,128,128]{2,1,0:T(8,128)(2,1)S(1)} %copy-done.3, s16[2064,128]{1,0:T(8,128)(2,1)S(1)} %collective-permute-done.19.in_r, ...), custom_call_target="tpu_custom_call" | custom-call | flops 335544320 | bytes 4194304 | tf_op jit(solution)/shard_map/last0/pallas_call | solution.py:228
  164.1 2.2 %all-to-all-done.1.two = s16[8,272,128]{2,1,0:T(8,128)(2,1)S(1)} async-done(((s16[8,272,128]{2,1,0:T(8,128)(2,1)}), s16[8,272,128]{2,1,0:T(8,128)(2,1)S(1)}, u32[]{:S(2)}, u32[]{:S(2)}) %all-to-all-start.1) | async-done | bytes 557088 | tf_op jit(solution)/shard_map/all_to_all | solution.py:308
  166.4 13.4 %all_to_all.10.one = s16[8,272,128]{2,1,0:T(8,128)(2,1)S(1)} all-to-all(s16[8,272,128]{2,1,0:T(8,128)(2,1)S(1)} %last0.1), channel_id=1, replica_groups=mesh['depth'=8,'row'=4,'col'=8] {'col'}, dimensions={0} | all-to-all | bytes 1114112 | tf_op jit(solution)/shard_map/all_to_all | solution.py:308
  179.8 1.7 deliver.1
  (66 shorter events, 14.2 us)
Async XLA Ops:
  0.0 31.5 %collective-permute-start.9 = (bf16[128,32,128]{2,1,0:T(8,128)(2,1)}, bf16[128,32,128]{2,1,0:T(8,128)(2,1)S(1)}, u32[]{:S(2)}, u32[]{:S(2)}) collective-permute-start(bf16[128,32,128]{2,1,0:T(8,128)(2,1)} %bitcast.11), channel_id=1, source_target_pairs={{0,8},{8,16},{16,24},{24,0},{1,9},{9,17},{17,25},{25,1},{2,10},{10... | collective-permute-start | bytes 3145736 | tf_op jit(solution)/shard_map/ppermute | solution.py:258
  2.1 29.4 %collective-permute-start.10 = (bf16[128,32,128]{2,1,0:T(8,128)(2,1)}, bf16[128,32,128]{2,1,0:T(8,128)(2,1)S(1)}, u32[]{:S(2)}, u32[]{:S(2)}) collective-permute-start(bf16[128,32,128]{2,1,0:T(8,128)(2,1)} %bitcast.12), channel_id=1, source_target_pairs={{0,24},{8,0},{16,8},{24,16},{1,25},{9,1},{17,9},{25,17},{2,26},{10... | collective-permute-start | bytes 3145736 | tf_op jit(solution)/shard_map/ppermute | solution.py:258
  3.6 14.7 %collective-permute-start.1 = (bf16[160,16,128]{2,1,0:T(8,128)(2,1)}, bf16[160,16,128]{2,1,0:T(8,128)(2,1)S(1)}, u32[]{:S(2)}, u32[]{:S(2)}) collective-permute-start(bf16[160,16,128]{2,1,0:T(8,128)(2,1)} %bitcast.14), channel_id=1, source_target_pairs={{0,2},{1,3},{2,4},{3,5},{4,6},{5,7},{6,0},{7,1},{8,10},{9,11},{10,... | collective-permute-start | bytes 1966088 | tf_op jit(solution)/shard_map/ppermute | solution.py:258
  4.8 16.5 %collective-permute-start.2 = (bf16[160,16,128]{2,1,0:T(8,128)(2,1)}, bf16[160,16,128]{2,1,0:T(8,128)(2,1)S(1)}, u32[]{:S(2)}, u32[]{:S(2)}) collective-permute-start(bf16[160,16,128]{2,1,0:T(8,128)(2,1)} %bitcast.15), channel_id=1, source_target_pairs={{0,6},{1,7},{2,0},{3,1},{4,2},{5,3},{6,4},{7,5},{8,14},{9,15},{10,... | collective-permute-start | bytes 1966088 | tf_op jit(solution)/shard_map/ppermute | solution.py:258
  6.2 27.4 %collective-permute-start = (bf16[160,16,128]{2,1,0:T(8,128)(2,1)}, bf16[160,16,128]{2,1,0:T(8,128)(2,1)}, u32[]{:S(2)}, u32[]{:S(2)}) collective-permute-start(bf16[160,16,128]{2,1,0:T(8,128)(2,1)} %bitcast.16), channel_id=1, source_target_pairs={{0,1},{1,0},{2,3},{3,2},{4,5},{5,4},{6,7},{7,6},{8,9},{9,8},{10,11... | collective-permute-start | bytes 1966088 | tf_op jit(solution)/shard_map/ppermute | solution.py:265
  19.0 8.0 %collective-permute-start.5 = (bf16[80,16,128]{2,1,0:T(8,128)(2,1)}, bf16[80,16,128]{2,1,0:T(8,128)(2,1)}, u32[]{:S(2)}, u32[]{:S(2)}) collective-permute-start(bf16[80,16,128]{2,1,0:T(8,128)(2,1)} %slice.16), channel_id=1, source_target_pairs={{0,2},{1,3},{2,4},{3,5},{4,6},{5,7},{6,0},{7,1},{8,10},{9,11},{10,... | collective-permute-start | bytes 983048 | tf_op jit(solution)/shard_map/ppermute | solution.py:258
  22.1 12.4 %collective-permute-start.6 = (bf16[80,16,128]{2,1,0:T(8,128)(2,1)}, bf16[80,16,128]{2,1,0:T(8,128)(2,1)}, u32[]{:S(2)}, u32[]{:S(2)}) collective-permute-start(bf16[80,16,128]{2,1,0:T(8,128)(2,1)} %slice.17), channel_id=1, source_target_pairs={{0,6},{1,7},{2,0},{3,1},{4,2},{5,3},{6,4},{7,5},{8,14},{9,15},{10,... | collective-permute-start | bytes 983048 | tf_op jit(solution)/shard_map/ppermute | solution.py:258
  27.0 12.4 %collective-permute-start.3 = (bf16[160,16,128]{2,1,0:T(8,128)(2,1)S(1)}, bf16[160,16,128]{2,1,0:T(8,128)(2,1)}, u32[]{:S(2)}, u32[]{:S(2)}) collective-permute-start(bf16[160,16,128]{2,1,0:T(8,128)(2,1)S(1)} %collective-permute-done.1.al), channel_id=1, source_target_pairs={{0,1},{1,0},{2,3},{3,2},{4,5},{5,4},{6,7},{7,6},{8,9},{9,8},{10,11... | collective-permute-start | bytes 1966088 | tf_op jit(solution)/shard_map/ppermute | solution.py:265
  31.5 8.0 %collective-permute-start.4 = (bf16[160,16,128]{2,1,0:T(8,128)(2,1)S(1)}, bf16[160,16,128]{2,1,0:T(8,128)(2,1)}, u32[]{:S(2)}, u32[]{:S(2)}) collective-permute-start(bf16[160,16,128]{2,1,0:T(8,128)(2,1)S(1)} %collective-permute-done.2.ar), channel_id=1, source_target_pairs={{0,1},{1,0},{2,3},{3,2},{4,5},{5,4},{6,7},{7,6},{8,9},{9,8},{10,11... | collective-permute-start | bytes 1966088 | tf_op jit(solution)/shard_map/ppermute | solution.py:265
  31.5 5.0 %collective-permute-start.7 = (bf16[80,16,128]{2,1,0:T(8,128)(2,1)}, bf16[80,16,128]{2,1,0:T(8,128)(2,1)S(1)}, u32[]{:S(2)}, u32[]{:S(2)}) collective-permute-start(bf16[80,16,128]{2,1,0:T(8,128)(2,1)} %collective-permute-done.5.a2), channel_id=1, source_target_pairs={{0,1},{1,0},{2,3},{3,2},{4,5},{5,4},{6,7},{7,6},{8,9},{9,8},{10,11... | collective-permute-start | bytes 983048 | tf_op jit(solution)/shard_map/ppermute | solution.py:265
  33.7 15.0 %collective-permute-start.11 = (bf16[64,32,128]{2,1,0:T(8,128)(2,1)}, bf16[64,32,128]{2,1,0:T(8,128)(2,1)}, u32[]{:S(2)}, u32[]{:S(2)}) collective-permute-start(bf16[64,32,128]{2,1,0:T(8,128)(2,1)} %slice.18), channel_id=1, source_target_pairs={{0,8},{8,16},{16,24},{24,0},{1,9},{9,17},{17,25},{25,1},{2,10},{10... | collective-permute-start | bytes 1572872 | tf_op jit(solution)/shard_map/ppermute | solution.py:258
  34.5 14.2 %collective-permute-start.12 = (bf16[64,32,128]{2,1,0:T(8,128)(2,1)}, bf16[64,32,128]{2,1,0:T(8,128)(2,1)}, u32[]{:S(2)}, u32[]{:S(2)}) collective-permute-start(bf16[64,32,128]{2,1,0:T(8,128)(2,1)} %slice.19), channel_id=1, source_target_pairs={{0,24},{8,0},{16,8},{24,16},{1,25},{9,1},{17,9},{25,17},{2,26},{10... | collective-permute-start | bytes 1572872 | tf_op jit(solution)/shard_map/ppermute | solution.py:258
  36.5 0.7 copy-start.6
  37.2 2.2 %collective-permute-start.8 = (bf16[80,16,128]{2,1,0:T(8,128)(2,1)}, bf16[80,16,128]{2,1,0:T(8,128)(2,1)}, u32[]{:S(2)}, u32[]{:S(2)}) collective-permute-start(bf16[80,16,128]{2,1,0:T(8,128)(2,1)} %collective-permute-done.6.a3), channel_id=1, source_target_pairs={{0,1},{1,0},{2,3},{3,2},{4,5},{5,4},{6,7},{7,6},{8,9},{9,8},{10,11... | collective-permute-start | bytes 983048 | tf_op jit(solution)/shard_map/ppermute | solution.py:265
  48.7 1.2 copy-start.4
  49.9 1.1 copy-start.5
  51.0 1.0 copy-start.7
  55.0 87.5 %copy-start = (bf16[160,128,128]{2,1,0:T(8,128)(2,1)}, bf16[160,128,128]{2,1,0:T(8,128)(2,1)S(1)}, u32[]{:S(2)}) copy-start(bf16[160,128,128]{2,1,0:T(8,128)(2,1)S(1)} %get-tuple-element.23.a) | copy-start | bytes 15728644
  55.1 87.5 %copy-start.2 = (bf16[129,128,128]{2,1,0:T(8,128)(2,1)}, bf16[129,128,128]{2,1,0:T(8,128)(2,1)S(1)}, u32[]{:S(2)}) copy-start(bf16[129,128,128]{2,1,0:T(8,128)(2,1)S(1)} %get-tuple-element.24.b) | copy-start | bytes 12681220
  57.2 12.5 %collective-permute-start.21 = (s16[1040,128]{1,0:T(8,128)(2,1)S(1)}, s16[1040,128]{1,0:T(8,128)(2,1)S(1)}, u32[]{:S(2)}, u32[]{:S(2)}) collective-permute-start(s16[1040,128]{1,0:T(8,128)(2,1)S(1)} %get-tuple-element.33), channel_id=1, source_target_pairs={{0,32},{32,64},{64,96},{96,128},{128,160},{160,192},{192,224},{224... | collective-permute-start | bytes 798728 | tf_op jit(solution)/shard_map/ppermute | solution.py:258
  59.9 9.8 %collective-permute-start.22 = (s16[1040,128]{1,0:T(8,128)(2,1)S(1)}, s16[1040,128]{1,0:T(8,128)(2,1)S(1)}, u32[]{:S(2)}, u32[]{:S(2)}) collective-permute-start(s16[1040,128]{1,0:T(8,128)(2,1)S(1)} %get-tuple-element.34), channel_id=1, source_target_pairs={{0,224},{32,0},{64,32},{96,64},{128,96},{160,128},{192,160},{224,1... | collective-permute-start | bytes 798728 | tf_op jit(solution)/shard_map/ppermute | solution.py:258
  73.5 25.5 %collective-permute-start.23 = (s16[2064,128]{1,0:T(8,128)(2,1)S(1)}, s16[2064,128]{1,0:T(8,128)(2,1)S(1)}, u32[]{:S(2)}, u32[]{:S(2)}) collective-permute-start(s16[2064,128]{1,0:T(8,128)(2,1)S(1)} %get-tuple-element.35), channel_id=1, source_target_pairs={{0,32},{32,64},{64,96},{96,128},{128,160},{160,192},{192,224},{224... | collective-permute-start | bytes 1585160 | tf_op jit(solution)/shard_map/ppermute | solution.py:258
  73.5 25.4 %collective-permute-start.24 = (s16[2064,128]{1,0:T(8,128)(2,1)S(1)}, s16[2064,128]{1,0:T(8,128)(2,1)S(1)}, u32[]{:S(2)}, u32[]{:S(2)}) collective-permute-start(s16[2064,128]{1,0:T(8,128)(2,1)S(1)} %get-tuple-element.36), channel_id=1, source_target_pairs={{0,224},{32,0},{64,32},{96,64},{128,96},{160,128},{192,160},{224,1... | collective-permute-start | bytes 1585160 | tf_op jit(solution)/shard_map/ppermute | solution.py:258
  78.4 14.1 %collective-permute-start.13 = (s16[1040,128]{1,0:T(8,128)(2,1)S(1)}, s16[1040,128]{1,0:T(8,128)(2,1)S(1)}, u32[]{:S(2)}, u32[]{:S(2)}) collective-permute-start(s16[1040,128]{1,0:T(8,128)(2,1)S(1)} %get-tuple-element.25), channel_id=1, source_target_pairs={{0,32},{32,64},{64,96},{96,128},{128,160},{160,192},{192,224},{224... | collective-permute-start | bytes 798728 | tf_op jit(solution)/shard_map/ppermute | solution.py:258
  78.5 14.0 %collective-permute-start.14 = (s16[1040,128]{1,0:T(8,128)(2,1)S(1)}, s16[1040,128]{1,0:T(8,128)(2,1)S(1)}, u32[]{:S(2)}, u32[]{:S(2)}) collective-permute-start(s16[1040,128]{1,0:T(8,128)(2,1)S(1)} %get-tuple-element.26), channel_id=1, source_target_pairs={{0,224},{32,0},{64,32},{96,64},{128,96},{160,128},{192,160},{224,1... | collective-permute-start | bytes 798728 | tf_op jit(solution)/shard_map/ppermute | solution.py:258
  96.2 12.4 %collective-permute-start.15 = (s16[2064,128]{1,0:T(8,128)(2,1)S(1)}, s16[2064,128]{1,0:T(8,128)(2,1)S(1)}, u32[]{:S(2)}, u32[]{:S(2)}) collective-permute-start(s16[2064,128]{1,0:T(8,128)(2,1)S(1)} %get-tuple-element.27), channel_id=1, source_target_pairs={{0,32},{32,64},{64,96},{96,128},{128,160},{160,192},{192,224},{224... | collective-permute-start | bytes 1585160 | tf_op jit(solution)/shard_map/ppermute | solution.py:258
  97.1 11.5 %collective-permute-start.16 = (s16[2064,128]{1,0:T(8,128)(2,1)S(1)}, s16[2064,128]{1,0:T(8,128)(2,1)S(1)}, u32[]{:S(2)}, u32[]{:S(2)}) collective-permute-start(s16[2064,128]{1,0:T(8,128)(2,1)S(1)} %get-tuple-element.28), channel_id=1, source_target_pairs={{0,224},{32,0},{64,32},{96,64},{128,96},{160,128},{192,160},{224,1... | collective-permute-start | bytes 1585160 | tf_op jit(solution)/shard_map/ppermute | solution.py:258
  102.6 17.3 %collective-permute-start.25 = (s16[2064,128]{1,0:T(8,128)(2,1)S(1)}, s16[2064,128]{1,0:T(8,128)(2,1)S(1)}, u32[]{:S(2)}, u32[]{:S(2)}) collective-permute-start(s16[2064,128]{1,0:T(8,128)(2,1)S(1)} %get-tuple-element.37), channel_id=1, source_target_pairs={{0,32},{32,64},{64,96},{96,128},{128,160},{160,192},{192,224},{224... | collective-permute-start | bytes 1585160 | tf_op jit(solution)/shard_map/ppermute | solution.py:258
  102.7 17.2 %collective-permute-start.26 = (s16[2064,128]{1,0:T(8,128)(2,1)S(1)}, s16[2064,128]{1,0:T(8,128)(2,1)S(1)}, u32[]{:S(2)}, u32[]{:S(2)}) collective-permute-start(s16[2064,128]{1,0:T(8,128)(2,1)S(1)} %get-tuple-element.38), channel_id=1, source_target_pairs={{0,224},{32,0},{64,32},{96,64},{128,96},{160,128},{192,160},{224,1... | collective-permute-start | bytes 1585160 | tf_op jit(solution)/shard_map/ppermute | solution.py:258
  112.3 18.9 %collective-permute-start.17 = (s16[2064,128]{1,0:T(8,128)(2,1)S(1)}, s16[2064,128]{1,0:T(8,128)(2,1)S(1)}, u32[]{:S(2)}, u32[]{:S(2)}) collective-permute-start(s16[2064,128]{1,0:T(8,128)(2,1)S(1)} %get-tuple-element.29), channel_id=1, source_target_pairs={{0,32},{32,64},{64,96},{96,128},{128,160},{160,192},{192,224},{224... | collective-permute-start | bytes 1585160 | tf_op jit(solution)/shard_map/ppermute | solution.py:258
  112.8 18.4 %collective-permute-start.18 = (s16[2064,128]{1,0:T(8,128)(2,1)S(1)}, s16[2064,128]{1,0:T(8,128)(2,1)S(1)}, u32[]{:S(2)}, u32[]{:S(2)}) collective-permute-start(s16[2064,128]{1,0:T(8,128)(2,1)S(1)} %get-tuple-element.30), channel_id=1, source_target_pairs={{0,224},{32,0},{64,32},{96,64},{128,96},{160,128},{192,160},{224,1... | collective-permute-start | bytes 1585160 | tf_op jit(solution)/shard_map/ppermute | solution.py:258
  123.6 19.0 %collective-permute-start.27 = (s16[2064,128]{1,0:T(8,128)(2,1)S(1)}, s16[2064,128]{1,0:T(8,128)(2,1)S(1)}, u32[]{:S(2)}, u32[]{:S(2)}) collective-permute-start(s16[2064,128]{1,0:T(8,128)(2,1)S(1)} %get-tuple-element.39), channel_id=1, source_target_pairs={{0,32},{32,64},{64,96},{96,128},{128,160},{160,192},{192,224},{224... | collective-permute-start | bytes 1585160 | tf_op jit(solution)/shard_map/ppermute | solution.py:258
  124.1 18.5 %collective-permute-start.28 = (s16[2064,128]{1,0:T(8,128)(2,1)S(1)}, s16[2064,128]{1,0:T(8,128)(2,1)S(1)}, u32[]{:S(2)}, u32[]{:S(2)}) collective-permute-start(s16[2064,128]{1,0:T(8,128)(2,1)S(1)} %get-tuple-element.40), channel_id=1, source_target_pairs={{0,224},{32,0},{64,32},{96,64},{128,96},{160,128},{192,160},{224,1... | collective-permute-start | bytes 1585160 | tf_op jit(solution)/shard_map/ppermute | solution.py:258
  134.9 21.6 %collective-permute-start.19 = (s16[2064,128]{1,0:T(8,128)(2,1)S(1)}, s16[2064,128]{1,0:T(8,128)(2,1)S(1)}, u32[]{:S(2)}, u32[]{:S(2)}) collective-permute-start(s16[2064,128]{1,0:T(8,128)(2,1)S(1)} %get-tuple-element.31), channel_id=1, source_target_pairs={{0,32},{32,64},{64,96},{96,128},{128,160},{160,192},{192,224},{224... | collective-permute-start | bytes 1585160 | tf_op jit(solution)/shard_map/ppermute | solution.py:258
  135.4 21.1 %collective-permute-start.20 = (s16[2064,128]{1,0:T(8,128)(2,1)S(1)}, s16[2064,128]{1,0:T(8,128)(2,1)S(1)}, u32[]{:S(2)}, u32[]{:S(2)}) collective-permute-start(s16[2064,128]{1,0:T(8,128)(2,1)S(1)} %get-tuple-element.32), channel_id=1, source_target_pairs={{0,224},{32,0},{64,32},{96,64},{128,96},{160,128},{192,160},{224,1... | collective-permute-start | bytes 1585160 | tf_op jit(solution)/shard_map/ppermute | solution.py:258
  146.3 20.1 %all-to-all-start.1 = ((s16[8,272,128]{2,1,0:T(8,128)(2,1)}), s16[8,272,128]{2,1,0:T(8,128)(2,1)S(1)}, u32[]{:S(2)}, u32[]{:S(2)}) async-start(s16[8,272,128]{2,1,0:T(8,128)(2,1)} %last1.1), calls=%async_computation.1 | async-start | bytes 1114112 | tf_op jit(solution)/shard_map/all_to_all | solution.py:308
  156.5 2.5 %copy-start.1 = (bf16[160,128,128]{2,1,0:T(8,128)(2,1)S(1)}, bf16[160,128,128]{2,1,0:T(8,128)(2,1)}, u32[]{:S(2)}) copy-start(bf16[160,128,128]{2,1,0:T(8,128)(2,1)} %copy-done) | copy-start | bytes 15728644
  159.0 2.2 %copy-start.3 = (bf16[129,128,128]{2,1,0:T(8,128)(2,1)S(1)}, bf16[129,128,128]{2,1,0:T(8,128)(2,1)}, u32[]{:S(2)}) copy-start(bf16[129,128,128]{2,1,0:T(8,128)(2,1)} %copy-done.2) | copy-start | bytes 12681220

commit v2 on v1

--- a/solution.py
+++ b/solution.py
@@ -47,41 +47,42 @@
     return table.reshape(rows * kept * (slots + 1))
 
 
-def assemble_kernel(pos, a0, ap, al, ar, alp, arp, a2, a3, a2p, a3p, b0, bl, br, b2, b3, a_out, b_out, sem):
-    row = pos[1]
-    col = pos[2]
-    other = col + 1 - 2 * (col % 2)
-    half_a = a2.shape[0]
-    half_b = b2.shape[0]
-    count_a, count_b = a0.shape[0], b0.shape[0]
-
-    def a_rows(c, lo, n):
-        return a_out.at[pl.ds(lo, n), pl.ds(pl.multiple_of(c % 8 * 16, 16), 16), :]
-
-    def b_rows(r, lo, n):
-        return b_out.at[pl.ds(lo, n), pl.ds(pl.multiple_of(r % 4 * 32, 16), 32), :]
-
-    copies = [
-        (a0, a_rows(col, 0, count_a)),
-        (ap, a_rows(other, 0, count_a)),
-        (al, a_rows(col + 6, 0, count_a)),
-        (ar, a_rows(col + 2, 0, count_a)),
-        (alp, a_rows(other + 6, 0, count_a)),
-        (arp, a_rows(other + 2, 0, count_a)),
-        (a2, a_rows(col + 4, 0, half_a)),
-        (a3, a_rows(col + 4, half_a, half_a)),
-        (a2p, a_rows(other + 4, 0, half_a)),
-        (a3p, a_rows(other + 4, half_a, half_a)),
-        (b0, b_rows(row, 0, count_b)),
-        (bl, b_rows(row + 3, 0, count_b)),
-        (br, b_rows(row + 1, 0, count_b)),
-        (b2, b_rows(row + 2, 0, half_b)),
-        (b3, b_rows(row + 2, half_b, half_b)),
-    ]
+def a_place(a_out, col):
+    return a_out.at[:, pl.ds(pl.multiple_of((col + 8) % 8 * 16, 16), 16), :]
+
+
+def b_place(b_out, row, count):
+    return b_out.at[pl.ds(0, count), pl.ds(pl.multiple_of(row % 4 * 32, 32), 32), :]
+
+
+def copy_all(copies, sem):
     started = [pltpu.make_async_copy(src, dst, sem.at[n]) for n, (src, dst) in enumerate(copies)]
     for one in started:
         one.start()
-    b_out[count_b] = jnp.zeros(b_out.shape[1:], BF16)
+    return started
+
+
+def assemble_kernel(pos, a0, ap, p1, p2, p3, s1, s2, s3, b0, q1, t2, a_out, b_out, sem):
+    row, col = pos[1], pos[2]
+    core = col % 2
+    other = col + 1 - 2 * core
+    ahead = 4 * core - 2
+    count = b0.shape[0]
+    copies = [
+        (a0, a_place(a_out, col)),
+        (ap, a_place(a_out, other)),
+        (p1, a_place(a_out, col + ahead)),
+        (p2, a_place(a_out, other + ahead)),
+        (p3, a_place(a_out, col + 4)),
+        (s1, a_place(a_out, other - ahead)),
+        (s2, a_place(a_out, col - ahead)),
+        (s3, a_place(a_out, other + 4)),
+        (b0, b_place(b_out, row, count)),
+        (q1, b_place(b_out, row + 3 + 2 * core, count)),
+        (t2, b_place(b_out, row + 1 + 2 * core, count)),
+    ]
+    started = copy_all(copies, sem)
+    b_out[count] = jnp.zeros(b_out.shape[1:], BF16)
     for one in started:
         one.wait()
 
@@ -114,6 +115,13 @@
 
 def write_codes(codes, out, row):
     out[pl.ds(row, CODE_ROWS), :] = codes[...].astype(jnp.int32).astype(I16)
+
+
+def finish_kernel(pos, tab, a, b_in, q3, out_r, out_l, b, code_r, code_l, sem):
+    late = pltpu.make_async_copy(q3, b_place(b, pos[1] + 2, q3.shape[0]), sem)
+    late.start()
+    late.wait()
+    first_kernel(0, pos, tab, a, b, out_r, out_l, code_r, code_l)
 
 
 def first_kernel(h, pos, tab, a, b, out_r, out_l, code_r, code_l):
@@ -173,21 +181,31 @@
     write_codes(code_l, out_l, ROWS)
 
 
-def last_kernel(h, pos, tab, a, b, in_r, in_l, out, code, scale_r, scale_l):
-    base = pos[0] * 32 + h * SUB
+def own_kernel(pos, tab, a, b, own):
+    def body(g, carry):
+        for u in range(4):
+            own[g * 4 + u] = own_sum(tab, a, b, pos[0] * 32 + g * 4 + u)
+        return carry
+
+    lax.fori_loop(0, own.shape[0] // 4, body, 0)
+
+
+def last_kernel(h, own, in_r, in_l, out, code, scale_r, scale_l):
     read_codes(in_r, ROWS, scale_r)
     read_codes(in_l, ROWS, scale_l)
     code[...] = jnp.zeros_like(code)
 
-    def body(oc, carry):
-        for ab in range(2):
-            t = ab * PART + oc
-            acc = own_sum(tab, a, b, base + t) + decoded(in_r, scale_r, t) + decoded(in_l, scale_l, t)
-            encode(acc, out.at[oc], ab * TILE, code, ab)
-        write_codes(code, out.at[oc], 2 * TILE)
-        return carry
-
-    lax.fori_loop(0, PART, body, 0)
+    def body(g, carry):
+        for u in range(2):
+            oc = g * 2 + u
+            for ab in range(2):
+                t = ab * PART + oc
+                acc = own[h * SUB + t] + decoded(in_r, scale_r, t) + decoded(in_l, scale_l, t)
+                encode(acc, out.at[oc], ab * TILE, code.at[u], ab)
+            write_codes(code.at[u], out.at[oc], 2 * TILE)
+        return carry
+
+    lax.fori_loop(0, PART // 2, body, 0)
 
 
 def deliver_kernel(one, two, out, scale):
@@ -211,8 +229,16 @@
     return pltpu.CompilerParams(vmem_limit_bytes=mib * 2**20)
 
 
-def cost(tiles, bytes_accessed):
-    return pl.CostEstimate(flops=tiles * 5 * 2 * TILE**3, bytes_accessed=bytes_accessed, transcendentals=0)
+COST_FIRST = 2
+COST_SECOND0 = 3
+COST_SECOND1 = 3
+COST_MIDDLE = 3
+COST_OWN = 3
+COST_LAST = 1
+
+
+def cost(us):
+    return pl.CostEstimate(flops=int(us * 1e9), bytes_accessed=int(us * 3e6), transcendentals=0)
 
 
 def scratch(count):
@@ -223,18 +249,54 @@
     return jax.ShapeDtypeStruct((rows + CODE_ROWS, TILE), I16)
 
 
-def step(kernel, name, tiles, out_shape, scratches, *args):
-    ins = [SMEM_SPEC, SMEM_SPEC] + [VMEM_SPEC] * (len(args) - 2)
+def step(kernel, name, weight, out_shape, scratches, after, *args):
+    ins = [SMEM_SPEC, SMEM_SPEC] + [VMEM_SPEC] * (len(args) - 2) + [ANY_SPEC]
+    count = len(args)
+
+    def body(*refs):
+        kernel(*refs[:count], *refs[count + 1 :])
+
     return pl.pallas_call(
-        kernel,
+        body,
         out_shape=out_shape,
         in_specs=ins,
         out_specs=jax.tree.map(lambda _: VMEM_SPEC, out_shape),
         scratch_shapes=scratch(scratches),
         compiler_params=params(16),
-        cost_estimate=cost(tiles, 2**22),
+        cost_estimate=cost(weight),
         name=name,
-    )(*args)
+    )(*args, after)
+
+
+def own_tiles(after, *args):
+    def body(pos, tab, a, b, unused, own):
+        own_kernel(pos, tab, a, b, own)
+
+    return pl.pallas_call(
+        body,
+        out_shape=VM((2 * SUB, TILE, TILE), F32),
+        in_specs=[SMEM_SPEC] * 2 + [VMEM_SPEC] * 2 + [ANY_SPEC],
+        out_specs=VMEM_SPEC,
+        compiler_params=params(16),
+        cost_estimate=cost(COST_OWN),
+        name="own",
+    )(*args, after)
+
+
+def last(h, out_shape, after, *args):
+    def body(own, in_r, in_l, unused, *rest):
+        last_kernel(h, own, in_r, in_l, *rest)
+
+    return pl.pallas_call(
+        body,
+        out_shape=out_shape,
+        in_specs=[VMEM_SPEC] * 3 + [ANY_SPEC],
+        out_specs=VMEM_SPEC,
+        scratch_shapes=[pltpu.VMEM((2, CODE_ROWS, TILE), F32)] + scratch(2),
+        compiler_params=params(16),
+        cost_estimate=cost(COST_LAST),
+        name=f"last{h}",
+    )(*args, after)
 
 
 def deliver(one, two, tiles):
@@ -245,7 +307,7 @@
         out_specs=VMEM_SPEC,
         scratch_shapes=scratch(1),
         compiler_params=params(16),
-        cost_estimate=cost(0, 2**22),
+        cost_estimate=cost(0),
         name="deliver",
     )(one, two)
 
@@ -257,8 +319,16 @@
         pairs = [(i, (i + by) % size) for i in range(size)]
         return lambda x: lax.ppermute(x, axis, pairs)
 
-    y_up, y_down = shift("row", row, 1), shift("row", row, -1)
-    x_up, x_down = shift("col", col, 2), shift("col", col, -2)
+    def x_split(x):
+        return lax.ppermute(x, "col", [(i, (i + 2 - 4 * (i % 2)) % col) for i in range(col)])
+
+    def y_split(x):
+        pairs = []
+        for r in range(row):
+            for c in range(col):
+                pairs.append((r * col + c, (r + 1 - 2 * (c % 2)) % row * col + c))
+        return lax.ppermute(x, ("row", "col"), pairs)
+
     z_up, z_down = shift("depth", depth, 1), shift("depth", depth, -1)
 
     def swap(x):
@@ -267,30 +337,42 @@
     pos = jnp.stack([lax.axis_index(n) for n in ("depth", "row", "col")]).astype(jnp.int32)
     b0 = b_tiles.reshape((-1,) + b_tiles.shape[2:])
     a0 = a_tiles.reshape((-1,) + a_tiles.shape[2:])
-    half_b, half_a = b0.shape[0] // 2, a0.shape[0] // 2
-    bl, br = y_up(b0), y_down(b0)
-    al, ar = x_up(a0), x_down(a0)
-    ap = swap(a0)
-    b2, b3 = y_up(bl[:half_b]), y_down(br[half_b:])
-    a2, a3 = x_up(al[:half_a]), x_down(ar[half_a:])
-    alp, arp, a2p, a3p = swap(al), swap(ar), swap(a2), swap(a3)
+    q1, p1 = y_split(b0), x_split(a0)
+    bp, ap = swap(b0), swap(a0)
+    q2, p2 = y_split(bp), x_split(ap)
+    q3, p3 = y_split(q1), x_split(p1)
+    t2, s1, s2, s3 = swap(q2), swap(p1), swap(p2), swap(p3)
     tab = make_table(a_kcol, b_jcol, c_jcol, c_place)
+    b_vmem = VM((b0.shape[0] + 1, TILE, TILE), BF16)
     a, b = pl.pallas_call(
         assemble_kernel,
-        out_shape=(VM((a0.shape[0], TILE, TILE), BF16), VM((b0.shape[0] + 1, TILE, TILE), BF16)),
-        in_specs=[SMEM_SPEC] + [ANY_SPEC] * 15,
+        out_shape=(VM((a0.shape[0], TILE, TILE), BF16), b_vmem),
+        in_specs=[SMEM_SPEC] + [ANY_SPEC] * 11,
         out_specs=(VMEM_SPEC, VMEM_SPEC),
-        scratch_shapes=[pltpu.SemaphoreType.DMA((15,))],
+        scratch_shapes=[pltpu.SemaphoreType.DMA((11,))],
         compiler_params=params(16),
-        cost_estimate=cost(0, 9 * 2**20),
+        cost_estimate=cost(0),
         name="assemble",
-    )(pos, a0, ap, al, ar, alp, arp, a2, a3, a2p, a3p, b0, bl, br, b2, b3)
+    )(pos, a0, ap, p1, p2, p3, s1, s2, s3, b0, q1, t2)
 
     short = (message(HALF_ROWS),) * 2
     full = (message(ROWS),) * 2
     flying = []
     for h in range(2):
-        r, l = step(functools.partial(first_kernel, h), f"first{h}", 16, short, 2, pos, tab, a, b)
+        if h == 0:
+            r, l, b = pl.pallas_call(
+                finish_kernel,
+                out_shape=short + (b_vmem,),
+                in_specs=[SMEM_SPEC] * 2 + [VMEM_SPEC] * 2 + [ANY_SPEC],
+                out_specs=(VMEM_SPEC,) * 3,
+                scratch_shapes=scratch(2) + [pltpu.SemaphoreType.DMA],
+                input_output_aliases={3: 2},
+                compiler_params=params(16),
+                cost_estimate=cost(COST_FIRST),
+                name="first0",
+            )(pos, tab, a, b, q3)
+        else:
+            r, l = step(functools.partial(first_kernel, h), f"first{h}", COST_FIRST, short, 2, r, pos, tab, a, b)
         flying.append((z_up(r), z_down(l)))
     for hop in range(3):
         landed, flying = flying, []
@@ -299,13 +381,17 @@
                 kernel, name = functools.partial(second_kernel, h), f"second{h}"
             else:
                 kernel, name = functools.partial(middle_kernel, h, 3 - hop), f"middle{hop}{h}"
-            r, l = step(kernel, name, 32, full, 4, pos, tab, a, b, *landed[h])
+            weight = (COST_SECOND0, COST_SECOND1)[h] if hop == 0 else COST_MIDDLE
+            r, l = step(kernel, name, weight, full, 4, r, pos, tab, a, b, *landed[h])
             flying.append((z_up(r), z_down(l)))
+    own = own_tiles(r, pos, tab, a, b)
     arrived = []
     for h in range(2):
         out = jax.ShapeDtypeStruct((col, 2 * TILE + CODE_ROWS, TILE), I16)
-        mine = step(functools.partial(last_kernel, h), f"last{h}", 16, out, 3, pos, tab, a, b, *flying[h])
-        arrived.append(lax.all_to_all(mine, "col", split_axis=0, concat_axis=0, tiled=True))
+        r = last(h, out, r, own, *flying[h])
+        if arrived:
+            r, arrived[0] = lax.optimization_barrier((r, arrived[0]))
+        arrived.append(lax.all_to_all(r, "col", split_axis=0, concat_axis=0, tiled=True))
     return deliver(*arrived, col * 4)
 
 

time: 182 us -> 156 us (0.86)
  local copies, waits for them, and re-layouts: 14 us -> 4.49 us
  starting transfers between devices: 57.4 us -> 48.6 us
  waiting for transfers between devices: 55.1 us -> 47.2 us
    ppermute x24 -> x16, waiting for transfers between devices: 51.9 us -> 23.9 us  [shift(): return lambda x: lax.ppermute(x, axis, pairs)]
    ppermute x0 -> x6, waiting for transfers between devices: none -> 15.8 us  [the longest x3 9.14 us: x_split(): lax.ppermute(x, 'col', [(i, (i + 2 - 4 * (i % 2)) % col) for i in range(c...]
    ppermute x24 -> x16, starting transfers between devices: 38.1 us -> 24.9 us  [shift(): return lambda x: lax.ppermute(x, axis, pairs)]
    ppermute x0 -> x6, starting transfers between devices: none -> 8.08 us  [the longest x3 5.92 us: x_split(): lax.ppermute(x, 'col', [(i, (i + 2 - 4 * (i % 2)) % col) for i in range(c...]
    unnamed x19 -> x7, local copies, waits for them, and re-layouts: 10.2 us -> 3.84 us
    all_to_all x1, waiting for transfers between devices: 2.24 us -> 5.65 us  [per_device(): lax.all_to_all(r, 'col', split_axis=0, concat_axis=0, tiled=True)]
    slice x4 -> x0, local copies, waits for them, and re-layouts: 3.19 us -> none  [the longest x2 1.67 us: per_device(): b2, b3 = (y_up(bl[:half_b]), y_down(br[half_b:]))]
    all_to_all x1, starting transfers between devices: 10.2 us -> 7.62 us  [per_device(): lax.all_to_all(r, 'col', split_axis=0, concat_axis=0, tiled=True)]
  transfers between devices with their start and end apart: 30 -> 29, of which waited for: 11 -> 13; matrix products, arithmetic and copies ran while one was open for 5% -> 4% of each run, Pallas kernels for 15% -> 22%
where the time goes in v2:
time: 156 us; the launch traced here: 155 us
  starting transfers between devices  48.6 us (31%)
  waiting for transfers between devices  47.2 us (30%)
  Pallas kernels  37.9 us (24%)
  blocking collectives  13.4 us (9%)
  local copies, waits for them, and re-layouts  4.49 us (3%)
  other arithmetic  3.48 us (2%)
    ppermute x16, starting transfers between devices, shift(): return lambda x: lax.ppermute(x, axis, pairs)  24.9 us
    pallas_call x7, Pallas kernels, step(): pl.pallas_call(body, out_shape=out_shape, in_specs=ins, out_specs=jax.tre...  24.6 us
    ppermute x16, waiting for transfers between devices, shift(): return lambda x: lax.ppermute(x, axis, pairs)  23.9 us
    all_to_all x1, blocking collectives, per_device(): lax.all_to_all(r, 'col', split_axis=0, concat_axis=0, tiled=True)  13.4 us
    ppermute x3, waiting for transfers between devices, x_split(): lax.ppermute(x, 'col', [(i, (i + 2 - 4 * (i % 2)) % col) for i in range(c...  9.14 us
    ppermute x6, starting transfers between devices, swap(): return lax.ppermute(x, 'col', [(i, i ^ 1) for i in range(col)])  7.91 us
    all_to_all x1, starting transfers between devices, per_device(): lax.all_to_all(r, 'col', split_axis=0, concat_axis=0, tiled=True)  7.62 us
    ppermute x3, waiting for transfers between devices, y_split(): return lax.ppermute(x, ('row', 'col'), pairs)  6.62 us
  transfers between devices with their start and end apart: 29, of which 13 were waited for; matrix products, arithmetic and copies ran while one was open for 4% of the time, Pallas kernels for 22%

profile of v2, /device:TPU:1, one launch (start us, length us, event | category | flops | bytes accessed | tf_op | source)
XLA Modules:
  0.0 155.3 jit_solution(2400105300130776593)
XLA Ops:
  0.0 3.2 %collective-permute-start.8 = (bf16[128,32,128]{2,1,0:T(8,128)(2,1)}, bf16[128,32,128]{2,1,0:T(8,128)(2,1)S(1)}, u32[]{:S(2)}, u32[]{:S(2)}) collective-permute-start(bf16[128,32,128]{2,1,0:T(8,128)(2,1)} %bitcast.11), channel_id=1, source_target_pairs={{0,1},{1,0},{2,3},{3,2},{4,5},{5,4},{6,7},{7,6},{8,9},{9,8},{10,11... | collective-permute-start | bytes 3145736 | tf_op jit(solution)/shard_map/ppermute | solution.py:335
  3.2 1.0 collective-permute-start.7
  4.2 1.5 collective-permute-done.8
  5.7 1.0 collective-permute-start.9
  6.7 2.5 %collective-permute-start.1 = (bf16[160,16,128]{2,1,0:T(8,128)(2,1)}, bf16[160,16,128]{2,1,0:T(8,128)(2,1)}, u32[]{:S(2)}, u32[]{:S(2)}) collective-permute-start(bf16[160,16,128]{2,1,0:T(8,128)(2,1)} %bitcast.14), channel_id=1, source_target_pairs={{0,2},{1,7},{2,4},{3,1},{4,6},{5,3},{6,0},{7,5},{8,10},{9,15},{10,... | collective-permute-start | bytes 1966088 | tf_op jit(solution)/shard_map/ppermute | solution.py:323
  10.8 6.3 %collective-permute-done.1.p1 = bf16[160,16,128]{2,1,0:T(8,128)(2,1)} collective-permute-done((bf16[160,16,128]{2,1,0:T(8,128)(2,1)}, bf16[160,16,128]{2,1,0:T(8,128)(2,1)}, u32[]{:S(2)}, u32[]{:S(2)}) %collective-permute-start.1) | collective-permute-done | bytes 655392 | tf_op jit(solution)/shard_map/ppermute | solution.py:323
  17.1 3.4 %collective-permute-start.3 = (bf16[160,16,128]{2,1,0:T(8,128)(2,1)}, bf16[160,16,128]{2,1,0:T(8,128)(2,1)}, u32[]{:S(2)}, u32[]{:S(2)}) collective-permute-start(bf16[160,16,128]{2,1,0:T(8,128)(2,1)} %collective-permute-done.1.p1), channel_id=1, source_target_pairs={{0,2},{1,7},{2,4},{3,1},{4,6},{5,3},{6,0},{7,5},{8,10},{9,15},{10,... | collective-permute-start | bytes 1966088 | tf_op jit(solution)/shard_map/ppermute | solution.py:323
  22.1 6.6 %collective-permute-done.9 = bf16[128,32,128]{2,1,0:T(8,128)(2,1)} collective-permute-done((bf16[128,32,128]{2,1,0:T(8,128)(2,1)S(1)}, bf16[128,32,128]{2,1,0:T(8,128)(2,1)}, u32[]{:S(2)}, u32[]{:S(2)}) %collective-permute-start.9) | collective-permute-done | bytes 1048608 | tf_op jit(solution)/shard_map/ppermute | solution.py:330
  28.7 2.1 %collective-permute-start.10 = (bf16[128,32,128]{2,1,0:T(8,128)(2,1)}, bf16[128,32,128]{2,1,0:T(8,128)(2,1)S(1)}, u32[]{:S(2)}, u32[]{:S(2)}) collective-permute-start(bf16[128,32,128]{2,1,0:T(8,128)(2,1)} %collective-permute-done.9), channel_id=1, source_target_pairs={{0,1},{1,0},{2,3},{3,2},{4,5},{5,4},{6,7},{7,6},{8,9},{9,8},{10,11... | collective-permute-start | bytes 3145736 | tf_op jit(solution)/shard_map/ppermute | solution.py:335
  32.5 2.9 %collective-permute-done.2.p2 = bf16[160,16,128]{2,1,0:T(8,128)(2,1)} collective-permute-done((bf16[160,16,128]{2,1,0:T(8,128)(2,1)}, bf16[160,16,128]{2,1,0:T(8,128)(2,1)}, u32[]{:S(2)}, u32[]{:S(2)}) %collective-permute-start.2) | collective-permute-done | bytes 655392 | tf_op jit(solution)/shard_map/ppermute | solution.py:323
  35.3 2.0 %collective-permute-start.5 = (bf16[160,16,128]{2,1,0:T(8,128)(2,1)}, bf16[160,16,128]{2,1,0:T(8,128)(2,1)}, u32[]{:S(2)}, u32[]{:S(2)}) collective-permute-start(bf16[160,16,128]{2,1,0:T(8,128)(2,1)} %collective-permute-done.2.p2), channel_id=1, source_target_pairs={{0,1},{1,0},{2,3},{3,2},{4,5},{5,4},{6,7},{7,6},{8,9},{9,8},{10,11... | collective-permute-start | bytes 1966088 | tf_op jit(solution)/shard_map/ppermute | solution.py:335
  39.4 1.2 copy-done
  40.7 1.1 copy-done.1
  41.7 3.0 %assemble.1 = (bf16[160,128,128]{2,1,0:T(8,128)(2,1)S(1)}, bf16[129,128,128]{2,1,0:T(8,128)(2,1)S(1)}) custom-call(s32[3]{0:T(128)S(1)} %pad_add_fusion.1.pos.refs_0_, bf16[160,16,128]{2,1,0:T(8,128)(2,1)S(1)} %bitcast.16, bf16[160,16,128]{2,1,0:T(8,128)(2,1)} %collective-permute-done.ap, bf16[160,16,128]{2,1,0:T(8,128)(2,1)} %collective-permute-done.1.p1, ...), custom_call_target="tpu_custom_call" | custom-call | tf_op jit(solution)/shard_map/assemble/pallas_call | solution.py:347
  44.8 2.3 %first0.1 = (s16[1040,128]{1,0:T(8,128)(2,1)S(1)}, s16[1040,128]{1,0:T(8,128)(2,1)S(1)}, bf16[129,128,128]{2,1,0:T(8,128)(2,1)S(1)}) custom-call(s32[3]{0:T(128)S(1)} %pad_add_fusion.1.pos.refs_0_, s32[1536]{0:T(1024)S(1)} %reshape.130.tab.refs_1_, bf16[160,128,128]{2,1,0:T(8,128)(2,1)S(1)} %get-tuple-element.26.a.refs_2_, ...), custom_call_target="tpu_custom_call", output_to_operand_aliasing={{2}: (3, {})} | custom-call | flops 2000000000 | bytes 6000000 | tf_op jit(solution)/shard_map/first0/pallas_call | solution.py:363
  47.1 1.6 %collective-permute-start.14 = (s16[1040,128]{1,0:T(8,128)(2,1)S(1)}, s16[1040,128]{1,0:T(8,128)(2,1)S(1)}, u32[]{:S(2)}, u32[]{:S(2)}) collective-permute-start(s16[1040,128]{1,0:T(8,128)(2,1)S(1)} %get-tuple-element.29.refs_4_), channel_id=1, source_target_pairs={{0,32},{32,64},{64,96},{96,128},{128,160},{160,192},{192,224},{224... | collective-permute-start | bytes 798728 | tf_op jit(solution)/shard_map/ppermute | solution.py:320
  48.7 4.0 %collective-permute-start.15 = (s16[1040,128]{1,0:T(8,128)(2,1)S(1)}, s16[1040,128]{1,0:T(8,128)(2,1)S(1)}, u32[]{:S(2)}, u32[]{:S(2)}) collective-permute-start(s16[1040,128]{1,0:T(8,128)(2,1)S(1)} %get-tuple-element.32), channel_id=1, source_target_pairs={{0,224},{32,0},{64,32},{96,64},{128,96},{160,128},{192,160},{224,1... | collective-permute-start | bytes 798728 | tf_op jit(solution)/shard_map/ppermute | solution.py:320
  52.7 2.1 %first1.1 = (s16[1040,128]{1,0:T(8,128)(2,1)S(1)}, s16[1040,128]{1,0:T(8,128)(2,1)S(1)}) custom-call(s32[3]{0:T(128)S(1)} %pad_add_fusion.1.pos.refs_0_, s32[1536]{0:T(1024)S(1)} %reshape.130.tab.refs_1_, bf16[160,128,128]{2,1,0:T(8,128)(2,1)S(1)} %get-tuple-element.26.a.refs_2_, bf16[129,128,128]{2,1,0:T(8,128)(2,1)S(1)} %get-tuple-element.28.refs_3_.b, ...), custom_call_target="tpu_custom_call" | custom-call | flops 2000000000 | bytes 6000000 | tf_op jit(solution)/shard_map/first1/pallas_call | solution.py:259
  55.1 2.7 %collective-permute-start.13 = (s16[1040,128]{1,0:T(8,128)(2,1)S(1)}, s16[1040,128]{1,0:T(8,128)(2,1)S(1)}, u32[]{:S(2)}, u32[]{:S(2)}) collective-permute-start(s16[1040,128]{1,0:T(8,128)(2,1)S(1)} %get-tuple-element.31), channel_id=1, source_target_pairs={{0,224},{32,0},{64,32},{96,64},{128,96},{160,128},{192,160},{224,1... | collective-permute-start | bytes 798728 | tf_op jit(solution)/shard_map/ppermute | solution.py:320
  57.7 1.3 collective-permute-done.14.refs_4_
  59.1 3.6 %second0.1 = (s16[2064,128]{1,0:T(8,128)(2,1)S(1)}, s16[2064,128]{1,0:T(8,128)(2,1)S(1)}) custom-call(s32[3]{0:T(128)S(1)} %pad_add_fusion.1.pos.refs_0_, s32[1536]{0:T(1024)S(1)} %reshape.130.tab.refs_1_, bf16[160,128,128]{2,1,0:T(8,128)(2,1)S(1)} %get-tuple-element.26.a.refs_2_, bf16[129,128,128]{2,1,0:T(8,128)(2,1)S(1)} %get-tuple-element.28.refs_3_.b, ...), custom_call_target="tpu_custom_call" | custom-call | flops 3000000000 | bytes 9000000 | tf_op jit(solution)/shard_map/second0/pallas_call | solution.py:259
  62.8 2.7 %collective-permute-start.19 = (s16[2064,128]{1,0:T(8,128)(2,1)S(1)}, s16[2064,128]{1,0:T(8,128)(2,1)S(1)}, u32[]{:S(2)}, u32[]{:S(2)}) collective-permute-start(s16[2064,128]{1,0:T(8,128)(2,1)S(1)} %get-tuple-element.36), channel_id=1, source_target_pairs={{0,224},{32,0},{64,32},{96,64},{128,96},{160,128},{192,160},{224,1... | collective-permute-start | bytes 1585160 | tf_op jit(solution)/shard_map/ppermute | solution.py:320
  65.5 3.6 %second1.1 = (s16[2064,128]{1,0:T(8,128)(2,1)S(1)}, s16[2064,128]{1,0:T(8,128)(2,1)S(1)}) custom-call(s32[3]{0:T(128)S(1)} %pad_add_fusion.1.pos.refs_0_, s32[1536]{0:T(1024)S(1)} %reshape.130.tab.refs_1_, bf16[160,128,128]{2,1,0:T(8,128)(2,1)S(1)} %get-tuple-element.26.a.refs_2_, bf16[129,128,128]{2,1,0:T(8,128)(2,1)S(1)} %get-tuple-element.28.refs_3_.b, ...), custom_call_target="tpu_custom_call" | custom-call | flops 3000000000 | bytes 9000000 | tf_op jit(solution)/shard_map/second1/pallas_call | solution.py:259
  69.1 2.7 %collective-permute-start.17 = (s16[2064,128]{1,0:T(8,128)(2,1)S(1)}, s16[2064,128]{1,0:T(8,128)(2,1)S(1)}, u32[]{:S(2)}, u32[]{:S(2)}) collective-permute-start(s16[2064,128]{1,0:T(8,128)(2,1)S(1)} %get-tuple-element.35), channel_id=1, source_target_pairs={{0,224},{32,0},{64,32},{96,64},{128,96},{160,128},{192,160},{224,1... | collective-permute-start | bytes 1585160 | tf_op jit(solution)/shard_map/ppermute | solution.py:320
  71.8 4.3 %collective-permute-done.18.refs_4_ = s16[2064,128]{1,0:T(8,128)(2,1)S(1)} collective-permute-done((s16[2064,128]{1,0:T(8,128)(2,1)S(1)}, s16[2064,128]{1,0:T(8,128)(2,1)S(1)}, u32[]{:S(2)}, u32[]{:S(2)}) %collective-permute-start.18) | collective-permute-done | bytes 528416 | tf_op jit(solution)/shard_map/ppermute | solution.py:320
  76.1 3.6 %middle10.1 = (s16[2064,128]{1,0:T(8,128)(2,1)S(1)}, s16[2064,128]{1,0:T(8,128)(2,1)S(1)}) custom-call(s32[3]{0:T(128)S(1)} %pad_add_fusion.1.pos.refs_0_, s32[1536]{0:T(1024)S(1)} %reshape.130.tab.refs_1_, bf16[160,128,128]{2,1,0:T(8,128)(2,1)S(1)} %get-tuple-element.26.a.refs_2_, bf16[129,128,128]{2,1,0:T(8,128)(2,1)S(1)} %get-tuple-element.28.refs_3_.b, ...), custom_call_target="tpu_custom_call" | custom-call | flops 3000000000 | bytes 9000000 | tf_op jit(solution)/shard_map/middle10/pallas_call | solution.py:259
  79.7 0.9 collective-permute-start.22
  80.6 1.9 %collective-permute-start.23 = (s16[2064,128]{1,0:T(8,128)(2,1)S(1)}, s16[2064,128]{1,0:T(8,128)(2,1)S(1)}, u32[]{:S(2)}, u32[]{:S(2)}) collective-permute-start(s16[2064,128]{1,0:T(8,128)(2,1)S(1)} %get-tuple-element.40), channel_id=1, source_target_pairs={{0,224},{32,0},{64,32},{96,64},{128,96},{160,128},{192,160},{224,1... | collective-permute-start | bytes 1585160 | tf_op jit(solution)/shard_map/ppermute | solution.py:320
  82.5 5.0 %collective-permute-done.16.refs_4_ = s16[2064,128]{1,0:T(8,128)(2,1)S(1)} collective-permute-done((s16[2064,128]{1,0:T(8,128)(2,1)S(1)}, s16[2064,128]{1,0:T(8,128)(2,1)S(1)}, u32[]{:S(2)}, u32[]{:S(2)}) %collective-permute-start.16) | collective-permute-done | bytes 528416 | tf_op jit(solution)/shard_map/ppermute | solution.py:320
  87.4 3.6 %middle11.1 = (s16[2064,128]{1,0:T(8,128)(2,1)S(1)}, s16[2064,128]{1,0:T(8,128)(2,1)S(1)}) custom-call(s32[3]{0:T(128)S(1)} %pad_add_fusion.1.pos.refs_0_, s32[1536]{0:T(1024)S(1)} %reshape.130.tab.refs_1_, bf16[160,128,128]{2,1,0:T(8,128)(2,1)S(1)} %get-tuple-element.26.a.refs_2_, bf16[129,128,128]{2,1,0:T(8,128)(2,1)S(1)} %get-tuple-element.28.refs_3_.b, ...), custom_call_target="tpu_custom_call" | custom-call | flops 3000000000 | bytes 9000000 | tf_op jit(solution)/shard_map/middle11/pallas_call | solution.py:259
  91.1 0.9 collective-permute-start.20
  91.9 1.9 %collective-permute-start.21 = (s16[2064,128]{1,0:T(8,128)(2,1)S(1)}, s16[2064,128]{1,0:T(8,128)(2,1)S(1)}, u32[]{:S(2)}, u32[]{:S(2)}) collective-permute-start(s16[2064,128]{1,0:T(8,128)(2,1)S(1)} %get-tuple-element.39), channel_id=1, source_target_pairs={{0,224},{32,0},{64,32},{96,64},{128,96},{160,128},{192,160},{224,1... | collective-permute-start | bytes 1585160 | tf_op jit(solution)/shard_map/ppermute | solution.py:320
  93.8 4.9 %collective-permute-done.22.refs_4_ = s16[2064,128]{1,0:T(8,128)(2,1)S(1)} collective-permute-done((s16[2064,128]{1,0:T(8,128)(2,1)S(1)}, s16[2064,128]{1,0:T(8,128)(2,1)S(1)}, u32[]{:S(2)}, u32[]{:S(2)}) %collective-permute-start.22) | collective-permute-done | bytes 528416 | tf_op jit(solution)/shard_map/ppermute | solution.py:320
  98.8 3.6 %middle20.1 = (s16[2064,128]{1,0:T(8,128)(2,1)S(1)}, s16[2064,128]{1,0:T(8,128)(2,1)S(1)}) custom-call(s32[3]{0:T(128)S(1)} %pad_add_fusion.1.pos.refs_0_, s32[1536]{0:T(1024)S(1)} %reshape.130.tab.refs_1_, bf16[160,128,128]{2,1,0:T(8,128)(2,1)S(1)} %get-tuple-element.26.a.refs_2_, bf16[129,128,128]{2,1,0:T(8,128)(2,1)S(1)} %get-tuple-element.28.refs_3_.b, ...), custom_call_target="tpu_custom_call" | custom-call | flops 3000000000 | bytes 9000000 | tf_op jit(solution)/shard_map/middle20/pallas_call | solution.py:259
  102.4 0.9 collective-permute-start.26
  103.3 1.9 %collective-permute-start.27 = (s16[2064,128]{1,0:T(8,128)(2,1)S(1)}, s16[2064,128]{1,0:T(8,128)(2,1)S(1)}, u32[]{:S(2)}, u32[]{:S(2)}) collective-permute-start(s16[2064,128]{1,0:T(8,128)(2,1)S(1)} %get-tuple-element.44), channel_id=1, source_target_pairs={{0,224},{32,0},{64,32},{96,64},{128,96},{160,128},{192,160},{224,1... | collective-permute-start | bytes 1585160 | tf_op jit(solution)/shard_map/ppermute | solution.py:320
  105.1 4.9 %collective-permute-done.20.refs_4_ = s16[2064,128]{1,0:T(8,128)(2,1)S(1)} collective-permute-done((s16[2064,128]{1,0:T(8,128)(2,1)S(1)}, s16[2064,128]{1,0:T(8,128)(2,1)S(1)}, u32[]{:S(2)}, u32[]{:S(2)}) %collective-permute-start.20) | collective-permute-done | bytes 528416 | tf_op jit(solution)/shard_map/ppermute | solution.py:320
  110.1 4.4 %middle21.1 = (s16[2064,128]{1,0:T(8,128)(2,1)S(1)}, s16[2064,128]{1,0:T(8,128)(2,1)}) custom-call(s32[3]{0:T(128)S(1)} %pad_add_fusion.1.pos.refs_0_, s32[1536]{0:T(1024)S(1)} %reshape.130.tab.refs_1_, bf16[160,128,128]{2,1,0:T(8,128)(2,1)S(1)} %get-tuple-element.26.a.refs_2_, bf16[129,128,128]{2,1,0:T(8,128)(2,1)S(1)} %get-tuple-element.28.refs_3_.b, ...), custom_call_target="tpu_custom_call" | custom-call | flops 3000000000 | bytes 9000000 | tf_op jit(solution)/shard_map/middle21/pallas_call | solution.py:259
  115.3 1.9 %collective-permute-start.25 = (s16[2064,128]{1,0:T(8,128)(2,1)}, s16[2064,128]{1,0:T(8,128)(2,1)}, u32[]{:S(2)}, u32[]{:S(2)}) collective-permute-start(s16[2064,128]{1,0:T(8,128)(2,1)} %get-tuple-element.43), channel_id=1, source_target_pairs={{0,224},{32,0},{64,32},{96,64},{128,96},{160,128},{192,160},{224,1... | collective-permute-start | bytes 1585160 | tf_op jit(solution)/shard_map/ppermute | solution.py:320
  117.2 3.3 %own.1 = f32[32,128,128]{2,1,0:T(8,128)S(1)} custom-call(s32[3]{0:T(128)S(1)} %pad_add_fusion.1.pos.refs_0_, s32[1536]{0:T(1024)S(1)} %reshape.130.tab.refs_1_, bf16[160,128,128]{2,1,0:T(8,128)(2,1)S(1)} %get-tuple-element.26.a.refs_2_, bf16[129,128,128]{2,1,0:T(8,128)(2,1)S(1)} %get-tuple-element.28.refs_3_.b, s16[2064,128]{1,0:T(8,128)(2,1)S(1)} %get-tuple-element.42.unused), custom_call_target="tpu_custom_call" | custom-call | flops 3000000000 | bytes 9000000 | tf_op jit(solution)/shard_map/own/pallas_call | solution.py:275
  120.5 0.9 collective-permute-done.26.in_r
  121.4 1.4 last0.1.unused
  122.8 7.6 %all-to-all-start = ((s16[8,272,128]{2,1,0:T(8,128)(2,1)}), s16[8,272,128]{2,1,0:T(8,128)(2,1)S(1)}, u32[]{:S(2)}, u32[]{:S(2)}) async-start(s16[8,272,128]{2,1,0:T(8,128)(2,1)} %last0.1.unused), calls=%async_computation | async-start | bytes 1114112 | tf_op jit(solution)/shard_map/all_to_all | solution.py:394
  130.4 2.4 %collective-permute-done.24.in_r = s16[2064,128]{1,0:T(8,128)(2,1)} collective-permute-done((s16[2064,128]{1,0:T(8,128)(2,1)S(1)}, s16[2064,128]{1,0:T(8,128)(2,1)}, u32[]{:S(2)}, u32[]{:S(2)}) %collective-permute-start.24) | collective-permute-done | bytes 528416 | tf_op jit(solution)/shard_map/ppermute | solution.py:320
  132.8 1.7 %last1.1 = s16[8,272,128]{2,1,0:T(8,128)(2,1)S(1)} custom-call(f32[32,128,128]{2,1,0:T(8,128)S(1)} %own.1, s16[2064,128]{1,0:T(8,128)(2,1)} %collective-permute-done.24.in_r, s16[2064,128]{1,0:T(8,128)(2,1)} %collective-permute-done.25.in_l, s16[8,272,128]{2,1,0:T(8,128)(2,1)} %last0.1.unused), custom_call_target="tpu_custom_call" | custom-call | flops 1000000000 | bytes 3000000 | tf_op jit(solution)/shard_map/last1/pallas_call | solution.py:290
  134.6 5.7 %all-to-all-done.one = s16[8,272,128]{2,1,0:T(8,128)(2,1)S(1)} async-done(((s16[8,272,128]{2,1,0:T(8,128)(2,1)}), s16[8,272,128]{2,1,0:T(8,128)(2,1)S(1)}, u32[]{:S(2)}, u32[]{:S(2)}) %all-to-all-start) | async-done | bytes 557088 | tf_op jit(solution)/shard_map/all_to_all | solution.py:394
  140.2 13.4 %all_to_all.10.two = s16[8,272,128]{2,1,0:T(8,128)(2,1)S(1)} all-to-all(s16[8,272,128]{2,1,0:T(8,128)(2,1)S(1)} %last1.1), channel_id=1, replica_groups=mesh['depth'=8,'row'=4,'col'=8] {'col'}, dimensions={0} | all-to-all | bytes 1114112 | tf_op jit(solution)/shard_map/all_to_all | solution.py:394
  153.6 1.7 %deliver.1 = f32[32,128,128]{2,1,0:T(8,128)} custom-call(s16[8,272,128]{2,1,0:T(8,128)(2,1)S(1)} %all-to-all-done.one, s16[8,272,128]{2,1,0:T(8,128)(2,1)S(1)} %all_to_all.10.two), custom_call_target="tpu_custom_call" | custom-call | tf_op jit(solution)/shard_map/deliver/pallas_call | solution.py:303
  (49 shorter events, 8.1 us)
Async XLA Ops:
  0.0 5.7 %collective-permute-start.8 = (bf16[128,32,128]{2,1,0:T(8,128)(2,1)}, bf16[128,32,128]{2,1,0:T(8,128)(2,1)S(1)}, u32[]{:S(2)}, u32[]{:S(2)}) collective-permute-start(bf16[128,32,128]{2,1,0:T(8,128)(2,1)} %bitcast.11), channel_id=1, source_target_pairs={{0,1},{1,0},{2,3},{3,2},{4,5},{5,4},{6,7},{7,6},{8,9},{9,8},{10,11... | collective-permute-start | bytes 3145736 | tf_op jit(solution)/shard_map/ppermute | solution.py:335
  3.2 18.7 %collective-permute-start.7 = (bf16[128,32,128]{2,1,0:T(8,128)(2,1)}, bf16[128,32,128]{2,1,0:T(8,128)(2,1)S(1)}, u32[]{:S(2)}, u32[]{:S(2)}) collective-permute-start(bf16[128,32,128]{2,1,0:T(8,128)(2,1)} %bitcast.12), channel_id=1, source_target_pairs={{0,8},{1,25},{2,10},{3,27},{4,12},{5,29},{6,14},{7,31},{8,16},{9,1... | collective-permute-start | bytes 3145736 | tf_op jit(solution)/shard_map/ppermute | solution.py:330
  5.7 23.0 %collective-permute-start.9 = (bf16[128,32,128]{2,1,0:T(8,128)(2,1)S(1)}, bf16[128,32,128]{2,1,0:T(8,128)(2,1)}, u32[]{:S(2)}, u32[]{:S(2)}) collective-permute-start(bf16[128,32,128]{2,1,0:T(8,128)(2,1)S(1)} %collective-permute-done.8), channel_id=1, source_target_pairs={{0,8},{1,25},{2,10},{3,27},{4,12},{5,29},{6,14},{7,31},{8,16},{9,1... | collective-permute-start | bytes 3145736 | tf_op jit(solution)/shard_map/ppermute | solution.py:330
  6.7 10.3 %collective-permute-start.1 = (bf16[160,16,128]{2,1,0:T(8,128)(2,1)}, bf16[160,16,128]{2,1,0:T(8,128)(2,1)}, u32[]{:S(2)}, u32[]{:S(2)}) collective-permute-start(bf16[160,16,128]{2,1,0:T(8,128)(2,1)} %bitcast.14), channel_id=1, source_target_pairs={{0,2},{1,7},{2,4},{3,1},{4,6},{5,3},{6,0},{7,5},{8,10},{9,15},{10,... | collective-permute-start | bytes 1966088 | tf_op jit(solution)/shard_map/ppermute | solution.py:323
  9.2 11.3 %collective-permute-start = (bf16[160,16,128]{2,1,0:T(8,128)(2,1)}, bf16[160,16,128]{2,1,0:T(8,128)(2,1)}, u32[]{:S(2)}, u32[]{:S(2)}) collective-permute-start(bf16[160,16,128]{2,1,0:T(8,128)(2,1)} %bitcast.15), channel_id=1, source_target_pairs={{0,1},{1,0},{2,3},{3,2},{4,5},{5,4},{6,7},{7,6},{8,9},{9,8},{10,11... | collective-permute-start | bytes 1966088 | tf_op jit(solution)/shard_map/ppermute | solution.py:335
  17.1 14.9 %collective-permute-start.3 = (bf16[160,16,128]{2,1,0:T(8,128)(2,1)}, bf16[160,16,128]{2,1,0:T(8,128)(2,1)}, u32[]{:S(2)}, u32[]{:S(2)}) collective-permute-start(bf16[160,16,128]{2,1,0:T(8,128)(2,1)} %collective-permute-done.1.p1), channel_id=1, source_target_pairs={{0,2},{1,7},{2,4},{3,1},{4,6},{5,3},{6,0},{7,5},{8,10},{9,15},{10,... | collective-permute-start | bytes 1966088 | tf_op jit(solution)/shard_map/ppermute | solution.py:323
  20.5 14.9 %collective-permute-start.2 = (bf16[160,16,128]{2,1,0:T(8,128)(2,1)}, bf16[160,16,128]{2,1,0:T(8,128)(2,1)}, u32[]{:S(2)}, u32[]{:S(2)}) collective-permute-start(bf16[160,16,128]{2,1,0:T(8,128)(2,1)} %collective-permute-done.ap), channel_id=1, source_target_pairs={{0,2},{1,7},{2,4},{3,1},{4,6},{5,3},{6,0},{7,5},{8,10},{9,15},{10,... | collective-permute-start | bytes 1966088 | tf_op jit(solution)/shard_map/ppermute | solution.py:323
  22.0 22.8 %collective-permute-start.11 = (bf16[128,32,128]{2,1,0:T(8,128)(2,1)S(1)}, bf16[128,32,128]{2,1,0:T(8,128)(2,1)S(1)}, u32[]{:S(2)}, u32[]{:S(2)}) collective-permute-start(bf16[128,32,128]{2,1,0:T(8,128)(2,1)S(1)} %collective-permute-done.7.q1), channel_id=1, source_target_pairs={{0,8},{1,25},{2,10},{3,27},{4,12},{5,29},{6,14},{7,31},{8,16},{9,1... | collective-permute-start | bytes 3145736 | tf_op jit(solution)/shard_map/ppermute | solution.py:330
  28.7 10.7 %collective-permute-start.10 = (bf16[128,32,128]{2,1,0:T(8,128)(2,1)}, bf16[128,32,128]{2,1,0:T(8,128)(2,1)S(1)}, u32[]{:S(2)}, u32[]{:S(2)}) collective-permute-start(bf16[128,32,128]{2,1,0:T(8,128)(2,1)} %collective-permute-done.9), channel_id=1, source_target_pairs={{0,1},{1,0},{2,3},{3,2},{4,5},{5,4},{6,7},{7,6},{8,9},{9,8},{10,11... | collective-permute-start | bytes 3145736 | tf_op jit(solution)/shard_map/ppermute | solution.py:335
  31.9 7.1 %collective-permute-start.4 = (bf16[160,16,128]{2,1,0:T(8,128)(2,1)}, bf16[160,16,128]{2,1,0:T(8,128)(2,1)}, u32[]{:S(2)}, u32[]{:S(2)}) collective-permute-start(bf16[160,16,128]{2,1,0:T(8,128)(2,1)} %collective-permute-done.1.p1), channel_id=1, source_target_pairs={{0,1},{1,0},{2,3},{3,2},{4,5},{5,4},{6,7},{7,6},{8,9},{9,8},{10,11... | collective-permute-start | bytes 1966088 | tf_op jit(solution)/shard_map/ppermute | solution.py:335
  32.0 7.0 %collective-permute-start.6 = (bf16[160,16,128]{2,1,0:T(8,128)(2,1)}, bf16[160,16,128]{2,1,0:T(8,128)(2,1)}, u32[]{:S(2)}, u32[]{:S(2)}) collective-permute-start(bf16[160,16,128]{2,1,0:T(8,128)(2,1)} %collective-permute-done.3.p3), channel_id=1, source_target_pairs={{0,1},{1,0},{2,3},{3,2},{4,5},{5,4},{6,7},{7,6},{8,9},{9,8},{10,11... | collective-permute-start | bytes 1966088 | tf_op jit(solution)/shard_map/ppermute | solution.py:335
  35.3 4.1 %collective-permute-start.5 = (bf16[160,16,128]{2,1,0:T(8,128)(2,1)}, bf16[160,16,128]{2,1,0:T(8,128)(2,1)}, u32[]{:S(2)}, u32[]{:S(2)}) collective-permute-start(bf16[160,16,128]{2,1,0:T(8,128)(2,1)} %collective-permute-done.2.p2), channel_id=1, source_target_pairs={{0,1},{1,0},{2,3},{3,2},{4,5},{5,4},{6,7},{7,6},{8,9},{9,8},{10,11... | collective-permute-start | bytes 1966088 | tf_op jit(solution)/shard_map/ppermute | solution.py:335
  39.4 1.2 copy-start
  40.7 1.1 copy-start.1
  47.1 12.0 %collective-permute-start.14 = (s16[1040,128]{1,0:T(8,128)(2,1)S(1)}, s16[1040,128]{1,0:T(8,128)(2,1)S(1)}, u32[]{:S(2)}, u32[]{:S(2)}) collective-permute-start(s16[1040,128]{1,0:T(8,128)(2,1)S(1)} %get-tuple-element.29.refs_4_), channel_id=1, source_target_pairs={{0,32},{32,64},{64,96},{96,128},{128,160},{160,192},{192,224},{224... | collective-permute-start | bytes 798728 | tf_op jit(solution)/shard_map/ppermute | solution.py:320
  48.7 10.4 %collective-permute-start.15 = (s16[1040,128]{1,0:T(8,128)(2,1)S(1)}, s16[1040,128]{1,0:T(8,128)(2,1)S(1)}, u32[]{:S(2)}, u32[]{:S(2)}) collective-permute-start(s16[1040,128]{1,0:T(8,128)(2,1)S(1)} %get-tuple-element.32), channel_id=1, source_target_pairs={{0,224},{32,0},{64,32},{96,64},{128,96},{160,128},{192,160},{224,1... | collective-permute-start | bytes 798728 | tf_op jit(solution)/shard_map/ppermute | solution.py:320
  54.8 10.6 %collective-permute-start.12 = (s16[1040,128]{1,0:T(8,128)(2,1)S(1)}, s16[1040,128]{1,0:T(8,128)(2,1)S(1)}, u32[]{:S(2)}, u32[]{:S(2)}) collective-permute-start(s16[1040,128]{1,0:T(8,128)(2,1)S(1)} %get-tuple-element.30.refs_6_), channel_id=1, source_target_pairs={{0,32},{32,64},{64,96},{96,128},{128,160},{160,192},{192,224},{224... | collective-permute-start | bytes 798728 | tf_op jit(solution)/shard_map/ppermute | solution.py:320
  55.1 10.4 %collective-permute-start.13 = (s16[1040,128]{1,0:T(8,128)(2,1)S(1)}, s16[1040,128]{1,0:T(8,128)(2,1)S(1)}, u32[]{:S(2)}, u32[]{:S(2)}) collective-permute-start(s16[1040,128]{1,0:T(8,128)(2,1)S(1)} %get-tuple-element.31), channel_id=1, source_target_pairs={{0,224},{32,0},{64,32},{96,64},{128,96},{160,128},{192,160},{224,1... | collective-permute-start | bytes 798728 | tf_op jit(solution)/shard_map/ppermute | solution.py:320
  62.7 13.4 %collective-permute-start.18 = (s16[2064,128]{1,0:T(8,128)(2,1)S(1)}, s16[2064,128]{1,0:T(8,128)(2,1)S(1)}, u32[]{:S(2)}, u32[]{:S(2)}) collective-permute-start(s16[2064,128]{1,0:T(8,128)(2,1)S(1)} %get-tuple-element.33.refs_6_), channel_id=1, source_target_pairs={{0,32},{32,64},{64,96},{96,128},{128,160},{160,192},{192,224},{224... | collective-permute-start | bytes 1585160 | tf_op jit(solution)/shard_map/ppermute | solution.py:320
  62.8 13.3 %collective-permute-start.19 = (s16[2064,128]{1,0:T(8,128)(2,1)S(1)}, s16[2064,128]{1,0:T(8,128)(2,1)S(1)}, u32[]{:S(2)}, u32[]{:S(2)}) collective-permute-start(s16[2064,128]{1,0:T(8,128)(2,1)S(1)} %get-tuple-element.36), channel_id=1, source_target_pairs={{0,224},{32,0},{64,32},{96,64},{128,96},{160,128},{192,160},{224,1... | collective-permute-start | bytes 1585160 | tf_op jit(solution)/shard_map/ppermute | solution.py:320
  69.0 18.4 %collective-permute-start.16 = (s16[2064,128]{1,0:T(8,128)(2,1)S(1)}, s16[2064,128]{1,0:T(8,128)(2,1)S(1)}, u32[]{:S(2)}, u32[]{:S(2)}) collective-permute-start(s16[2064,128]{1,0:T(8,128)(2,1)S(1)} %get-tuple-element.34.refs_6_), channel_id=1, source_target_pairs={{0,32},{32,64},{64,96},{96,128},{128,160},{160,192},{192,224},{224... | collective-permute-start | bytes 1585160 | tf_op jit(solution)/shard_map/ppermute | solution.py:320
  69.1 18.3 %collective-permute-start.17 = (s16[2064,128]{1,0:T(8,128)(2,1)S(1)}, s16[2064,128]{1,0:T(8,128)(2,1)S(1)}, u32[]{:S(2)}, u32[]{:S(2)}) collective-permute-start(s16[2064,128]{1,0:T(8,128)(2,1)S(1)} %get-tuple-element.35), channel_id=1, source_target_pairs={{0,224},{32,0},{64,32},{96,64},{128,96},{160,128},{192,160},{224,1... | collective-permute-start | bytes 1585160 | tf_op jit(solution)/shard_map/ppermute | solution.py:320
  79.7 19.0 %collective-permute-start.22 = (s16[2064,128]{1,0:T(8,128)(2,1)S(1)}, s16[2064,128]{1,0:T(8,128)(2,1)S(1)}, u32[]{:S(2)}, u32[]{:S(2)}) collective-permute-start(s16[2064,128]{1,0:T(8,128)(2,1)S(1)} %get-tuple-element.37.refs_6_), channel_id=1, source_target_pairs={{0,32},{32,64},{64,96},{96,128},{128,160},{160,192},{192,224},{224... | collective-permute-start | bytes 1585160 | tf_op jit(solution)/shard_map/ppermute | solution.py:320
  80.6 18.1 %collective-permute-start.23 = (s16[2064,128]{1,0:T(8,128)(2,1)S(1)}, s16[2064,128]{1,0:T(8,128)(2,1)S(1)}, u32[]{:S(2)}, u32[]{:S(2)}) collective-permute-start(s16[2064,128]{1,0:T(8,128)(2,1)S(1)} %get-tuple-element.40), channel_id=1, source_target_pairs={{0,224},{32,0},{64,32},{96,64},{128,96},{160,128},{192,160},{224,1... | collective-permute-start | bytes 1585160 | tf_op jit(solution)/shard_map/ppermute | solution.py:320
  91.1 19.0 %collective-permute-start.20 = (s16[2064,128]{1,0:T(8,128)(2,1)S(1)}, s16[2064,128]{1,0:T(8,128)(2,1)S(1)}, u32[]{:S(2)}, u32[]{:S(2)}) collective-permute-start(s16[2064,128]{1,0:T(8,128)(2,1)S(1)} %get-tuple-element.38.refs_6_), channel_id=1, source_target_pairs={{0,32},{32,64},{64,96},{96,128},{128,160},{160,192},{192,224},{224... | collective-permute-start | bytes 1585160 | tf_op jit(solution)/shard_map/ppermute | solution.py:320
  91.9 18.1 %collective-permute-start.21 = (s16[2064,128]{1,0:T(8,128)(2,1)S(1)}, s16[2064,128]{1,0:T(8,128)(2,1)S(1)}, u32[]{:S(2)}, u32[]{:S(2)}) collective-permute-start(s16[2064,128]{1,0:T(8,128)(2,1)S(1)} %get-tuple-element.39), channel_id=1, source_target_pairs={{0,224},{32,0},{64,32},{96,64},{128,96},{160,128},{192,160},{224,1... | collective-permute-start | bytes 1585160 | tf_op jit(solution)/shard_map/ppermute | solution.py:320
  102.4 19.0 %collective-permute-start.26 = (s16[2064,128]{1,0:T(8,128)(2,1)S(1)}, s16[2064,128]{1,0:T(8,128)(2,1)S(1)}, u32[]{:S(2)}, u32[]{:S(2)}) collective-permute-start(s16[2064,128]{1,0:T(8,128)(2,1)S(1)} %get-tuple-element.41.refs_6_), channel_id=1, source_target_pairs={{0,32},{32,64},{64,96},{96,128},{128,160},{160,192},{192,224},{224... | collective-permute-start | bytes 1585160 | tf_op jit(solution)/shard_map/ppermute | solution.py:320
  103.3 18.1 %collective-permute-start.27 = (s16[2064,128]{1,0:T(8,128)(2,1)S(1)}, s16[2064,128]{1,0:T(8,128)(2,1)S(1)}, u32[]{:S(2)}, u32[]{:S(2)}) collective-permute-start(s16[2064,128]{1,0:T(8,128)(2,1)S(1)} %get-tuple-element.44), channel_id=1, source_target_pairs={{0,224},{32,0},{64,32},{96,64},{128,96},{160,128},{192,160},{224,1... | collective-permute-start | bytes 1585160 | tf_op jit(solution)/shard_map/ppermute | solution.py:320
  114.5 18.3 %collective-permute-start.24 = (s16[2064,128]{1,0:T(8,128)(2,1)S(1)}, s16[2064,128]{1,0:T(8,128)(2,1)}, u32[]{:S(2)}, u32[]{:S(2)}) collective-permute-start(s16[2064,128]{1,0:T(8,128)(2,1)S(1)} %get-tuple-element.42.unused), channel_id=1, source_target_pairs={{0,32},{32,64},{64,96},{96,128},{128,160},{160,192},{192,224},{224... | collective-permute-start | bytes 1585160 | tf_op jit(solution)/shard_map/ppermute | solution.py:320
  115.3 17.5 %collective-permute-start.25 = (s16[2064,128]{1,0:T(8,128)(2,1)}, s16[2064,128]{1,0:T(8,128)(2,1)}, u32[]{:S(2)}, u32[]{:S(2)}) collective-permute-start(s16[2064,128]{1,0:T(8,128)(2,1)} %get-tuple-element.43), channel_id=1, source_target_pairs={{0,224},{32,0},{64,32},{96,64},{128,96},{160,128},{192,160},{224,1... | collective-permute-start | bytes 1585160 | tf_op jit(solution)/shard_map/ppermute | solution.py:320
  122.8 17.5 %all-to-all-start = ((s16[8,272,128]{2,1,0:T(8,128)(2,1)}), s16[8,272,128]{2,1,0:T(8,128)(2,1)S(1)}, u32[]{:S(2)}, u32[]{:S(2)}) async-start(s16[8,272,128]{2,1,0:T(8,128)(2,1)} %last0.1.unused), calls=%async_computation | async-start | bytes 1114112 | tf_op jit(solution)/shard_map/all_to_all | solution.py:394

commit v3 on v2

--- a/solution.py
+++ b/solution.py
@@ -35,13 +35,24 @@
     return jnp.where(located, flat_index, k_rows * b_count)
 
 
+ORDER = (
+    [(2, k, j) for k in range(2) for j in range(4)]
+    + [(d, k, j) for d in (1, 3) for k in range(2) for j in (0, 1)]
+    + [(d, k, j) for d in (1, 3) for k in range(2) for j in (2, 3)]
+    + [(0, k, j) for k in range(2) for j in range(4)]
+)
+
+
 def make_table(a_kcol, b_jcol, c_jcol, c_place):
+    col = lax.axis_index("col")
+    away, core, tile = (jnp.array([entry[n] for entry in ORDER], jnp.int32) for n in range(3))
+    owner = (col // 2 + away) % 4 * 2 + (col + core) % 2
     picks = select_blocks(a_kcol, b_jcol, c_jcol)
     rows, kept, slots = picks.shape
     row_ids = jnp.broadcast_to(jnp.arange(rows, dtype=jnp.int32)[:, None, None], (rows, kept, 1))
     fields = jnp.concatenate([row_ids, picks], axis=2).reshape(rows * kept, slots + 1)
     q = jnp.arange(rows * kept, dtype=jnp.int32)
-    target = q // 32 * 32 + q % 8 * 4 + q // 8 % 4
+    target = q // 32 * 32 + jnp.tile(owner * 4 + tile, rows * kept // 32)
     hit = c_place.reshape(1, rows * kept) == target[:, None]
     table = jnp.sum(jnp.where(hit[:, :, None], fields[None], 0), axis=1)
     return table.reshape(rows * kept * (slots + 1))
@@ -190,34 +201,64 @@
     lax.fori_loop(0, own.shape[0] // 4, body, 0)
 
 
-def last_kernel(h, own, in_r, in_l, out, code, scale_r, scale_l):
+def final_sum(own, in_r, in_l, scale_r, scale_l, h, t):
+    return own[h * SUB + t] + decoded(in_r, scale_r, t) + decoded(in_l, scale_l, t)
+
+
+def put_block(sums, out, code):
+    for n, one in enumerate(sums):
+        encode(one, out, n * TILE, code, n)
+    write_codes(code, out, len(sums) * TILE)
+
+
+def spread_kernel(own, in_r, in_l, unused, far, up, down, code, scale_r, scale_l):
     read_codes(in_r, ROWS, scale_r)
     read_codes(in_l, ROWS, scale_l)
     code[...] = jnp.zeros_like(code)
-
-    def body(g, carry):
-        for u in range(2):
-            oc = g * 2 + u
-            for ab in range(2):
-                t = ab * PART + oc
-                acc = own[h * SUB + t] + decoded(in_r, scale_r, t) + decoded(in_l, scale_l, t)
-                encode(acc, out.at[oc], ab * TILE, code.at[u], ab)
-            write_codes(code.at[u], out.at[oc], 2 * TILE)
-        return carry
-
-    lax.fori_loop(0, PART // 2, body, 0)
-
-
-def deliver_kernel(one, two, out, scale):
-    def body(g, carry):
-        for h, src in enumerate((one, two)):
-            read_codes(src.at[g], 2 * TILE, scale)
-            for ab in range(2):
-                rows = src[g, pl.ds(ab * TILE, TILE), :].astype(jnp.int32).astype(F32)
-                out[g * 4 + 2 * h + ab] = rows * scale[ab : ab + 1, :]
-        return carry
-
-    lax.fori_loop(0, out.shape[0] // 4, body, 0)
+    total = functools.partial(final_sum, own, in_r, in_l, scale_r, scale_l, 0)
+    for k in range(2):
+        put_block([total(4 * k + n) for n in range(4)], far.at[k], code.at[k])
+        put_block([total(8 + 2 * k + n) for n in range(2)], up.at[k], code.at[2 + k])
+        put_block([total(12 + 2 * k + n) for n in range(2)], down.at[k], code.at[4 + k])
+
+
+def last_kernel(own, in_r, in_l, unused, up, down, cross, home, code, scale_r, scale_l):
+    read_codes(in_r, ROWS, scale_r)
+    read_codes(in_l, ROWS, scale_l)
+    code[...] = jnp.zeros_like(code)
+    total = functools.partial(final_sum, own, in_r, in_l, scale_r, scale_l, 1)
+    for k in range(2):
+        put_block([total(2 * k + n) for n in range(2)], up.at[k], code.at[k])
+        put_block([total(4 + 2 * k + n) for n in range(2)], down.at[k], code.at[2 + k])
+    put_block([total(12 + n) for n in range(4)], cross, code.at[4])
+    for n in range(4):
+        home[n] = total(8 + n)
+
+
+def deliver_kernel(pos, far, up0, down0, up1, down1, swapped0, swapped1, cross, home, out, scale):
+    col = pos[2]
+    other = col + 1 - 2 * (col % 2)
+    wide, slim = 4 * TILE + CODE_ROWS, 2 * TILE + CODE_ROWS
+
+    def block(src, row, g, first, count):
+        read_codes(src, row + count * TILE, scale)
+        for n in range(count):
+            rows = src[row + n * TILE : row + (n + 1) * TILE, :].astype(jnp.int32).astype(F32)
+            out[(g + 8) % 8 * 4 + first + n] = rows * scale[n : n + 1, :]
+
+    block(far.at[0], 0, col + 4, 0, 4)
+    block(up0.at[0], 0, col - 2, 0, 2)
+    block(down0.at[0], 0, col + 2, 0, 2)
+    block(swapped0, 0, other + 4, 0, 4)
+    block(swapped0, wide, other - 2, 0, 2)
+    block(swapped0, wide + slim, other + 2, 0, 2)
+    block(up1.at[0], 0, col - 2, 2, 2)
+    block(down1.at[0], 0, col + 2, 2, 2)
+    block(swapped1, 0, other - 2, 2, 2)
+    block(swapped1, slim, other + 2, 2, 2)
+    block(cross, 0, other, 0, 4)
+    for n in range(4):
+        out[col * 4 + n] = home[n]
 
 
 SMEM_SPEC = pl.BlockSpec(memory_space=pltpu.SMEM)
@@ -283,33 +324,38 @@
     )(*args, after)
 
 
-def last(h, out_shape, after, *args):
-    def body(own, in_r, in_l, unused, *rest):
-        last_kernel(h, own, in_r, in_l, *rest)
-
+def coded(tiles, *lead):
+    return jax.ShapeDtypeStruct(lead + (tiles * TILE + CODE_ROWS, TILE), I16)
+
+
+def finals(kernel, name, out_shape, after, *args):
     return pl.pallas_call(
-        body,
+        kernel,
         out_shape=out_shape,
         in_specs=[VMEM_SPEC] * 3 + [ANY_SPEC],
-        out_specs=VMEM_SPEC,
-        scratch_shapes=[pltpu.VMEM((2, CODE_ROWS, TILE), F32)] + scratch(2),
+        out_specs=(VMEM_SPEC,) * len(out_shape),
+        scratch_shapes=[pltpu.VMEM((6, CODE_ROWS, TILE), F32)] + scratch(2),
         compiler_params=params(16),
         cost_estimate=cost(COST_LAST),
-        name=f"last{h}",
+        name=name,
     )(*args, after)
 
 
-def deliver(one, two, tiles):
+def deliver(tiles, *args):
     return pl.pallas_call(
         deliver_kernel,
         out_shape=jax.ShapeDtypeStruct((tiles, TILE, TILE), F32),
-        in_specs=[VMEM_SPEC] * 2,
+        in_specs=[SMEM_SPEC] + [VMEM_SPEC] * (len(args) - 1),
         out_specs=VMEM_SPEC,
         scratch_shapes=scratch(1),
         compiler_params=params(16),
-        cost_estimate=cost(0),
+        cost_estimate=cost(COST_LAST),
         name="deliver",
-    )(one, two)
+    )(*args)
+
+
+def in_hbm(x):
+    return pltpu.with_memory_space_constraint(x, pltpu.HBM)
 
 
 def per_device(a_tiles, a_kcol, b_tiles, b_jcol, c_jcol, c_place):
@@ -353,7 +399,7 @@
         compiler_params=params(16),
         cost_estimate=cost(0),
         name="assemble",
-    )(pos, a0, ap, p1, p2, p3, s1, s2, s3, b0, q1, t2)
+    )(pos, in_hbm(a0), ap, p1, p2, p3, s1, s2, s3, in_hbm(b0), q1, t2)
 
     short = (message(HALF_ROWS),) * 2
     full = (message(ROWS),) * 2
@@ -385,14 +431,21 @@
             r, l = step(kernel, name, weight, full, 4, r, pos, tab, a, b, *landed[h])
             flying.append((z_up(r), z_down(l)))
     own = own_tiles(r, pos, tab, a, b)
-    arrived = []
-    for h in range(2):
-        out = jax.ShapeDtypeStruct((col, 2 * TILE + CODE_ROWS, TILE), I16)
-        r = last(h, out, r, own, *flying[h])
-        if arrived:
-            r, arrived[0] = lax.optimization_barrier((r, arrived[0]))
-        arrived.append(lax.all_to_all(r, "col", split_axis=0, concat_axis=0, tiled=True))
-    return deliver(*arrived, col * 4)
+    x_up, x_down, x_far = (shift("col", col, n) for n in (2, -2, 4))
+    far, up, down = finals(spread_kernel, "spread", (coded(4, 2), coded(2, 2), coded(2, 2)), r, own, *flying[0])
+    far, up, down = x_far(far), x_up(up), x_down(down)
+    up1, down1, cross, home = finals(
+        last_kernel,
+        "last",
+        (coded(2, 2), coded(2, 2), coded(4), jax.ShapeDtypeStruct((4, TILE, TILE), F32)),
+        up,
+        own,
+        *flying[1],
+    )
+    up1, down1, cross = x_up(up1), x_down(down1), swap(cross)
+    swapped = swap(jnp.concatenate([far[1], up[1], down[1]]))
+    swapped1 = swap(jnp.concatenate([up1[1], down1[1]]))
+    return deliver(col * 4, pos, far, up, down, up1, down1, swapped, swapped1, cross, home)
 
 
 def solution(mesh):

time: 156 us -> 146 us (0.936)
  blocking collectives: 13.4 us -> 0 us
  starting transfers between devices: 48.6 us -> 53 us
  waiting for transfers between devices: 47.2 us -> 50.4 us
  Pallas kernels: 37.9 us -> 35.5 us
  local copies, waits for them, and re-layouts: 4.49 us -> 2.29 us
    all_to_all x1 -> x0, blocking collectives: 13.4 us -> none  [per_device(): lax.all_to_all(r, 'col', split_axis=0, concat_axis=0, tiled=True)]
    ppermute x16 -> x21, waiting for transfers between devices: 23.9 us -> 32.3 us  [shift(): return lambda x: lax.ppermute(x, axis, pairs)]
    all_to_all x1 -> x0, starting transfers between devices: 7.62 us -> none  [per_device(): lax.all_to_all(r, 'col', split_axis=0, concat_axis=0, tiled=True)]
    ppermute x16 -> x21, starting transfers between devices: 24.9 us -> 31 us  [shift(): return lambda x: lax.ppermute(x, axis, pairs)]
    ppermute x6 -> x9, starting transfers between devices: 7.91 us -> 13.9 us  [swap(): return lax.ppermute(x, 'col', [(i, i ^ 1) for i in range(col)])]
    all_to_all x1 -> x0, waiting for transfers between devices: 5.65 us -> none  [per_device(): lax.all_to_all(r, 'col', split_axis=0, concat_axis=0, tiled=True)]
    ppermute x3, waiting for transfers between devices: 9.14 us -> 6.74 us  [x_split(): lax.ppermute(x, 'col', [(i, (i + 2 - 4 * (i % 2)) % col) for i in range(c...]
    unnamed x7 -> x3, local copies, waits for them, and re-layouts: 3.84 us -> 1.52 us
  transfers between devices with their start and end apart: 29 -> 36, of which waited for: 13 -> 14; matrix products, arithmetic and copies ran while one was open for 4% -> 4% of each run, Pallas kernels for 22% -> 21%
where the time goes in v3:
time: 146 us
  starting transfers between devices  53 us (36%)
  waiting for transfers between devices  50.4 us (35%)
  Pallas kernels  35.5 us (24%)
  other arithmetic  4.21 us (3%)
  local copies, waits for them, and re-layouts  2.29 us (2%)
    ppermute x21, waiting for transfers between devices, shift(): return lambda x: lax.ppermute(x, axis, pairs)  32.3 us
    ppermute x21, starting transfers between devices, shift(): return lambda x: lax.ppermute(x, axis, pairs)  31 us
    pallas_call x7, Pallas kernels, step(): pl.pallas_call(body, out_shape=out_shape, in_specs=ins, out_specs=jax.tre...  23.4 us
    ppermute x9, starting transfers between devices, swap(): return lax.ppermute(x, 'col', [(i, i ^ 1) for i in range(col)])  13.9 us
    ppermute x3, waiting for transfers between devices, y_split(): return lax.ppermute(x, ('row', 'col'), pairs)  7.28 us
    ppermute x3, waiting for transfers between devices, x_split(): lax.ppermute(x, 'col', [(i, (i + 2 - 4 * (i % 2)) % col) for i in range(c...  6.74 us
    ppermute x3, starting transfers between devices, x_split(): lax.ppermute(x, 'col', [(i, (i + 2 - 4 * (i % 2)) % col) for i in range(c...  5.92 us
    ppermute x9, waiting for transfers between devices, swap(): return lax.ppermute(x, 'col', [(i, i ^ 1) for i in range(col)])  4.04 us
  transfers between devices with their start and end apart: 36, of which 14 were waited for; matrix products, arithmetic and copies ran while one was open for 4% of the time, Pallas kernels for 21%

profile of v3, /device:TPU:1, one launch (start us, length us, event | category | flops | bytes accessed | tf_op | source)
XLA Modules:
  0.0 145.7 jit_solution(7512808263422791471)
XLA Ops:
  0.0 3.2 %collective-permute-start.8 = (bf16[128,32,128]{2,1,0:T(8,128)(2,1)}, bf16[128,32,128]{2,1,0:T(8,128)(2,1)S(1)}, u32[]{:S(2)}, u32[]{:S(2)}) collective-permute-start(bf16[128,32,128]{2,1,0:T(8,128)(2,1)} %bitcast.21), channel_id=1, source_target_pairs={{0,1},{1,0},{2,3},{3,2},{4,5},{5,4},{6,7},{7,6},{8,9},{9,8},{10,11... | collective-permute-start | bytes 3145736 | tf_op jit(solution)/shard_map/ppermute | solution.py:381
  3.2 1.0 collective-permute-start.7
  4.2 1.5 %collective-permute-done.8 = bf16[128,32,128]{2,1,0:T(8,128)(2,1)S(1)} collective-permute-done((bf16[128,32,128]{2,1,0:T(8,128)(2,1)}, bf16[128,32,128]{2,1,0:T(8,128)(2,1)S(1)}, u32[]{:S(2)}, u32[]{:S(2)}) %collective-permute-start.8) | collective-permute-done | bytes 1048608 | tf_op jit(solution)/shard_map/ppermute | solution.py:381
  5.7 1.0 collective-permute-start.9
  6.7 2.5 %collective-permute-start.1 = (bf16[160,16,128]{2,1,0:T(8,128)(2,1)}, bf16[160,16,128]{2,1,0:T(8,128)(2,1)}, u32[]{:S(2)}, u32[]{:S(2)}) collective-permute-start(bf16[160,16,128]{2,1,0:T(8,128)(2,1)} %bitcast.24), channel_id=1, source_target_pairs={{0,2},{1,7},{2,4},{3,1},{4,6},{5,3},{6,0},{7,5},{8,10},{9,15},{10,... | collective-permute-start | bytes 1966088 | tf_op jit(solution)/shard_map/ppermute | solution.py:369
  12.2 4.8 %collective-permute-done.1.p1 = bf16[160,16,128]{2,1,0:T(8,128)(2,1)} collective-permute-done((bf16[160,16,128]{2,1,0:T(8,128)(2,1)}, bf16[160,16,128]{2,1,0:T(8,128)(2,1)}, u32[]{:S(2)}, u32[]{:S(2)}) %collective-permute-start.1) | collective-permute-done | bytes 655392 | tf_op jit(solution)/shard_map/ppermute | solution.py:369
  17.1 3.4 %collective-permute-start.3 = (bf16[160,16,128]{2,1,0:T(8,128)(2,1)}, bf16[160,16,128]{2,1,0:T(8,128)(2,1)}, u32[]{:S(2)}, u32[]{:S(2)}) collective-permute-start(bf16[160,16,128]{2,1,0:T(8,128)(2,1)} %collective-permute-done.1.p1), channel_id=1, source_target_pairs={{0,2},{1,7},{2,4},{3,1},{4,6},{5,3},{6,0},{7,5},{8,10},{9,15},{10,... | collective-permute-start | bytes 1966088 | tf_op jit(solution)/shard_map/ppermute | solution.py:369
  21.5 7.3 %collective-permute-done.9 = bf16[128,32,128]{2,1,0:T(8,128)(2,1)} collective-permute-done((bf16[128,32,128]{2,1,0:T(8,128)(2,1)S(1)}, bf16[128,32,128]{2,1,0:T(8,128)(2,1)}, u32[]{:S(2)}, u32[]{:S(2)}) %collective-permute-start.9) | collective-permute-done | bytes 1048608 | tf_op jit(solution)/shard_map/ppermute | solution.py:376
  28.7 2.1 %collective-permute-start.10 = (bf16[128,32,128]{2,1,0:T(8,128)(2,1)}, bf16[128,32,128]{2,1,0:T(8,128)(2,1)S(1)}, u32[]{:S(2)}, u32[]{:S(2)}) collective-permute-start(bf16[128,32,128]{2,1,0:T(8,128)(2,1)} %collective-permute-done.9), channel_id=1, source_target_pairs={{0,1},{1,0},{2,3},{3,2},{4,5},{5,4},{6,7},{7,6},{8,9},{9,8},{10,11... | collective-permute-start | bytes 3145736 | tf_op jit(solution)/shard_map/ppermute | solution.py:381
  33.5 1.9 %collective-permute-done.2.p2 = bf16[160,16,128]{2,1,0:T(8,128)(2,1)} collective-permute-done((bf16[160,16,128]{2,1,0:T(8,128)(2,1)}, bf16[160,16,128]{2,1,0:T(8,128)(2,1)}, u32[]{:S(2)}, u32[]{:S(2)}) %collective-permute-start.2) | collective-permute-done | bytes 655392 | tf_op jit(solution)/shard_map/ppermute | solution.py:369
  35.3 2.0 %collective-permute-start.5 = (bf16[160,16,128]{2,1,0:T(8,128)(2,1)}, bf16[160,16,128]{2,1,0:T(8,128)(2,1)}, u32[]{:S(2)}, u32[]{:S(2)}) collective-permute-start(bf16[160,16,128]{2,1,0:T(8,128)(2,1)} %collective-permute-done.2.p2), channel_id=1, source_target_pairs={{0,1},{1,0},{2,3},{3,2},{4,5},{5,4},{6,7},{7,6},{8,9},{9,8},{10,11... | collective-permute-start | bytes 1966088 | tf_op jit(solution)/shard_map/ppermute | solution.py:381
  38.2 1.3 collective-permute-done.5.s2
  39.4 3.5 %assemble.1 = (bf16[160,128,128]{2,1,0:T(8,128)(2,1)S(1)}, bf16[129,128,128]{2,1,0:T(8,128)(2,1)S(1)}) custom-call(s32[3]{0:T(128)S(1)} %pad_add_fusion.3.pos.refs_0_, bf16[160,16,128]{2,1,0:T(8,128)(2,1)} %bitcast.26, bf16[160,16,128]{2,1,0:T(8,128)(2,1)} %collective-permute-done.ap, bf16[160,16,128]{2,1,0:T(8,128)(2,1)} %collective-permute-done.1.p1, ...), custom_call_target="tpu_custom_call" | custom-call | tf_op jit(solution)/shard_map/assemble/pallas_call | solution.py:393
  42.9 2.2 %first0.1 = (s16[1040,128]{1,0:T(8,128)(2,1)S(1)}, s16[1040,128]{1,0:T(8,128)(2,1)S(1)}, bf16[129,128,128]{2,1,0:T(8,128)(2,1)S(1)}) custom-call(s32[3]{0:T(128)S(1)} %pad_add_fusion.3.pos.refs_0_, s32[1536]{0:T(1024)S(1)} %reshape.107.tab.refs_1_, bf16[160,128,128]{2,1,0:T(8,128)(2,1)S(1)} %get-tuple-element.31.a.refs_2_, ...), custom_call_target="tpu_custom_call", output_to_operand_aliasing={{2}: (3, {})} | custom-call | flops 2000000000 | bytes 6000000 | tf_op jit(solution)/shard_map/first0/pallas_call | solution.py:409
  45.2 1.6 %collective-permute-start.14 = (s16[1040,128]{1,0:T(8,128)(2,1)S(1)}, s16[1040,128]{1,0:T(8,128)(2,1)S(1)}, u32[]{:S(2)}, u32[]{:S(2)}) collective-permute-start(s16[1040,128]{1,0:T(8,128)(2,1)S(1)} %get-tuple-element.34.refs_4_), channel_id=1, source_target_pairs={{0,32},{32,64},{64,96},{96,128},{128,160},{160,192},{192,224},{224... | collective-permute-start | bytes 798728 | tf_op jit(solution)/shard_map/ppermute | solution.py:366
  46.7 4.0 %collective-permute-start.15 = (s16[1040,128]{1,0:T(8,128)(2,1)S(1)}, s16[1040,128]{1,0:T(8,128)(2,1)S(1)}, u32[]{:S(2)}, u32[]{:S(2)}) collective-permute-start(s16[1040,128]{1,0:T(8,128)(2,1)S(1)} %get-tuple-element.37), channel_id=1, source_target_pairs={{0,224},{32,0},{64,32},{96,64},{128,96},{160,128},{192,160},{224,1... | collective-permute-start | bytes 798728 | tf_op jit(solution)/shard_map/ppermute | solution.py:366
  50.8 2.1 %first1.1 = (s16[1040,128]{1,0:T(8,128)(2,1)S(1)}, s16[1040,128]{1,0:T(8,128)(2,1)S(1)}) custom-call(s32[3]{0:T(128)S(1)} %pad_add_fusion.3.pos.refs_0_, s32[1536]{0:T(1024)S(1)} %reshape.107.tab.refs_1_, bf16[160,128,128]{2,1,0:T(8,128)(2,1)S(1)} %get-tuple-element.31.a.refs_2_, bf16[129,128,128]{2,1,0:T(8,128)(2,1)S(1)} %get-tuple-element.33.refs_3_.b, ...), custom_call_target="tpu_custom_call" | custom-call | flops 2000000000 | bytes 6000000 | tf_op jit(solution)/shard_map/first1/pallas_call | solution.py:300
  53.0 2.7 %collective-permute-start.13 = (s16[1040,128]{1,0:T(8,128)(2,1)S(1)}, s16[1040,128]{1,0:T(8,128)(2,1)S(1)}, u32[]{:S(2)}, u32[]{:S(2)}) collective-permute-start(s16[1040,128]{1,0:T(8,128)(2,1)S(1)} %get-tuple-element.36), channel_id=1, source_target_pairs={{0,224},{32,0},{64,32},{96,64},{128,96},{160,128},{192,160},{224,1... | collective-permute-start | bytes 798728 | tf_op jit(solution)/shard_map/ppermute | solution.py:366
  55.6 1.5 %collective-permute-done.14.refs_4_ = s16[1040,128]{1,0:T(8,128)(2,1)S(1)} collective-permute-done((s16[1040,128]{1,0:T(8,128)(2,1)S(1)}, s16[1040,128]{1,0:T(8,128)(2,1)S(1)}, u32[]{:S(2)}, u32[]{:S(2)}) %collective-permute-start.14) | collective-permute-done | bytes 266272 | tf_op jit(solution)/shard_map/ppermute | solution.py:366
  57.1 3.5 %second0.1 = (s16[2064,128]{1,0:T(8,128)(2,1)S(1)}, s16[2064,128]{1,0:T(8,128)(2,1)S(1)}) custom-call(s32[3]{0:T(128)S(1)} %pad_add_fusion.3.pos.refs_0_, s32[1536]{0:T(1024)S(1)} %reshape.107.tab.refs_1_, bf16[160,128,128]{2,1,0:T(8,128)(2,1)S(1)} %get-tuple-element.31.a.refs_2_, bf16[129,128,128]{2,1,0:T(8,128)(2,1)S(1)} %get-tuple-element.33.refs_3_.b, ...), custom_call_target="tpu_custom_call" | custom-call | flops 3000000000 | bytes 9000000 | tf_op jit(solution)/shard_map/second0/pallas_call | solution.py:300
  60.8 2.7 %collective-permute-start.19 = (s16[2064,128]{1,0:T(8,128)(2,1)S(1)}, s16[2064,128]{1,0:T(8,128)(2,1)S(1)}, u32[]{:S(2)}, u32[]{:S(2)}) collective-permute-start(s16[2064,128]{1,0:T(8,128)(2,1)S(1)} %get-tuple-element.41), channel_id=1, source_target_pairs={{0,224},{32,0},{64,32},{96,64},{128,96},{160,128},{192,160},{224,1... | collective-permute-start | bytes 1585160 | tf_op jit(solution)/shard_map/ppermute | solution.py:366
  63.5 3.5 %second1.1 = (s16[2064,128]{1,0:T(8,128)(2,1)S(1)}, s16[2064,128]{1,0:T(8,128)(2,1)S(1)}) custom-call(s32[3]{0:T(128)S(1)} %pad_add_fusion.3.pos.refs_0_, s32[1536]{0:T(1024)S(1)} %reshape.107.tab.refs_1_, bf16[160,128,128]{2,1,0:T(8,128)(2,1)S(1)} %get-tuple-element.31.a.refs_2_, bf16[129,128,128]{2,1,0:T(8,128)(2,1)S(1)} %get-tuple-element.33.refs_3_.b, ...), custom_call_target="tpu_custom_call" | custom-call | flops 3000000000 | bytes 9000000 | tf_op jit(solution)/shard_map/second1/pallas_call | solution.py:300
  67.1 2.7 %collective-permute-start.17 = (s16[2064,128]{1,0:T(8,128)(2,1)S(1)}, s16[2064,128]{1,0:T(8,128)(2,1)S(1)}, u32[]{:S(2)}, u32[]{:S(2)}) collective-permute-start(s16[2064,128]{1,0:T(8,128)(2,1)S(1)} %get-tuple-element.40), channel_id=1, source_target_pairs={{0,224},{32,0},{64,32},{96,64},{128,96},{160,128},{192,160},{224,1... | collective-permute-start | bytes 1585160 | tf_op jit(solution)/shard_map/ppermute | solution.py:366
  69.8 4.2 %collective-permute-done.18.refs_4_ = s16[2064,128]{1,0:T(8,128)(2,1)S(1)} collective-permute-done((s16[2064,128]{1,0:T(8,128)(2,1)S(1)}, s16[2064,128]{1,0:T(8,128)(2,1)S(1)}, u32[]{:S(2)}, u32[]{:S(2)}) %collective-permute-start.18) | collective-permute-done | bytes 528416 | tf_op jit(solution)/shard_map/ppermute | solution.py:366
  74.0 3.6 %middle10.1 = (s16[2064,128]{1,0:T(8,128)(2,1)S(1)}, s16[2064,128]{1,0:T(8,128)(2,1)S(1)}) custom-call(s32[3]{0:T(128)S(1)} %pad_add_fusion.3.pos.refs_0_, s32[1536]{0:T(1024)S(1)} %reshape.107.tab.refs_1_, bf16[160,128,128]{2,1,0:T(8,128)(2,1)S(1)} %get-tuple-element.31.a.refs_2_, bf16[129,128,128]{2,1,0:T(8,128)(2,1)S(1)} %get-tuple-element.33.refs_3_.b, ...), custom_call_target="tpu_custom_call" | custom-call | flops 3000000000 | bytes 9000000 | tf_op jit(solution)/shard_map/middle10/pallas_call | solution.py:300
  77.6 0.8 collective-permute-start.22
  78.4 1.9 %collective-permute-start.23 = (s16[2064,128]{1,0:T(8,128)(2,1)S(1)}, s16[2064,128]{1,0:T(8,128)(2,1)S(1)}, u32[]{:S(2)}, u32[]{:S(2)}) collective-permute-start(s16[2064,128]{1,0:T(8,128)(2,1)S(1)} %get-tuple-element.45), channel_id=1, source_target_pairs={{0,224},{32,0},{64,32},{96,64},{128,96},{160,128},{192,160},{224,1... | collective-permute-start | bytes 1585160 | tf_op jit(solution)/shard_map/ppermute | solution.py:366
  80.3 5.0 %collective-permute-done.16.refs_4_ = s16[2064,128]{1,0:T(8,128)(2,1)S(1)} collective-permute-done((s16[2064,128]{1,0:T(8,128)(2,1)S(1)}, s16[2064,128]{1,0:T(8,128)(2,1)S(1)}, u32[]{:S(2)}, u32[]{:S(2)}) %collective-permute-start.16) | collective-permute-done | bytes 528416 | tf_op jit(solution)/shard_map/ppermute | solution.py:366
  85.3 3.6 %middle11.1 = (s16[2064,128]{1,0:T(8,128)(2,1)S(1)}, s16[2064,128]{1,0:T(8,128)(2,1)S(1)}) custom-call(s32[3]{0:T(128)S(1)} %pad_add_fusion.3.pos.refs_0_, s32[1536]{0:T(1024)S(1)} %reshape.107.tab.refs_1_, bf16[160,128,128]{2,1,0:T(8,128)(2,1)S(1)} %get-tuple-element.31.a.refs_2_, bf16[129,128,128]{2,1,0:T(8,128)(2,1)S(1)} %get-tuple-element.33.refs_3_.b, ...), custom_call_target="tpu_custom_call" | custom-call | flops 3000000000 | bytes 9000000 | tf_op jit(solution)/shard_map/middle11/pallas_call | solution.py:300
  89.7 1.9 %collective-permute-start.21 = (s16[2064,128]{1,0:T(8,128)(2,1)S(1)}, s16[2064,128]{1,0:T(8,128)(2,1)S(1)}, u32[]{:S(2)}, u32[]{:S(2)}) collective-permute-start(s16[2064,128]{1,0:T(8,128)(2,1)S(1)} %get-tuple-element.44), channel_id=1, source_target_pairs={{0,224},{32,0},{64,32},{96,64},{128,96},{160,128},{192,160},{224,1... | collective-permute-start | bytes 1585160 | tf_op jit(solution)/shard_map/ppermute | solution.py:366
  91.6 5.0 %collective-permute-done.22.refs_4_ = s16[2064,128]{1,0:T(8,128)(2,1)S(1)} collective-permute-done((s16[2064,128]{1,0:T(8,128)(2,1)S(1)}, s16[2064,128]{1,0:T(8,128)(2,1)S(1)}, u32[]{:S(2)}, u32[]{:S(2)}) %collective-permute-start.22) | collective-permute-done | bytes 528416 | tf_op jit(solution)/shard_map/ppermute | solution.py:366
  96.6 3.6 %middle20.1 = (s16[2064,128]{1,0:T(8,128)(2,1)S(1)}, s16[2064,128]{1,0:T(8,128)(2,1)S(1)}) custom-call(s32[3]{0:T(128)S(1)} %pad_add_fusion.3.pos.refs_0_, s32[1536]{0:T(1024)S(1)} %reshape.107.tab.refs_1_, bf16[160,128,128]{2,1,0:T(8,128)(2,1)S(1)} %get-tuple-element.31.a.refs_2_, bf16[129,128,128]{2,1,0:T(8,128)(2,1)S(1)} %get-tuple-element.33.refs_3_.b, ...), custom_call_target="tpu_custom_call" | custom-call | flops 3000000000 | bytes 9000000 | tf_op jit(solution)/shard_map/middle20/pallas_call | solution.py:300
  100.2 0.8 collective-permute-start.24
  101.0 1.9 %collective-permute-start.25 = (s16[2064,128]{1,0:T(8,128)(2,1)S(1)}, s16[2064,128]{1,0:T(8,128)(2,1)S(1)}, u32[]{:S(2)}, u32[]{:S(2)}) collective-permute-start(s16[2064,128]{1,0:T(8,128)(2,1)S(1)} %get-tuple-element.48), channel_id=1, source_target_pairs={{0,224},{32,0},{64,32},{96,64},{128,96},{160,128},{192,160},{224,1... | collective-permute-start | bytes 1585160 | tf_op jit(solution)/shard_map/ppermute | solution.py:366
  103.0 5.0 %collective-permute-done.20.refs_4_ = s16[2064,128]{1,0:T(8,128)(2,1)S(1)} collective-permute-done((s16[2064,128]{1,0:T(8,128)(2,1)S(1)}, s16[2064,128]{1,0:T(8,128)(2,1)S(1)}, u32[]{:S(2)}, u32[]{:S(2)}) %collective-permute-start.20) | collective-permute-done | bytes 528416 | tf_op jit(solution)/shard_map/ppermute | solution.py:366
  108.0 3.6 %middle21.1 = (s16[2064,128]{1,0:T(8,128)(2,1)S(1)}, s16[2064,128]{1,0:T(8,128)(2,1)S(1)}) custom-call(s32[3]{0:T(128)S(1)} %pad_add_fusion.3.pos.refs_0_, s32[1536]{0:T(1024)S(1)} %reshape.107.tab.refs_1_, bf16[160,128,128]{2,1,0:T(8,128)(2,1)S(1)} %get-tuple-element.31.a.refs_2_, bf16[129,128,128]{2,1,0:T(8,128)(2,1)S(1)} %get-tuple-element.33.refs_3_.b, ...), custom_call_target="tpu_custom_call" | custom-call | flops 3000000000 | bytes 9000000 | tf_op jit(solution)/shard_map/middle21/pallas_call | solution.py:300
  111.5 0.8 collective-permute-start.29
  112.3 1.9 %collective-permute-start.30 = (s16[2064,128]{1,0:T(8,128)(2,1)S(1)}, s16[2064,128]{1,0:T(8,128)(2,1)S(1)}, u32[]{:S(2)}, u32[]{:S(2)}) collective-permute-start(s16[2064,128]{1,0:T(8,128)(2,1)S(1)} %get-tuple-element.52), channel_id=1, source_target_pairs={{0,224},{32,0},{64,32},{96,64},{128,96},{160,128},{192,160},{224,1... | collective-permute-start | bytes 1585160 | tf_op jit(solution)/shard_map/ppermute | solution.py:366
  114.3 3.3 %own.1 = f32[32,128,128]{2,1,0:T(8,128)S(1)} custom-call(s32[3]{0:T(128)S(1)} %pad_add_fusion.3.pos.refs_0_, s32[1536]{0:T(1024)S(1)} %reshape.107.tab.refs_1_, bf16[160,128,128]{2,1,0:T(8,128)(2,1)S(1)} %get-tuple-element.31.a.refs_2_, bf16[129,128,128]{2,1,0:T(8,128)(2,1)S(1)} %get-tuple-element.33.refs_3_.b, s16[2064,128]{1,0:T(8,128)(2,1)S(1)} %get-tuple-element.47.unused), custom_call_target="tpu_custom_call" | custom-call | flops 3000000000 | bytes 9000000 | tf_op jit(solution)/shard_map/own/pallas_call | solution.py:316
  117.6 1.7 %collective-permute-done.24.in_r = s16[2064,128]{1,0:T(8,128)(2,1)S(1)} collective-permute-done((s16[2064,128]{1,0:T(8,128)(2,1)S(1)}, s16[2064,128]{1,0:T(8,128)(2,1)S(1)}, u32[]{:S(2)}, u32[]{:S(2)}) %collective-permute-start.24) | collective-permute-done | bytes 528416 | tf_op jit(solution)/shard_map/ppermute | solution.py:366
  119.9 3.6 %collective-permute-start.26 = (s16[2,528,128]{2,1,0:T(8,128)(2,1)S(1)}, s16[2,528,128]{2,1,0:T(8,128)(2,1)S(1)}, u32[]{:S(2)}, u32[]{:S(2)}) collective-permute-start(s16[2,528,128]{2,1,0:T(8,128)(2,1)S(1)} %get-tuple-element.49), channel_id=1, source_target_pairs={{0,4},{1,5},{2,6},{3,7},{4,0},{5,1},{6,2},{7,3},{8,12},{9,13},{10,... | collective-permute-start | bytes 811016 | tf_op jit(solution)/shard_map/ppermute | solution.py:366
  123.5 7.2 %collective-permute-done.29.in_r = s16[2064,128]{1,0:T(8,128)(2,1)S(1)} collective-permute-done((s16[2064,128]{1,0:T(8,128)(2,1)S(1)}, s16[2064,128]{1,0:T(8,128)(2,1)S(1)}, u32[]{:S(2)}, u32[]{:S(2)}) %collective-permute-start.29) | collective-permute-done | bytes 528416 | tf_op jit(solution)/shard_map/ppermute | solution.py:366
  131.1 2.5 %collective-permute-start.32 = (s16[2,272,128]{2,1,0:T(8,128)(2,1)S(1)}, s16[2,272,128]{2,1,0:T(8,128)(2,1)S(1)}, u32[]{:S(2)}, u32[]{:S(2)}) collective-permute-start(s16[2,272,128]{2,1,0:T(8,128)(2,1)S(1)} %get-tuple-element.54), channel_id=1, source_target_pairs={{0,6},{1,7},{2,0},{3,1},{4,2},{5,3},{6,4},{7,5},{8,14},{9,15},{10,... | collective-permute-start | bytes 417800 | tf_op jit(solution)/shard_map/ppermute | solution.py:366
  133.6 2.4 %collective-permute-start.33 = (s16[1072,128]{1,0:T(8,128)(2,1)S(1)}, s16[1072,128]{1,0:T(8,128)(2,1)S(1)}, u32[]{:S(2)}, u32[]{:S(2)}) collective-permute-start(s16[1072,128]{1,0:T(8,128)(2,1)S(1)} %pad_add_fusion), channel_id=1, source_target_pairs={{0,1},{1,0},{2,3},{3,2},{4,5},{5,4},{6,7},{7,6},{8,9},{9,8},{10,11... | collective-permute-start | bytes 823304 | tf_op jit(solution)/shard_map/ppermute | solution.py:381
  136.0 2.6 %collective-permute-done.31.up1 = s16[2,272,128]{2,1,0:T(8,128)(2,1)S(1)} collective-permute-done((s16[2,272,128]{2,1,0:T(8,128)(2,1)S(1)}, s16[2,272,128]{2,1,0:T(8,128)(2,1)S(1)}, u32[]{:S(2)}, u32[]{:S(2)}) %collective-permute-start.31) | collective-permute-done | bytes 139296 | tf_op jit(solution)/shard_map/ppermute | solution.py:366
  138.7 3.5 %collective-permute-start.34 = (s16[544,128]{1,0:T(8,128)(2,1)S(1)}, s16[544,128]{1,0:T(8,128)(2,1)S(1)}, u32[]{:S(2)}, u32[]{:S(2)}) collective-permute-start(s16[544,128]{1,0:T(8,128)(2,1)S(1)} %pad_add_fusion.1), channel_id=1, source_target_pairs={{0,1},{1,0},{2,3},{3,2},{4,5},{5,4},{6,7},{7,6},{8,9},{9,8},{10,11... | collective-permute-start | bytes 417800 | tf_op jit(solution)/shard_map/ppermute | solution.py:381
  142.3 1.3 collective-permute-done.35.cross
  143.6 2.1 %deliver.1 = f32[32,128,128]{2,1,0:T(8,128)} custom-call(s32[3]{0:T(128)S(1)} %pad_add_fusion.3.pos.refs_0_, s16[2,528,128]{2,1,0:T(8,128)(2,1)S(1)} %collective-permute-done.26.far, s16[2,272,128]{2,1,0:T(8,128)(2,1)S(1)} %collective-permute-done.27.unused.up0, s16[2,272,128]{2,1,0:T(8,128)(2,1)S(1)} %collective-permute-done.28.down0, ...), custom_call_target="tpu_custom_call" | custom-call | flops 1000000000 | bytes 3000000 | tf_op jit(solution)/shard_map/deliver/pallas_call | solution.py:345
  (68 shorter events, 9.6 us)
Async XLA Ops:
  0.0 5.7 %collective-permute-start.8 = (bf16[128,32,128]{2,1,0:T(8,128)(2,1)}, bf16[128,32,128]{2,1,0:T(8,128)(2,1)S(1)}, u32[]{:S(2)}, u32[]{:S(2)}) collective-permute-start(bf16[128,32,128]{2,1,0:T(8,128)(2,1)} %bitcast.21), channel_id=1, source_target_pairs={{0,1},{1,0},{2,3},{3,2},{4,5},{5,4},{6,7},{7,6},{8,9},{9,8},{10,11... | collective-permute-start | bytes 3145736 | tf_op jit(solution)/shard_map/ppermute | solution.py:381
  3.2 18.0 %collective-permute-start.7 = (bf16[128,32,128]{2,1,0:T(8,128)(2,1)}, bf16[128,32,128]{2,1,0:T(8,128)(2,1)S(1)}, u32[]{:S(2)}, u32[]{:S(2)}) collective-permute-start(bf16[128,32,128]{2,1,0:T(8,128)(2,1)} %bitcast.22), channel_id=1, source_target_pairs={{0,8},{1,25},{2,10},{3,27},{4,12},{5,29},{6,14},{7,31},{8,16},{9,1... | collective-permute-start | bytes 3145736 | tf_op jit(solution)/shard_map/ppermute | solution.py:376
  5.7 23.0 %collective-permute-start.9 = (bf16[128,32,128]{2,1,0:T(8,128)(2,1)S(1)}, bf16[128,32,128]{2,1,0:T(8,128)(2,1)}, u32[]{:S(2)}, u32[]{:S(2)}) collective-permute-start(bf16[128,32,128]{2,1,0:T(8,128)(2,1)S(1)} %collective-permute-done.8), channel_id=1, source_target_pairs={{0,8},{1,25},{2,10},{3,27},{4,12},{5,29},{6,14},{7,31},{8,16},{9,1... | collective-permute-start | bytes 3145736 | tf_op jit(solution)/shard_map/ppermute | solution.py:376
  6.7 10.3 %collective-permute-start.1 = (bf16[160,16,128]{2,1,0:T(8,128)(2,1)}, bf16[160,16,128]{2,1,0:T(8,128)(2,1)}, u32[]{:S(2)}, u32[]{:S(2)}) collective-permute-start(bf16[160,16,128]{2,1,0:T(8,128)(2,1)} %bitcast.24), channel_id=1, source_target_pairs={{0,2},{1,7},{2,4},{3,1},{4,6},{5,3},{6,0},{7,5},{8,10},{9,15},{10,... | collective-permute-start | bytes 1966088 | tf_op jit(solution)/shard_map/ppermute | solution.py:369
  9.2 11.3 %collective-permute-start = (bf16[160,16,128]{2,1,0:T(8,128)(2,1)}, bf16[160,16,128]{2,1,0:T(8,128)(2,1)}, u32[]{:S(2)}, u32[]{:S(2)}) collective-permute-start(bf16[160,16,128]{2,1,0:T(8,128)(2,1)} %bitcast.25), channel_id=1, source_target_pairs={{0,1},{1,0},{2,3},{3,2},{4,5},{5,4},{6,7},{7,6},{8,9},{9,8},{10,11... | collective-permute-start | bytes 1966088 | tf_op jit(solution)/shard_map/ppermute | solution.py:381
  17.1 15.9 %collective-permute-start.3 = (bf16[160,16,128]{2,1,0:T(8,128)(2,1)}, bf16[160,16,128]{2,1,0:T(8,128)(2,1)}, u32[]{:S(2)}, u32[]{:S(2)}) collective-permute-start(bf16[160,16,128]{2,1,0:T(8,128)(2,1)} %collective-permute-done.1.p1), channel_id=1, source_target_pairs={{0,2},{1,7},{2,4},{3,1},{4,6},{5,3},{6,0},{7,5},{8,10},{9,15},{10,... | collective-permute-start | bytes 1966088 | tf_op jit(solution)/shard_map/ppermute | solution.py:369
  20.5 14.9 %collective-permute-start.2 = (bf16[160,16,128]{2,1,0:T(8,128)(2,1)}, bf16[160,16,128]{2,1,0:T(8,128)(2,1)}, u32[]{:S(2)}, u32[]{:S(2)}) collective-permute-start(bf16[160,16,128]{2,1,0:T(8,128)(2,1)} %collective-permute-done.ap), channel_id=1, source_target_pairs={{0,2},{1,7},{2,4},{3,1},{4,6},{5,3},{6,0},{7,5},{8,10},{9,15},{10,... | collective-permute-start | bytes 1966088 | tf_op jit(solution)/shard_map/ppermute | solution.py:369
  21.2 21.7 %collective-permute-start.11 = (bf16[128,32,128]{2,1,0:T(8,128)(2,1)S(1)}, bf16[128,32,128]{2,1,0:T(8,128)(2,1)S(1)}, u32[]{:S(2)}, u32[]{:S(2)}) collective-permute-start(bf16[128,32,128]{2,1,0:T(8,128)(2,1)S(1)} %collective-permute-done.7.q1), channel_id=1, source_target_pairs={{0,8},{1,25},{2,10},{3,27},{4,12},{5,29},{6,14},{7,31},{8,16},{9,1... | collective-permute-start | bytes 3145736 | tf_op jit(solution)/shard_map/ppermute | solution.py:376
  28.7 10.7 %collective-permute-start.10 = (bf16[128,32,128]{2,1,0:T(8,128)(2,1)}, bf16[128,32,128]{2,1,0:T(8,128)(2,1)S(1)}, u32[]{:S(2)}, u32[]{:S(2)}) collective-permute-start(bf16[128,32,128]{2,1,0:T(8,128)(2,1)} %collective-permute-done.9), channel_id=1, source_target_pairs={{0,1},{1,0},{2,3},{3,2},{4,5},{5,4},{6,7},{7,6},{8,9},{9,8},{10,11... | collective-permute-start | bytes 3145736 | tf_op jit(solution)/shard_map/ppermute | solution.py:381
  32.8 5.3 %collective-permute-start.4 = (bf16[160,16,128]{2,1,0:T(8,128)(2,1)}, bf16[160,16,128]{2,1,0:T(8,128)(2,1)}, u32[]{:S(2)}, u32[]{:S(2)}) collective-permute-start(bf16[160,16,128]{2,1,0:T(8,128)(2,1)} %collective-permute-done.1.p1), channel_id=1, source_target_pairs={{0,1},{1,0},{2,3},{3,2},{4,5},{5,4},{6,7},{7,6},{8,9},{9,8},{10,11... | collective-permute-start | bytes 1966088 | tf_op jit(solution)/shard_map/ppermute | solution.py:381
  33.0 5.2 %collective-permute-start.6 = (bf16[160,16,128]{2,1,0:T(8,128)(2,1)}, bf16[160,16,128]{2,1,0:T(8,128)(2,1)}, u32[]{:S(2)}, u32[]{:S(2)}) collective-permute-start(bf16[160,16,128]{2,1,0:T(8,128)(2,1)} %collective-permute-done.3.p3), channel_id=1, source_target_pairs={{0,1},{1,0},{2,3},{3,2},{4,5},{5,4},{6,7},{7,6},{8,9},{9,8},{10,11... | collective-permute-start | bytes 1966088 | tf_op jit(solution)/shard_map/ppermute | solution.py:381
  35.3 4.1 %collective-permute-start.5 = (bf16[160,16,128]{2,1,0:T(8,128)(2,1)}, bf16[160,16,128]{2,1,0:T(8,128)(2,1)}, u32[]{:S(2)}, u32[]{:S(2)}) collective-permute-start(bf16[160,16,128]{2,1,0:T(8,128)(2,1)} %collective-permute-done.2.p2), channel_id=1, source_target_pairs={{0,1},{1,0},{2,3},{3,2},{4,5},{5,4},{6,7},{7,6},{8,9},{9,8},{10,11... | collective-permute-start | bytes 1966088 | tf_op jit(solution)/shard_map/ppermute | solution.py:381
  45.2 12.0 %collective-permute-start.14 = (s16[1040,128]{1,0:T(8,128)(2,1)S(1)}, s16[1040,128]{1,0:T(8,128)(2,1)S(1)}, u32[]{:S(2)}, u32[]{:S(2)}) collective-permute-start(s16[1040,128]{1,0:T(8,128)(2,1)S(1)} %get-tuple-element.34.refs_4_), channel_id=1, source_target_pairs={{0,32},{32,64},{64,96},{96,128},{128,160},{160,192},{192,224},{224... | collective-permute-start | bytes 798728 | tf_op jit(solution)/shard_map/ppermute | solution.py:366
  46.7 10.4 %collective-permute-start.15 = (s16[1040,128]{1,0:T(8,128)(2,1)S(1)}, s16[1040,128]{1,0:T(8,128)(2,1)S(1)}, u32[]{:S(2)}, u32[]{:S(2)}) collective-permute-start(s16[1040,128]{1,0:T(8,128)(2,1)S(1)} %get-tuple-element.37), channel_id=1, source_target_pairs={{0,224},{32,0},{64,32},{96,64},{128,96},{160,128},{192,160},{224,1... | collective-permute-start | bytes 798728 | tf_op jit(solution)/shard_map/ppermute | solution.py:366
  52.9 10.6 %collective-permute-start.12 = (s16[1040,128]{1,0:T(8,128)(2,1)S(1)}, s16[1040,128]{1,0:T(8,128)(2,1)S(1)}, u32[]{:S(2)}, u32[]{:S(2)}) collective-permute-start(s16[1040,128]{1,0:T(8,128)(2,1)S(1)} %get-tuple-element.35.refs_6_), channel_id=1, source_target_pairs={{0,32},{32,64},{64,96},{96,128},{128,160},{160,192},{192,224},{224... | collective-permute-start | bytes 798728 | tf_op jit(solution)/shard_map/ppermute | solution.py:366
  53.0 10.5 %collective-permute-start.13 = (s16[1040,128]{1,0:T(8,128)(2,1)S(1)}, s16[1040,128]{1,0:T(8,128)(2,1)S(1)}, u32[]{:S(2)}, u32[]{:S(2)}) collective-permute-start(s16[1040,128]{1,0:T(8,128)(2,1)S(1)} %get-tuple-element.36), channel_id=1, source_target_pairs={{0,224},{32,0},{64,32},{96,64},{128,96},{160,128},{192,160},{224,1... | collective-permute-start | bytes 798728 | tf_op jit(solution)/shard_map/ppermute | solution.py:366
  60.7 13.3 %collective-permute-start.18 = (s16[2064,128]{1,0:T(8,128)(2,1)S(1)}, s16[2064,128]{1,0:T(8,128)(2,1)S(1)}, u32[]{:S(2)}, u32[]{:S(2)}) collective-permute-start(s16[2064,128]{1,0:T(8,128)(2,1)S(1)} %get-tuple-element.38.refs_6_), channel_id=1, source_target_pairs={{0,32},{32,64},{64,96},{96,128},{128,160},{160,192},{192,224},{224... | collective-permute-start | bytes 1585160 | tf_op jit(solution)/shard_map/ppermute | solution.py:366
  60.8 13.2 %collective-permute-start.19 = (s16[2064,128]{1,0:T(8,128)(2,1)S(1)}, s16[2064,128]{1,0:T(8,128)(2,1)S(1)}, u32[]{:S(2)}, u32[]{:S(2)}) collective-permute-start(s16[2064,128]{1,0:T(8,128)(2,1)S(1)} %get-tuple-element.41), channel_id=1, source_target_pairs={{0,224},{32,0},{64,32},{96,64},{128,96},{160,128},{192,160},{224,1... | collective-permute-start | bytes 1585160 | tf_op jit(solution)/shard_map/ppermute | solution.py:366
  67.0 18.3 %collective-permute-start.16 = (s16[2064,128]{1,0:T(8,128)(2,1)S(1)}, s16[2064,128]{1,0:T(8,128)(2,1)S(1)}, u32[]{:S(2)}, u32[]{:S(2)}) collective-permute-start(s16[2064,128]{1,0:T(8,128)(2,1)S(1)} %get-tuple-element.39.refs_6_), channel_id=1, source_target_pairs={{0,32},{32,64},{64,96},{96,128},{128,160},{160,192},{192,224},{224... | collective-permute-start | bytes 1585160 | tf_op jit(solution)/shard_map/ppermute | solution.py:366
  67.1 18.2 %collective-permute-start.17 = (s16[2064,128]{1,0:T(8,128)(2,1)S(1)}, s16[2064,128]{1,0:T(8,128)(2,1)S(1)}, u32[]{:S(2)}, u32[]{:S(2)}) collective-permute-start(s16[2064,128]{1,0:T(8,128)(2,1)S(1)} %get-tuple-element.40), channel_id=1, source_target_pairs={{0,224},{32,0},{64,32},{96,64},{128,96},{160,128},{192,160},{224,1... | collective-permute-start | bytes 1585160 | tf_op jit(solution)/shard_map/ppermute | solution.py:366
  77.6 19.1 %collective-permute-start.22 = (s16[2064,128]{1,0:T(8,128)(2,1)S(1)}, s16[2064,128]{1,0:T(8,128)(2,1)S(1)}, u32[]{:S(2)}, u32[]{:S(2)}) collective-permute-start(s16[2064,128]{1,0:T(8,128)(2,1)S(1)} %get-tuple-element.42.refs_6_), channel_id=1, source_target_pairs={{0,32},{32,64},{64,96},{96,128},{128,160},{160,192},{192,224},{224... | collective-permute-start | bytes 1585160 | tf_op jit(solution)/shard_map/ppermute | solution.py:366
  78.4 18.3 %collective-permute-start.23 = (s16[2064,128]{1,0:T(8,128)(2,1)S(1)}, s16[2064,128]{1,0:T(8,128)(2,1)S(1)}, u32[]{:S(2)}, u32[]{:S(2)}) collective-permute-start(s16[2064,128]{1,0:T(8,128)(2,1)S(1)} %get-tuple-element.45), channel_id=1, source_target_pairs={{0,224},{32,0},{64,32},{96,64},{128,96},{160,128},{192,160},{224,1... | collective-permute-start | bytes 1585160 | tf_op jit(solution)/shard_map/ppermute | solution.py:366
  88.9 19.1 %collective-permute-start.20 = (s16[2064,128]{1,0:T(8,128)(2,1)S(1)}, s16[2064,128]{1,0:T(8,128)(2,1)S(1)}, u32[]{:S(2)}, u32[]{:S(2)}) collective-permute-start(s16[2064,128]{1,0:T(8,128)(2,1)S(1)} %get-tuple-element.43.refs_6_), channel_id=1, source_target_pairs={{0,32},{32,64},{64,96},{96,128},{128,160},{160,192},{192,224},{224... | collective-permute-start | bytes 1585160 | tf_op jit(solution)/shard_map/ppermute | solution.py:366
  89.7 18.3 %collective-permute-start.21 = (s16[2064,128]{1,0:T(8,128)(2,1)S(1)}, s16[2064,128]{1,0:T(8,128)(2,1)S(1)}, u32[]{:S(2)}, u32[]{:S(2)}) collective-permute-start(s16[2064,128]{1,0:T(8,128)(2,1)S(1)} %get-tuple-element.44), channel_id=1, source_target_pairs={{0,224},{32,0},{64,32},{96,64},{128,96},{160,128},{192,160},{224,1... | collective-permute-start | bytes 1585160 | tf_op jit(solution)/shard_map/ppermute | solution.py:366
  100.2 19.1 %collective-permute-start.24 = (s16[2064,128]{1,0:T(8,128)(2,1)S(1)}, s16[2064,128]{1,0:T(8,128)(2,1)S(1)}, u32[]{:S(2)}, u32[]{:S(2)}) collective-permute-start(s16[2064,128]{1,0:T(8,128)(2,1)S(1)} %get-tuple-element.46.refs_6_), channel_id=1, source_target_pairs={{0,32},{32,64},{64,96},{96,128},{128,160},{160,192},{192,224},{224... | collective-permute-start | bytes 1585160 | tf_op jit(solution)/shard_map/ppermute | solution.py:366
  101.0 18.3 %collective-permute-start.25 = (s16[2064,128]{1,0:T(8,128)(2,1)S(1)}, s16[2064,128]{1,0:T(8,128)(2,1)S(1)}, u32[]{:S(2)}, u32[]{:S(2)}) collective-permute-start(s16[2064,128]{1,0:T(8,128)(2,1)S(1)} %get-tuple-element.48), channel_id=1, source_target_pairs={{0,224},{32,0},{64,32},{96,64},{128,96},{160,128},{192,160},{224,1... | collective-permute-start | bytes 1585160 | tf_op jit(solution)/shard_map/ppermute | solution.py:366
  111.5 19.1 %collective-permute-start.29 = (s16[2064,128]{1,0:T(8,128)(2,1)S(1)}, s16[2064,128]{1,0:T(8,128)(2,1)S(1)}, u32[]{:S(2)}, u32[]{:S(2)}) collective-permute-start(s16[2064,128]{1,0:T(8,128)(2,1)S(1)} %get-tuple-element.47.unused), channel_id=1, source_target_pairs={{0,32},{32,64},{64,96},{96,128},{128,160},{160,192},{192,224},{224... | collective-permute-start | bytes 1585160 | tf_op jit(solution)/shard_map/ppermute | solution.py:366
  112.3 18.3 %collective-permute-start.30 = (s16[2064,128]{1,0:T(8,128)(2,1)S(1)}, s16[2064,128]{1,0:T(8,128)(2,1)S(1)}, u32[]{:S(2)}, u32[]{:S(2)}) collective-permute-start(s16[2064,128]{1,0:T(8,128)(2,1)S(1)} %get-tuple-element.52), channel_id=1, source_target_pairs={{0,224},{32,0},{64,32},{96,64},{128,96},{160,128},{192,160},{224,1... | collective-permute-start | bytes 1585160 | tf_op jit(solution)/shard_map/ppermute | solution.py:366
  119.8 10.8 %collective-permute-start.27 = (s16[2,272,128]{2,1,0:T(8,128)(2,1)S(1)}, s16[2,272,128]{2,1,0:T(8,128)(2,1)S(1)}, u32[]{:S(2)}, u32[]{:S(2)}) collective-permute-start(s16[2,272,128]{2,1,0:T(8,128)(2,1)S(1)} %get-tuple-element.50), channel_id=1, source_target_pairs={{0,2},{1,3},{2,4},{3,5},{4,6},{5,7},{6,0},{7,1},{8,10},{9,11},{10,... | collective-permute-start | bytes 417800 | tf_op jit(solution)/shard_map/ppermute | solution.py:366
  119.9 13.7 %collective-permute-start.26 = (s16[2,528,128]{2,1,0:T(8,128)(2,1)S(1)}, s16[2,528,128]{2,1,0:T(8,128)(2,1)S(1)}, u32[]{:S(2)}, u32[]{:S(2)}) collective-permute-start(s16[2,528,128]{2,1,0:T(8,128)(2,1)S(1)} %get-tuple-element.49), channel_id=1, source_target_pairs={{0,4},{1,5},{2,6},{3,7},{4,0},{5,1},{6,2},{7,3},{8,12},{9,13},{10,... | collective-permute-start | bytes 811016 | tf_op jit(solution)/shard_map/ppermute | solution.py:366
  123.4 10.1 %collective-permute-start.28 = (s16[2,272,128]{2,1,0:T(8,128)(2,1)S(1)}, s16[2,272,128]{2,1,0:T(8,128)(2,1)S(1)}, u32[]{:S(2)}, u32[]{:S(2)}) collective-permute-start(s16[2,272,128]{2,1,0:T(8,128)(2,1)S(1)} %get-tuple-element.51), channel_id=1, source_target_pairs={{0,6},{1,7},{2,0},{3,1},{4,2},{5,3},{6,4},{7,5},{8,14},{9,15},{10,... | collective-permute-start | bytes 417800 | tf_op jit(solution)/shard_map/ppermute | solution.py:366
  131.1 4.9 %collective-permute-start.32 = (s16[2,272,128]{2,1,0:T(8,128)(2,1)S(1)}, s16[2,272,128]{2,1,0:T(8,128)(2,1)S(1)}, u32[]{:S(2)}, u32[]{:S(2)}) collective-permute-start(s16[2,272,128]{2,1,0:T(8,128)(2,1)S(1)} %get-tuple-element.54), channel_id=1, source_target_pairs={{0,6},{1,7},{2,0},{3,1},{4,2},{5,3},{6,4},{7,5},{8,14},{9,15},{10,... | collective-permute-start | bytes 417800 | tf_op jit(solution)/shard_map/ppermute | solution.py:366
  133.6 5.1 %collective-permute-start.31 = (s16[2,272,128]{2,1,0:T(8,128)(2,1)S(1)}, s16[2,272,128]{2,1,0:T(8,128)(2,1)S(1)}, u32[]{:S(2)}, u32[]{:S(2)}) collective-permute-start(s16[2,272,128]{2,1,0:T(8,128)(2,1)S(1)} %get-tuple-element.53), channel_id=1, source_target_pairs={{0,2},{1,3},{2,4},{3,5},{4,6},{5,7},{6,0},{7,1},{8,10},{9,11},{10,... | collective-permute-start | bytes 417800 | tf_op jit(solution)/shard_map/ppermute | solution.py:366
  133.6 9.9 %collective-permute-start.33 = (s16[1072,128]{1,0:T(8,128)(2,1)S(1)}, s16[1072,128]{1,0:T(8,128)(2,1)S(1)}, u32[]{:S(2)}, u32[]{:S(2)}) collective-permute-start(s16[1072,128]{1,0:T(8,128)(2,1)S(1)} %pad_add_fusion), channel_id=1, source_target_pairs={{0,1},{1,0},{2,3},{3,2},{4,5},{5,4},{6,7},{7,6},{8,9},{9,8},{10,11... | collective-permute-start | bytes 823304 | tf_op jit(solution)/shard_map/ppermute | solution.py:381
  138.7 4.9 %collective-permute-start.34 = (s16[544,128]{1,0:T(8,128)(2,1)S(1)}, s16[544,128]{1,0:T(8,128)(2,1)S(1)}, u32[]{:S(2)}, u32[]{:S(2)}) collective-permute-start(s16[544,128]{1,0:T(8,128)(2,1)S(1)} %pad_add_fusion.1), channel_id=1, source_target_pairs={{0,1},{1,0},{2,3},{3,2},{4,5},{5,4},{6,7},{7,6},{8,9},{9,8},{10,11... | collective-permute-start | bytes 417800 | tf_op jit(solution)/shard_map/ppermute | solution.py:381
  142.2 1.4 collective-permute-start.35

commit v4 on v3

--- a/solution.py
+++ b/solution.py
@@ -73,7 +73,7 @@
     return started
 
 
-def assemble_kernel(pos, a0, ap, p1, p2, p3, s1, s2, s3, b0, q1, t2, a_out, b_out, sem):
+def assemble_kernel(pos, a0, ap, p1, p2, p3, s1, b0, q1, t2, a_out, b_out, sem):
     row, col = pos[1], pos[2]
     core = col % 2
     other = col + 1 - 2 * core
@@ -86,8 +86,6 @@
         (p2, a_place(a_out, other + ahead)),
         (p3, a_place(a_out, col + 4)),
         (s1, a_place(a_out, other - ahead)),
-        (s2, a_place(a_out, col - ahead)),
-        (s3, a_place(a_out, other + 4)),
         (b0, b_place(b_out, row, count)),
         (q1, b_place(b_out, row + 3 + 2 * core, count)),
         (t2, b_place(b_out, row + 1 + 2 * core, count)),
@@ -128,10 +126,16 @@
     out[pl.ds(row, CODE_ROWS), :] = codes[...].astype(jnp.int32).astype(I16)
 
 
-def finish_kernel(pos, tab, a, b_in, q3, out_r, out_l, b, code_r, code_l, sem):
-    late = pltpu.make_async_copy(q3, b_place(b, pos[1] + 2, q3.shape[0]), sem)
-    late.start()
-    late.wait()
+def finish_kernel(pos, tab, a_in, b_in, s2, s3, q3, out_r, out_l, a, b, code_r, code_l, sem):
+    row, col = pos[1], pos[2]
+    core = col % 2
+    copies = [
+        (s2, a_place(a, col + 2 - 4 * core)),
+        (s3, a_place(a, col + 5 - 2 * core)),
+        (q3, b_place(b, row + 2, q3.shape[0])),
+    ]
+    for one in copy_all(copies, sem):
+        one.wait()
     first_kernel(0, pos, tab, a, b, out_r, out_l, code_r, code_l)
 
 
@@ -141,14 +145,15 @@
     code_l[...] = jnp.zeros_like(code_l)
 
     def body(g, carry):
-        for u in range(2):
-            t = g * 2 + u
+        places = [g * 4 + u for u in range(4)]
+        sums = [(own_sum(tab, a, b, base + t), own_sum(tab, a, b, base + PART + t)) for t in places]
+        for t, (r, l) in zip(places, sums):
             row = pl.multiple_of(t * TILE, TILE)
-            encode(own_sum(tab, a, b, base + t), out_r, row, code_r, t)
-            encode(own_sum(tab, a, b, base + PART + t), out_l, row, code_l, t)
+            encode(r, out_r, row, code_r, t)
+            encode(l, out_l, row, code_l, t)
         return carry
 
-    lax.fori_loop(0, PART // 2, body, 0)
+    lax.fori_loop(0, PART // 4, body, 0)
     write_codes(code_r, out_r, HALF_ROWS)
     write_codes(code_l, out_l, HALF_ROWS)
 
@@ -159,16 +164,21 @@
     read_codes(in_r, HALF_ROWS, scale_r)
     read_codes(in_l, HALF_ROWS, scale_l)
 
-    def body(t, carry):
-        row = pl.multiple_of(t * TILE, TILE)
-        late = pl.multiple_of((t + PART) * TILE, TILE)
-        encode(own_sum(tab, a, b, base_r + t) + decoded(in_r, scale_r, t), out_r, row, code_r, t)
-        encode(own_sum(tab, a, b, base_r + PART + t), out_r, late, code_r, t + PART)
-        encode(own_sum(tab, a, b, base_l + t), out_l, row, code_l, t)
-        encode(own_sum(tab, a, b, base_l + PART + t) + decoded(in_l, scale_l, t), out_l, late, code_l, t + PART)
+    def body(g, carry):
+        places = [g * 2 + u for u in range(2)]
+        sums = []
+        for t in places:
+            sums.append([own_sum(tab, a, b, q + t) for q in (base_r, base_r + PART, base_l, base_l + PART)])
+        for t, (r, late_r, l, late_l) in zip(places, sums):
+            row = pl.multiple_of(t * TILE, TILE)
+            late = pl.multiple_of((t + PART) * TILE, TILE)
+            encode(r + decoded(in_r, scale_r, t), out_r, row, code_r, t)
+            encode(late_r, out_r, late, code_r, t + PART)
+            encode(l, out_l, row, code_l, t)
+            encode(late_l + decoded(in_l, scale_l, t), out_l, late, code_l, t + PART)
         return carry
 
-    lax.fori_loop(0, PART, body, 0)
+    lax.fori_loop(0, PART // 2, body, 0)
     write_codes(code_r, out_r, ROWS)
     write_codes(code_l, out_l, ROWS)
 
@@ -180,25 +190,27 @@
     read_codes(in_l, ROWS, scale_l)
 
     def body(g, carry):
-        for u in range(2):
-            t = g * 2 + u
+        places = [g * 4 + u for u in range(4)]
+        sums = [(own_sum(tab, a, b, base_r + t), own_sum(tab, a, b, base_l + t)) for t in places]
+        for t, (r, l) in zip(places, sums):
             row = pl.multiple_of(t * TILE, TILE)
-            encode(own_sum(tab, a, b, base_r + t) + decoded(in_r, scale_r, t), out_r, row, code_r, t)
-            encode(own_sum(tab, a, b, base_l + t) + decoded(in_l, scale_l, t), out_l, row, code_l, t)
+            encode(r + decoded(in_r, scale_r, t), out_r, row, code_r, t)
+            encode(l + decoded(in_l, scale_l, t), out_l, row, code_l, t)
         return carry
 
-    lax.fori_loop(0, SUB // 2, body, 0)
+    lax.fori_loop(0, SUB // 4, body, 0)
     write_codes(code_r, out_r, ROWS)
     write_codes(code_l, out_l, ROWS)
 
 
 def own_kernel(pos, tab, a, b, own):
     def body(g, carry):
-        for u in range(4):
-            own[g * 4 + u] = own_sum(tab, a, b, pos[0] * 32 + g * 4 + u)
+        sums = [own_sum(tab, a, b, pos[0] * 32 + g * 8 + u) for u in range(8)]
+        for u, one in enumerate(sums):
+            own[g * 8 + u] = one
         return carry
 
-    lax.fori_loop(0, own.shape[0] // 4, body, 0)
+    lax.fori_loop(0, own.shape[0] // 8, body, 0)
 
 
 def final_sum(own, in_r, in_l, scale_r, scale_l, h, t):
@@ -235,30 +247,52 @@
         home[n] = total(8 + n)
 
 
-def deliver_kernel(pos, far, up0, down0, up1, down1, swapped0, swapped1, cross, home, out, scale):
+def deliver_blocks(blocks, out, tiles, scale, sem):
+    started, at = [], 0
+    for n, (src, row, g, first, count) in enumerate(blocks):
+        read_codes(src, row + count * TILE, scale)
+        for m in range(count):
+            rows = src[row + m * TILE : row + (m + 1) * TILE, :].astype(jnp.int32).astype(F32)
+            tiles[at + m] = rows * scale[m : m + 1, :]
+        to = out.at[pl.ds((g + 8) % 8 * 4 + first, count)]
+        started.append(pltpu.make_async_copy(tiles.at[pl.ds(at, count)], to, sem.at[n]))
+        started[-1].start()
+        at += count
+    return started
+
+
+WIDE, SLIM = 4 * TILE + CODE_ROWS, 2 * TILE + CODE_ROWS
+
+
+def deliver_early_kernel(pos, far, up, down, swapped, home, out, tiles, scale, sem):
     col = pos[2]
     other = col + 1 - 2 * (col % 2)
-    wide, slim = 4 * TILE + CODE_ROWS, 2 * TILE + CODE_ROWS
-
-    def block(src, row, g, first, count):
-        read_codes(src, row + count * TILE, scale)
-        for n in range(count):
-            rows = src[row + n * TILE : row + (n + 1) * TILE, :].astype(jnp.int32).astype(F32)
-            out[(g + 8) % 8 * 4 + first + n] = rows * scale[n : n + 1, :]
-
-    block(far.at[0], 0, col + 4, 0, 4)
-    block(up0.at[0], 0, col - 2, 0, 2)
-    block(down0.at[0], 0, col + 2, 0, 2)
-    block(swapped0, 0, other + 4, 0, 4)
-    block(swapped0, wide, other - 2, 0, 2)
-    block(swapped0, wide + slim, other + 2, 0, 2)
-    block(up1.at[0], 0, col - 2, 2, 2)
-    block(down1.at[0], 0, col + 2, 2, 2)
-    block(swapped1, 0, other - 2, 2, 2)
-    block(swapped1, slim, other + 2, 2, 2)
-    block(cross, 0, other, 0, 4)
-    for n in range(4):
-        out[col * 4 + n] = home[n]
+    blocks = [
+        (far.at[0], 0, col + 4, 0, 4),
+        (up.at[0], 0, col - 2, 0, 2),
+        (down.at[0], 0, col + 2, 0, 2),
+        (swapped, 0, other + 4, 0, 4),
+        (swapped, WIDE, other - 2, 0, 2),
+        (swapped, WIDE + SLIM, other + 2, 0, 2),
+    ]
+    kept = pltpu.make_async_copy(home, out.at[pl.ds(col * 4, 4)], sem.at[len(blocks)])
+    kept.start()
+    for one in deliver_blocks(blocks, out, tiles, scale, sem) + [kept]:
+        one.wait()
+
+
+def deliver_late_kernel(pos, early, up, down, swapped, cross, out, tiles, scale, sem):
+    col = pos[2]
+    other = col + 1 - 2 * (col % 2)
+    blocks = [
+        (cross, 0, other, 0, 4),
+        (up.at[0], 0, col - 2, 2, 2),
+        (down.at[0], 0, col + 2, 2, 2),
+        (swapped, 0, other - 2, 2, 2),
+        (swapped, SLIM, other + 2, 2, 2),
+    ]
+    for one in deliver_blocks(blocks, out, tiles, scale, sem):
+        one.wait()
 
 
 SMEM_SPEC = pl.BlockSpec(memory_space=pltpu.SMEM)
@@ -341,16 +375,17 @@
     )(*args, after)
 
 
-def deliver(tiles, *args):
+def deliver(kernel, name, specs, tiles, moved, aliases, *args):
     return pl.pallas_call(
-        deliver_kernel,
+        kernel,
         out_shape=jax.ShapeDtypeStruct((tiles, TILE, TILE), F32),
-        in_specs=[SMEM_SPEC] + [VMEM_SPEC] * (len(args) - 1),
-        out_specs=VMEM_SPEC,
-        scratch_shapes=scratch(1),
+        in_specs=[SMEM_SPEC] + specs,
+        out_specs=ANY_SPEC,
+        scratch_shapes=[pltpu.VMEM((moved, TILE, TILE), F32)] + scratch(1) + [pltpu.SemaphoreType.DMA((7,))],
+        input_output_aliases=aliases,
         compiler_params=params(16),
         cost_estimate=cost(COST_LAST),
-        name="deliver",
+        name=name,
     )(*args)
 
 
@@ -389,40 +424,42 @@
     q3, p3 = y_split(q1), x_split(p1)
     t2, s1, s2, s3 = swap(q2), swap(p1), swap(p2), swap(p3)
     tab = make_table(a_kcol, b_jcol, c_jcol, c_place)
-    b_vmem = VM((b0.shape[0] + 1, TILE, TILE), BF16)
+    held = (VM((a0.shape[0], TILE, TILE), BF16), VM((b0.shape[0] + 1, TILE, TILE), BF16))
     a, b = pl.pallas_call(
         assemble_kernel,
-        out_shape=(VM((a0.shape[0], TILE, TILE), BF16), b_vmem),
-        in_specs=[SMEM_SPEC] + [ANY_SPEC] * 11,
+        out_shape=held,
+        in_specs=[SMEM_SPEC] + [ANY_SPEC] * 9,
         out_specs=(VMEM_SPEC, VMEM_SPEC),
-        scratch_shapes=[pltpu.SemaphoreType.DMA((11,))],
+        scratch_shapes=[pltpu.SemaphoreType.DMA((9,))],
         compiler_params=params(16),
         cost_estimate=cost(0),
         name="assemble",
-    )(pos, in_hbm(a0), ap, p1, p2, p3, s1, s2, s3, in_hbm(b0), q1, t2)
+    )(pos, in_hbm(a0), ap, p1, p2, p3, s1, in_hbm(b0), q1, t2)
 
     short = (message(HALF_ROWS),) * 2
     full = (message(ROWS),) * 2
     flying = []
     for h in range(2):
         if h == 0:
-            r, l, b = pl.pallas_call(
+            r, l, a, b = pl.pallas_call(
                 finish_kernel,
-                out_shape=short + (b_vmem,),
-                in_specs=[SMEM_SPEC] * 2 + [VMEM_SPEC] * 2 + [ANY_SPEC],
-                out_specs=(VMEM_SPEC,) * 3,
-                scratch_shapes=scratch(2) + [pltpu.SemaphoreType.DMA],
-                input_output_aliases={3: 2},
+                out_shape=short + held,
+                in_specs=[SMEM_SPEC] * 2 + [VMEM_SPEC] * 2 + [ANY_SPEC] * 3,
+                out_specs=(VMEM_SPEC,) * 4,
+                scratch_shapes=scratch(2) + [pltpu.SemaphoreType.DMA((3,))],
+                input_output_aliases={2: 2, 3: 3},
                 compiler_params=params(16),
                 cost_estimate=cost(COST_FIRST),
                 name="first0",
-            )(pos, tab, a, b, q3)
+            )(pos, tab, a, b, s2, s3, q3)
         else:
             r, l = step(functools.partial(first_kernel, h), f"first{h}", COST_FIRST, short, 2, r, pos, tab, a, b)
         flying.append((z_up(r), z_down(l)))
     for hop in range(3):
         landed, flying = flying, []
         for h in range(2):
+            if (hop, h) == (2, 1):
+                own = r = own_tiles(r, pos, tab, a, b)
             if hop == 0:
                 kernel, name = functools.partial(second_kernel, h), f"second{h}"
             else:
@@ -430,7 +467,6 @@
             weight = (COST_SECOND0, COST_SECOND1)[h] if hop == 0 else COST_MIDDLE
             r, l = step(kernel, name, weight, full, 4, r, pos, tab, a, b, *landed[h])
             flying.append((z_up(r), z_down(l)))
-    own = own_tiles(r, pos, tab, a, b)
     x_up, x_down, x_far = (shift("col", col, n) for n in (2, -2, 4))
     far, up, down = finals(spread_kernel, "spread", (coded(4, 2), coded(2, 2), coded(2, 2)), r, own, *flying[0])
     far, up, down = x_far(far), x_up(up), x_down(down)
@@ -443,9 +479,26 @@
         *flying[1],
     )
     up1, down1, cross = x_up(up1), x_down(down1), swap(cross)
+    far, down, home = lax.optimization_barrier((far, down, home))
     swapped = swap(jnp.concatenate([far[1], up[1], down[1]]))
+    early = deliver(
+        deliver_early_kernel, "deliver0", [VMEM_SPEC] * 5, col * 4, 16, {}, pos, far, up, down, swapped, home
+    )
     swapped1 = swap(jnp.concatenate([up1[1], down1[1]]))
-    return deliver(col * 4, pos, far, up, down, up1, down1, swapped, swapped1, cross, home)
+    return deliver(
+        deliver_late_kernel,
+        "deliver1",
+        [ANY_SPEC] + [VMEM_SPEC] * 4,
+        col * 4,
+        12,
+        {1: 0},
+        pos,
+        early,
+        up1,
+        down1,
+        swapped1,
+        cross,
+    )
 
 
 def solution(mesh):

time: 146 us -> 145 us (level)
  waiting for transfers between devices: 50.4 us -> 60.5 us
  starting transfers between devices: 53 us -> 45.7 us
  Pallas kernels: 35.5 us -> 31.5 us
    ppermute x21, waiting for transfers between devices: 32.3 us -> 44.9 us  [shift(): return lambda x: lax.ppermute(x, axis, pairs)]
    ppermute x21, starting transfers between devices: 31 us -> 23.4 us  [shift(): return lambda x: lax.ppermute(x, axis, pairs)]
    pallas_call x7, Pallas kernels: 23.4 us -> 18.7 us  [step(): pl.pallas_call(body, out_shape=out_shape, in_specs=ins, out_specs=jax.tre...]
    ppermute x9, waiting for transfers between devices: 4.04 us -> 1.65 us  [swap(): return lax.ppermute(x, 'col', [(i, i ^ 1) for i in range(col)])]
    pallas_call x3 -> x4, Pallas kernels: 7.83 us -> 9.25 us  [the longest x2 3.16 us: deliver(): pl.pallas_call(kernel, out_shape=jax.ShapeDtypeStruct((tiles, TILE, TILE)...]
  transfers between devices with their start and end apart: 36 -> 36, of which waited for: 14 -> 19; matrix products, arithmetic and copies ran while one was open for 4% -> 4% of each run, Pallas kernels for 21% -> 19%
where the time goes in v4:
time: 145 us
  waiting for transfers between devices  60.5 us (42%)
  starting transfers between devices  45.7 us (32%)
  Pallas kernels  31.5 us (22%)
  other arithmetic  4.21 us (3%)
  local copies, waits for them, and re-layouts  2.29 us (2%)
    ppermute x21, waiting for transfers between devices, shift(): return lambda x: lax.ppermute(x, axis, pairs)  44.9 us
    ppermute x21, starting transfers between devices, shift(): return lambda x: lax.ppermute(x, axis, pairs)  23.4 us
    pallas_call x7, Pallas kernels, step(): pl.pallas_call(body, out_shape=out_shape, in_specs=ins, out_specs=jax.tre...  18.7 us
    ppermute x9, starting transfers between devices, swap(): return lax.ppermute(x, 'col', [(i, i ^ 1) for i in range(col)])  14.1 us
    ppermute x3, waiting for transfers between devices, y_split(): return lax.ppermute(x, ('row', 'col'), pairs)  7.15 us
    ppermute x3, waiting for transfers between devices, x_split(): lax.ppermute(x, 'col', [(i, (i + 2 - 4 * (i % 2)) % col) for i in range(c...  6.86 us
    ppermute x3, starting transfers between devices, x_split(): lax.ppermute(x, 'col', [(i, (i + 2 - 4 * (i % 2)) % col) for i in range(c...  5.92 us
    pallas_call x2, Pallas kernels, deliver(): pl.pallas_call(kernel, out_shape=jax.ShapeDtypeStruct((tiles, TILE, TILE)...  3.16 us
  transfers between devices with their start and end apart: 36, of which 19 were waited for; matrix products, arithmetic and copies ran while one was open for 4% of the time, Pallas kernels for 19%

profile of v4, /device:TPU:1, one launch (start us, length us, event | category | flops | bytes accessed | tf_op | source)
XLA Modules:
  0.0 144.7 jit_solution(13596944690980520171)
XLA Ops:
  0.0 3.2 %collective-permute-start.6 = (bf16[128,32,128]{2,1,0:T(8,128)(2,1)}, bf16[128,32,128]{2,1,0:T(8,128)(2,1)}, u32[]{:S(2)}, u32[]{:S(2)}) collective-permute-start(bf16[128,32,128]{2,1,0:T(8,128)(2,1)} %bitcast.21), channel_id=1, source_target_pairs={{0,1},{1,0},{2,3},{3,2},{4,5},{5,4},{6,7},{7,6},{8,9},{9,8},{10,11... | collective-permute-start | bytes 3145736 | tf_op jit(solution)/shard_map/ppermute | solution.py:416
  4.2 1.6 %collective-permute-done.6 = bf16[128,32,128]{2,1,0:T(8,128)(2,1)} collective-permute-done((bf16[128,32,128]{2,1,0:T(8,128)(2,1)}, bf16[128,32,128]{2,1,0:T(8,128)(2,1)}, u32[]{:S(2)}, u32[]{:S(2)}) %collective-permute-start.6) | collective-permute-done | bytes 1048608 | tf_op jit(solution)/shard_map/ppermute | solution.py:416
  6.9 2.5 %collective-permute-start.1 = (bf16[160,16,128]{2,1,0:T(8,128)(2,1)}, bf16[160,16,128]{2,1,0:T(8,128)(2,1)}, u32[]{:S(2)}, u32[]{:S(2)}) collective-permute-start(bf16[160,16,128]{2,1,0:T(8,128)(2,1)} %bitcast.24), channel_id=1, source_target_pairs={{0,2},{1,7},{2,4},{3,1},{4,6},{5,3},{6,0},{7,5},{8,10},{9,15},{10,... | collective-permute-start | bytes 1966088 | tf_op jit(solution)/shard_map/ppermute | solution.py:404
  12.4 4.8 %collective-permute-done.1.p1 = bf16[160,16,128]{2,1,0:T(8,128)(2,1)} collective-permute-done((bf16[160,16,128]{2,1,0:T(8,128)(2,1)}, bf16[160,16,128]{2,1,0:T(8,128)(2,1)}, u32[]{:S(2)}, u32[]{:S(2)}) %collective-permute-start.1) | collective-permute-done | bytes 655392 | tf_op jit(solution)/shard_map/ppermute | solution.py:404
  17.2 3.4 %collective-permute-start.3 = (bf16[160,16,128]{2,1,0:T(8,128)(2,1)}, bf16[160,16,128]{2,1,0:T(8,128)(2,1)}, u32[]{:S(2)}, u32[]{:S(2)}) collective-permute-start(bf16[160,16,128]{2,1,0:T(8,128)(2,1)} %collective-permute-done.1.p1), channel_id=1, source_target_pairs={{0,2},{1,7},{2,4},{3,1},{4,6},{5,3},{6,0},{7,5},{8,10},{9,15},{10,... | collective-permute-start | bytes 1966088 | tf_op jit(solution)/shard_map/ppermute | solution.py:404
  21.6 7.1 %collective-permute-done.7 = bf16[128,32,128]{2,1,0:T(8,128)(2,1)} collective-permute-done((bf16[128,32,128]{2,1,0:T(8,128)(2,1)}, bf16[128,32,128]{2,1,0:T(8,128)(2,1)}, u32[]{:S(2)}, u32[]{:S(2)}) %collective-permute-start.7) | collective-permute-done | bytes 1048608 | tf_op jit(solution)/shard_map/ppermute | solution.py:411
  28.7 2.1 %collective-permute-start.8 = (bf16[128,32,128]{2,1,0:T(8,128)(2,1)}, bf16[128,32,128]{2,1,0:T(8,128)(2,1)S(1)}, u32[]{:S(2)}, u32[]{:S(2)}) collective-permute-start(bf16[128,32,128]{2,1,0:T(8,128)(2,1)} %collective-permute-done.7), channel_id=1, source_target_pairs={{0,1},{1,0},{2,3},{3,2},{4,5},{5,4},{6,7},{7,6},{8,9},{9,8},{10,11... | collective-permute-start | bytes 3145736 | tf_op jit(solution)/shard_map/ppermute | solution.py:416
  33.5 2.0 %collective-permute-done.2.p2 = bf16[160,16,128]{2,1,0:T(8,128)(2,1)} collective-permute-done((bf16[160,16,128]{2,1,0:T(8,128)(2,1)}, bf16[160,16,128]{2,1,0:T(8,128)(2,1)}, u32[]{:S(2)}, u32[]{:S(2)}) %collective-permute-start.2) | collective-permute-done | bytes 655392 | tf_op jit(solution)/shard_map/ppermute | solution.py:404
  35.5 2.0 %collective-permute-start.9 = (bf16[160,16,128]{2,1,0:T(8,128)(2,1)}, bf16[160,16,128]{2,1,0:T(8,128)(2,1)}, u32[]{:S(2)}, u32[]{:S(2)}) collective-permute-start(bf16[160,16,128]{2,1,0:T(8,128)(2,1)} %collective-permute-done.2.p2), channel_id=1, source_target_pairs={{0,1},{1,0},{2,3},{3,2},{4,5},{5,4},{6,7},{7,6},{8,9},{9,8},{10,11... | collective-permute-start | bytes 1966088 | tf_op jit(solution)/shard_map/ppermute | solution.py:416
  38.3 3.1 %assemble.1 = (bf16[160,128,128]{2,1,0:T(8,128)(2,1)S(1)}, bf16[129,128,128]{2,1,0:T(8,128)(2,1)S(1)}) custom-call(s32[3]{0:T(128)S(1)} %pad_add_fusion.3.pos.refs_0_, bf16[160,16,128]{2,1,0:T(8,128)(2,1)} %bitcast.26, bf16[160,16,128]{2,1,0:T(8,128)(2,1)} %collective-permute-done.ap, bf16[160,16,128]{2,1,0:T(8,128)(2,1)} %collective-permute-done.1.p1, ...), custom_call_target="tpu_custom_call" | custom-call | tf_op jit(solution)/shard_map/assemble/pallas_call | solution.py:428
  41.4 3.0 %first0.1 = (s16[1040,128]{1,0:T(8,128)(2,1)S(1)}, s16[1040,128]{1,0:T(8,128)(2,1)S(1)}, bf16[160,128,128]{2,1,0:T(8,128)(2,1)S(1)}, bf16[129,128,128]{2,1,0:T(8,128)(2,1)S(1)}) custom-call(s32[3]{0:T(128)S(1)} %pad_add_fusion.3.pos.refs_0_, s32[1536]{0:T(1024)S(1)} %reshape.107.tab.refs_1_, ...), custom_call_target="tpu_custom_call", output_to_operand_aliasing={{2}: (2, {}), {3}: (3, {})} | custom-call | flops 2000000000 | bytes 6000000 | tf_op jit(solution)/shard_map/first0/pallas_call | solution.py:444
  44.4 5.5 %collective-permute-start.13 = (s16[1040,128]{1,0:T(8,128)(2,1)S(1)}, s16[1040,128]{1,0:T(8,128)(2,1)S(1)}, u32[]{:S(2)}, u32[]{:S(2)}) collective-permute-start(s16[1040,128]{1,0:T(8,128)(2,1)S(1)} %get-tuple-element.40), channel_id=1, source_target_pairs={{0,224},{32,0},{64,32},{96,64},{128,96},{160,128},{192,160},{224,1... | collective-permute-start | bytes 798728 | tf_op jit(solution)/shard_map/ppermute | solution.py:401
  49.9 1.7 %first1.1 = (s16[1040,128]{1,0:T(8,128)(2,1)S(1)}, s16[1040,128]{1,0:T(8,128)(2,1)S(1)}) custom-call(s32[3]{0:T(128)S(1)} %pad_add_fusion.3.pos.refs_0_, s32[1536]{0:T(1024)S(1)} %reshape.107.tab.refs_1_, bf16[160,128,128]{2,1,0:T(8,128)(2,1)S(1)} %get-tuple-element.37.refs_2_.a, bf16[129,128,128]{2,1,0:T(8,128)(2,1)S(1)} %get-tuple-element.38.refs_3_.b, ...), custom_call_target="tpu_custom_call" | custom-call | flops 2000000000 | bytes 6000000 | tf_op jit(solution)/shard_map/first1/pallas_call | solution.py:334
  51.6 2.9 %collective-permute-start.17 = (s16[1040,128]{1,0:T(8,128)(2,1)S(1)}, s16[1040,128]{1,0:T(8,128)(2,1)S(1)}, u32[]{:S(2)}, u32[]{:S(2)}) collective-permute-start(s16[1040,128]{1,0:T(8,128)(2,1)S(1)} %get-tuple-element.44), channel_id=1, source_target_pairs={{0,224},{32,0},{64,32},{96,64},{128,96},{160,128},{192,160},{224,1... | collective-permute-start | bytes 798728 | tf_op jit(solution)/shard_map/ppermute | solution.py:401
  54.6 1.2 collective-permute-done.13.refs_5_
  55.7 3.1 %collective-permute-done.12.refs_4_ = s16[1040,128]{1,0:T(8,128)(2,1)S(1)} collective-permute-done((s16[1040,128]{1,0:T(8,128)(2,1)S(1)}, s16[1040,128]{1,0:T(8,128)(2,1)S(1)}, u32[]{:S(2)}, u32[]{:S(2)}) %collective-permute-start.12) | collective-permute-done | bytes 266272 | tf_op jit(solution)/shard_map/ppermute | solution.py:401
  58.8 2.8 %second0.1 = (s16[2064,128]{1,0:T(8,128)(2,1)S(1)}, s16[2064,128]{1,0:T(8,128)(2,1)S(1)}) custom-call(s32[3]{0:T(128)S(1)} %pad_add_fusion.3.pos.refs_0_, s32[1536]{0:T(1024)S(1)} %reshape.107.tab.refs_1_, bf16[160,128,128]{2,1,0:T(8,128)(2,1)S(1)} %get-tuple-element.37.refs_2_.a, bf16[129,128,128]{2,1,0:T(8,128)(2,1)S(1)} %get-tuple-element.38.refs_3_.b, ...), custom_call_target="tpu_custom_call" | custom-call | flops 3000000000 | bytes 9000000 | tf_op jit(solution)/shard_map/second0/pallas_call | solution.py:334
  62.1 1.1 collective-permute-start.14
  63.2 1.3 collective-permute-done.16.refs_4_
  64.5 2.8 %second1.1 = (s16[2064,128]{1,0:T(8,128)(2,1)S(1)}, s16[2064,128]{1,0:T(8,128)(2,1)S(1)}) custom-call(s32[3]{0:T(128)S(1)} %pad_add_fusion.3.pos.refs_0_, s32[1536]{0:T(1024)S(1)} %reshape.107.tab.refs_1_, bf16[160,128,128]{2,1,0:T(8,128)(2,1)S(1)} %get-tuple-element.37.refs_2_.a, bf16[129,128,128]{2,1,0:T(8,128)(2,1)S(1)} %get-tuple-element.38.refs_3_.b, ...), custom_call_target="tpu_custom_call" | custom-call | flops 3000000000 | bytes 9000000 | tf_op jit(solution)/shard_map/second1/pallas_call | solution.py:334
  67.8 1.1 collective-permute-start.20
  68.9 4.5 %collective-permute-done.15.refs_5_ = s16[2064,128]{1,0:T(8,128)(2,1)S(1)} collective-permute-done((s16[2064,128]{1,0:T(8,128)(2,1)S(1)}, s16[2064,128]{1,0:T(8,128)(2,1)S(1)}, u32[]{:S(2)}, u32[]{:S(2)}) %collective-permute-start.15) | collective-permute-done | bytes 528416 | tf_op jit(solution)/shard_map/ppermute | solution.py:401
  73.4 1.8 %collective-permute-done.14.refs_4_ = s16[2064,128]{1,0:T(8,128)(2,1)S(1)} collective-permute-done((s16[2064,128]{1,0:T(8,128)(2,1)S(1)}, s16[2064,128]{1,0:T(8,128)(2,1)S(1)}, u32[]{:S(2)}, u32[]{:S(2)}) %collective-permute-start.14) | collective-permute-done | bytes 528416 | tf_op jit(solution)/shard_map/ppermute | solution.py:401
  75.2 2.8 %middle10.1 = (s16[2064,128]{1,0:T(8,128)(2,1)S(1)}, s16[2064,128]{1,0:T(8,128)(2,1)S(1)}) custom-call(s32[3]{0:T(128)S(1)} %pad_add_fusion.3.pos.refs_0_, s32[1536]{0:T(1024)S(1)} %reshape.107.tab.refs_1_, bf16[160,128,128]{2,1,0:T(8,128)(2,1)S(1)} %get-tuple-element.37.refs_2_.a, bf16[129,128,128]{2,1,0:T(8,128)(2,1)S(1)} %get-tuple-element.38.refs_3_.b, ...), custom_call_target="tpu_custom_call" | custom-call | flops 3000000000 | bytes 9000000 | tf_op jit(solution)/shard_map/middle10/pallas_call | solution.py:334
  78.5 1.1 collective-permute-start.18
  79.6 5.2 %collective-permute-done.21.refs_5_ = s16[2064,128]{1,0:T(8,128)(2,1)S(1)} collective-permute-done((s16[2064,128]{1,0:T(8,128)(2,1)S(1)}, s16[2064,128]{1,0:T(8,128)(2,1)S(1)}, u32[]{:S(2)}, u32[]{:S(2)}) %collective-permute-start.21) | collective-permute-done | bytes 528416 | tf_op jit(solution)/shard_map/ppermute | solution.py:401
  84.8 1.8 %collective-permute-done.20.refs_4_ = s16[2064,128]{1,0:T(8,128)(2,1)S(1)} collective-permute-done((s16[2064,128]{1,0:T(8,128)(2,1)S(1)}, s16[2064,128]{1,0:T(8,128)(2,1)S(1)}, u32[]{:S(2)}, u32[]{:S(2)}) %collective-permute-start.20) | collective-permute-done | bytes 528416 | tf_op jit(solution)/shard_map/ppermute | solution.py:401
  86.5 2.8 %middle11.1 = (s16[2064,128]{1,0:T(8,128)(2,1)S(1)}, s16[2064,128]{1,0:T(8,128)(2,1)S(1)}) custom-call(s32[3]{0:T(128)S(1)} %pad_add_fusion.3.pos.refs_0_, s32[1536]{0:T(1024)S(1)} %reshape.107.tab.refs_1_, bf16[160,128,128]{2,1,0:T(8,128)(2,1)S(1)} %get-tuple-element.37.refs_2_.a, bf16[129,128,128]{2,1,0:T(8,128)(2,1)S(1)} %get-tuple-element.38.refs_3_.b, ...), custom_call_target="tpu_custom_call" | custom-call | flops 3000000000 | bytes 9000000 | tf_op jit(solution)/shard_map/middle11/pallas_call | solution.py:334
  89.8 1.1 collective-permute-start.24
  90.9 5.2 %collective-permute-done.19.refs_5_ = s16[2064,128]{1,0:T(8,128)(2,1)S(1)} collective-permute-done((s16[2064,128]{1,0:T(8,128)(2,1)S(1)}, s16[2064,128]{1,0:T(8,128)(2,1)S(1)}, u32[]{:S(2)}, u32[]{:S(2)}) %collective-permute-start.19) | collective-permute-done | bytes 528416 | tf_op jit(solution)/shard_map/ppermute | solution.py:401
  96.1 1.8 %collective-permute-done.18.refs_4_ = s16[2064,128]{1,0:T(8,128)(2,1)S(1)} collective-permute-done((s16[2064,128]{1,0:T(8,128)(2,1)S(1)}, s16[2064,128]{1,0:T(8,128)(2,1)S(1)}, u32[]{:S(2)}, u32[]{:S(2)}) %collective-permute-start.18) | collective-permute-done | bytes 528416 | tf_op jit(solution)/shard_map/ppermute | solution.py:401
  97.8 2.8 %middle20.1 = (s16[2064,128]{1,0:T(8,128)(2,1)S(1)}, s16[2064,128]{1,0:T(8,128)(2,1)S(1)}) custom-call(s32[3]{0:T(128)S(1)} %pad_add_fusion.3.pos.refs_0_, s32[1536]{0:T(1024)S(1)} %reshape.107.tab.refs_1_, bf16[160,128,128]{2,1,0:T(8,128)(2,1)S(1)} %get-tuple-element.37.refs_2_.a, bf16[129,128,128]{2,1,0:T(8,128)(2,1)S(1)} %get-tuple-element.38.refs_3_.b, ...), custom_call_target="tpu_custom_call" | custom-call | flops 3000000000 | bytes 9000000 | tf_op jit(solution)/shard_map/middle20/pallas_call | solution.py:334
  101.1 1.1 collective-permute-start.22
  102.2 2.6 %own.1.refs_6_ = f32[32,128,128]{2,1,0:T(8,128)S(1)} custom-call(s32[3]{0:T(128)S(1)} %pad_add_fusion.3.pos.refs_0_, s32[1536]{0:T(1024)S(1)} %reshape.107.tab.refs_1_, bf16[160,128,128]{2,1,0:T(8,128)(2,1)S(1)} %get-tuple-element.37.refs_2_.a, bf16[129,128,128]{2,1,0:T(8,128)(2,1)S(1)} %get-tuple-element.38.refs_3_.b, ...), custom_call_target="tpu_custom_call" | custom-call | flops 3000000000 | bytes 9000000 | tf_op jit(solution)/shard_map/own/pallas_call | solution.py:350
  104.9 2.5 %collective-permute-done.25.refs_5_ = s16[2064,128]{1,0:T(8,128)(2,1)S(1)} collective-permute-done((s16[2064,128]{1,0:T(8,128)(2,1)S(1)}, s16[2064,128]{1,0:T(8,128)(2,1)S(1)}, u32[]{:S(2)}, u32[]{:S(2)}) %collective-permute-start.25) | collective-permute-done | bytes 528416 | tf_op jit(solution)/shard_map/ppermute | solution.py:401
  107.4 1.8 %collective-permute-done.24.refs_4_ = s16[2064,128]{1,0:T(8,128)(2,1)S(1)} collective-permute-done((s16[2064,128]{1,0:T(8,128)(2,1)S(1)}, s16[2064,128]{1,0:T(8,128)(2,1)S(1)}, u32[]{:S(2)}, u32[]{:S(2)}) %collective-permute-start.24) | collective-permute-done | bytes 528416 | tf_op jit(solution)/shard_map/ppermute | solution.py:401
  109.2 2.8 %middle21.1 = (s16[2064,128]{1,0:T(8,128)(2,1)S(1)}, s16[2064,128]{1,0:T(8,128)(2,1)S(1)}) custom-call(s32[3]{0:T(128)S(1)} %pad_add_fusion.3.pos.refs_0_, s32[1536]{0:T(1024)S(1)} %reshape.107.tab.refs_1_, bf16[160,128,128]{2,1,0:T(8,128)(2,1)S(1)} %get-tuple-element.37.refs_2_.a, bf16[129,128,128]{2,1,0:T(8,128)(2,1)S(1)} %get-tuple-element.38.refs_3_.b, ...), custom_call_target="tpu_custom_call" | custom-call | flops 3000000000 | bytes 9000000 | tf_op jit(solution)/shard_map/middle21/pallas_call | solution.py:334
  112.7 1.1 collective-permute-start.28
  113.8 5.0 %collective-permute-done.23.in_l = s16[2064,128]{1,0:T(8,128)(2,1)S(1)} collective-permute-done((s16[2064,128]{1,0:T(8,128)(2,1)S(1)}, s16[2064,128]{1,0:T(8,128)(2,1)S(1)}, u32[]{:S(2)}, u32[]{:S(2)}) %collective-permute-start.23) | collective-permute-done | bytes 528416 | tf_op jit(solution)/shard_map/ppermute | solution.py:401
  118.7 1.8 %collective-permute-done.22.in_r = s16[2064,128]{1,0:T(8,128)(2,1)S(1)} collective-permute-done((s16[2064,128]{1,0:T(8,128)(2,1)S(1)}, s16[2064,128]{1,0:T(8,128)(2,1)S(1)}, u32[]{:S(2)}, u32[]{:S(2)}) %collective-permute-start.22) | collective-permute-done | bytes 528416 | tf_op jit(solution)/shard_map/ppermute | solution.py:401
  121.1 2.7 %collective-permute-start.27 = (s16[2,272,128]{2,1,0:T(8,128)(2,1)S(1)}, s16[2,272,128]{2,1,0:T(8,128)(2,1)S(1)}, u32[]{:S(2)}, u32[]{:S(2)}) collective-permute-start(s16[2,272,128]{2,1,0:T(8,128)(2,1)S(1)} %get-tuple-element.55), channel_id=1, source_target_pairs={{0,6},{1,7},{2,0},{3,1},{4,2},{5,3},{6,4},{7,5},{8,14},{9,15},{10,... | collective-permute-start | bytes 417800 | tf_op jit(solution)/shard_map/ppermute | solution.py:401
  123.7 6.3 %collective-permute-done.29.in_l = s16[2064,128]{1,0:T(8,128)(2,1)S(1)} collective-permute-done((s16[2064,128]{1,0:T(8,128)(2,1)S(1)}, s16[2064,128]{1,0:T(8,128)(2,1)S(1)}, u32[]{:S(2)}, u32[]{:S(2)}) %collective-permute-start.29) | collective-permute-done | bytes 528416 | tf_op jit(solution)/shard_map/ppermute | solution.py:401
  130.0 1.8 %collective-permute-done.28.in_r = s16[2064,128]{1,0:T(8,128)(2,1)S(1)} collective-permute-done((s16[2064,128]{1,0:T(8,128)(2,1)S(1)}, s16[2064,128]{1,0:T(8,128)(2,1)S(1)}, u32[]{:S(2)}, u32[]{:S(2)}) %collective-permute-start.28) | collective-permute-done | bytes 528416 | tf_op jit(solution)/shard_map/ppermute | solution.py:401
  132.4 2.7 %collective-permute-start.33 = (s16[2,272,128]{2,1,0:T(8,128)(2,1)S(1)}, s16[2,272,128]{2,1,0:T(8,128)(2,1)S(1)}, u32[]{:S(2)}, u32[]{:S(2)}) collective-permute-start(s16[2,272,128]{2,1,0:T(8,128)(2,1)S(1)} %get-tuple-element.63), channel_id=1, source_target_pairs={{0,6},{1,7},{2,0},{3,1},{4,2},{5,3},{6,4},{7,5},{8,14},{9,15},{10,... | collective-permute-start | bytes 417800 | tf_op jit(solution)/shard_map/ppermute | solution.py:401
  135.1 3.5 %collective-permute-start.31 = (s16[1072,128]{1,0:T(8,128)(2,1)S(1)}, s16[1072,128]{1,0:T(8,128)(2,1)S(1)}, u32[]{:S(2)}, u32[]{:S(2)}) collective-permute-start(s16[1072,128]{1,0:T(8,128)(2,1)S(1)} %pad_add_fusion), channel_id=1, source_target_pairs={{0,1},{1,0},{2,3},{3,2},{4,5},{5,4},{6,7},{7,6},{8,9},{9,8},{10,11... | collective-permute-start | bytes 823304 | tf_op jit(solution)/shard_map/ppermute | solution.py:416
  138.6 2.6 %collective-permute-start.34 = (s16[544,128]{1,0:T(8,128)(2,1)S(1)}, s16[544,128]{1,0:T(8,128)(2,1)S(1)}, u32[]{:S(2)}, u32[]{:S(2)}) collective-permute-start(s16[544,128]{1,0:T(8,128)(2,1)S(1)} %pad_add_fusion.1), channel_id=1, source_target_pairs={{0,1},{1,0},{2,3},{3,2},{4,5},{5,4},{6,7},{7,6},{8,9},{9,8},{10,11... | collective-permute-start | bytes 417800 | tf_op jit(solution)/shard_map/ppermute | solution.py:416
  141.3 1.6 %deliver0.1.early = f32[32,128,128]{2,1,0:T(8,128)} custom-call(s32[3]{0:T(128)S(1)} %pad_add_fusion.3.pos.refs_0_, s16[2,528,128]{2,1,0:T(8,128)(2,1)S(1)} %collective-permute-done.26.far, s16[2,272,128]{2,1,0:T(8,128)(2,1)S(1)} %collective-permute-done.30.unused.up, s16[2,272,128]{2,1,0:T(8,128)(2,1)S(1)} %collective-permute-done.27.down, ...), custom_call_target="tpu_custom_call" | custom-call | flops 1000000000 | bytes 3000000 | tf_op jit(solution)/shard_map/deliver0/pallas_call | solution.py:379
  143.0 1.5 %deliver1.1 = f32[32,128,128]{2,1,0:T(8,128)} custom-call(s32[3]{0:T(128)S(1)} %pad_add_fusion.3.pos.refs_0_, f32[32,128,128]{2,1,0:T(8,128)} %deliver0.1.early, s16[2,272,128]{2,1,0:T(8,128)(2,1)S(1)} %collective-permute-done.32.up, s16[2,272,128]{2,1,0:T(8,128)(2,1)S(1)} %collective-permute-done.33.down, ...), custom_call_target="tpu_custom_call", output_to_operand_aliasing={{}: (1, {})} | custom-call | flops 1000000000 | bytes 3000000 | tf_op jit(solution)/shard_map/deliver1/pallas_call | solution.py:379
  (69 shorter events, 13.4 us)
Async XLA Ops:
  0.0 5.9 %collective-permute-start.6 = (bf16[128,32,128]{2,1,0:T(8,128)(2,1)}, bf16[128,32,128]{2,1,0:T(8,128)(2,1)}, u32[]{:S(2)}, u32[]{:S(2)}) collective-permute-start(bf16[128,32,128]{2,1,0:T(8,128)(2,1)} %bitcast.21), channel_id=1, source_target_pairs={{0,1},{1,0},{2,3},{3,2},{4,5},{5,4},{6,7},{7,6},{8,9},{9,8},{10,11... | collective-permute-start | bytes 3145736 | tf_op jit(solution)/shard_map/ppermute | solution.py:416
  3.2 18.1 %collective-permute-start.5 = (bf16[128,32,128]{2,1,0:T(8,128)(2,1)}, bf16[128,32,128]{2,1,0:T(8,128)(2,1)S(1)}, u32[]{:S(2)}, u32[]{:S(2)}) collective-permute-start(bf16[128,32,128]{2,1,0:T(8,128)(2,1)} %bitcast.22), channel_id=1, source_target_pairs={{0,8},{1,25},{2,10},{3,27},{4,12},{5,29},{6,14},{7,31},{8,16},{9,1... | collective-permute-start | bytes 3145736 | tf_op jit(solution)/shard_map/ppermute | solution.py:411
  5.9 22.9 %collective-permute-start.7 = (bf16[128,32,128]{2,1,0:T(8,128)(2,1)}, bf16[128,32,128]{2,1,0:T(8,128)(2,1)}, u32[]{:S(2)}, u32[]{:S(2)}) collective-permute-start(bf16[128,32,128]{2,1,0:T(8,128)(2,1)} %collective-permute-done.6), channel_id=1, source_target_pairs={{0,8},{1,25},{2,10},{3,27},{4,12},{5,29},{6,14},{7,31},{8,16},{9,1... | collective-permute-start | bytes 3145736 | tf_op jit(solution)/shard_map/ppermute | solution.py:411
  6.9 10.3 %collective-permute-start.1 = (bf16[160,16,128]{2,1,0:T(8,128)(2,1)}, bf16[160,16,128]{2,1,0:T(8,128)(2,1)}, u32[]{:S(2)}, u32[]{:S(2)}) collective-permute-start(bf16[160,16,128]{2,1,0:T(8,128)(2,1)} %bitcast.24), channel_id=1, source_target_pairs={{0,2},{1,7},{2,4},{3,1},{4,6},{5,3},{6,0},{7,5},{8,10},{9,15},{10,... | collective-permute-start | bytes 1966088 | tf_op jit(solution)/shard_map/ppermute | solution.py:404
  9.3 11.3 %collective-permute-start = (bf16[160,16,128]{2,1,0:T(8,128)(2,1)}, bf16[160,16,128]{2,1,0:T(8,128)(2,1)}, u32[]{:S(2)}, u32[]{:S(2)}) collective-permute-start(bf16[160,16,128]{2,1,0:T(8,128)(2,1)} %bitcast.25), channel_id=1, source_target_pairs={{0,1},{1,0},{2,3},{3,2},{4,5},{5,4},{6,7},{7,6},{8,9},{9,8},{10,11... | collective-permute-start | bytes 1966088 | tf_op jit(solution)/shard_map/ppermute | solution.py:416
  17.2 15.8 %collective-permute-start.3 = (bf16[160,16,128]{2,1,0:T(8,128)(2,1)}, bf16[160,16,128]{2,1,0:T(8,128)(2,1)}, u32[]{:S(2)}, u32[]{:S(2)}) collective-permute-start(bf16[160,16,128]{2,1,0:T(8,128)(2,1)} %collective-permute-done.1.p1), channel_id=1, source_target_pairs={{0,2},{1,7},{2,4},{3,1},{4,6},{5,3},{6,0},{7,5},{8,10},{9,15},{10,... | collective-permute-start | bytes 1966088 | tf_op jit(solution)/shard_map/ppermute | solution.py:404
  20.6 14.9 %collective-permute-start.2 = (bf16[160,16,128]{2,1,0:T(8,128)(2,1)}, bf16[160,16,128]{2,1,0:T(8,128)(2,1)}, u32[]{:S(2)}, u32[]{:S(2)}) collective-permute-start(bf16[160,16,128]{2,1,0:T(8,128)(2,1)} %collective-permute-done.ap), channel_id=1, source_target_pairs={{0,2},{1,7},{2,4},{3,1},{4,6},{5,3},{6,0},{7,5},{8,10},{9,15},{10,... | collective-permute-start | bytes 1966088 | tf_op jit(solution)/shard_map/ppermute | solution.py:404
  21.4 20.0 %collective-permute-start.11 = (bf16[128,32,128]{2,1,0:T(8,128)(2,1)S(1)}, bf16[128,32,128]{2,1,0:T(8,128)(2,1)S(1)}, u32[]{:S(2)}, u32[]{:S(2)}) collective-permute-start(bf16[128,32,128]{2,1,0:T(8,128)(2,1)S(1)} %collective-permute-done.5.q1), channel_id=1, source_target_pairs={{0,8},{1,25},{2,10},{3,27},{4,12},{5,29},{6,14},{7,31},{8,16},{9,1... | collective-permute-start | bytes 3145736 | tf_op jit(solution)/shard_map/ppermute | solution.py:411
  28.7 9.5 %collective-permute-start.8 = (bf16[128,32,128]{2,1,0:T(8,128)(2,1)}, bf16[128,32,128]{2,1,0:T(8,128)(2,1)S(1)}, u32[]{:S(2)}, u32[]{:S(2)}) collective-permute-start(bf16[128,32,128]{2,1,0:T(8,128)(2,1)} %collective-permute-done.7), channel_id=1, source_target_pairs={{0,1},{1,0},{2,3},{3,2},{4,5},{5,4},{6,7},{7,6},{8,9},{9,8},{10,11... | collective-permute-start | bytes 3145736 | tf_op jit(solution)/shard_map/ppermute | solution.py:416
  32.9 5.4 %collective-permute-start.4 = (bf16[160,16,128]{2,1,0:T(8,128)(2,1)}, bf16[160,16,128]{2,1,0:T(8,128)(2,1)}, u32[]{:S(2)}, u32[]{:S(2)}) collective-permute-start(bf16[160,16,128]{2,1,0:T(8,128)(2,1)} %collective-permute-done.1.p1), channel_id=1, source_target_pairs={{0,1},{1,0},{2,3},{3,2},{4,5},{5,4},{6,7},{7,6},{8,9},{9,8},{10,11... | collective-permute-start | bytes 1966088 | tf_op jit(solution)/shard_map/ppermute | solution.py:416
  33.0 8.4 %collective-permute-start.10 = (bf16[160,16,128]{2,1,0:T(8,128)(2,1)}, bf16[160,16,128]{2,1,0:T(8,128)(2,1)}, u32[]{:S(2)}, u32[]{:S(2)}) collective-permute-start(bf16[160,16,128]{2,1,0:T(8,128)(2,1)} %collective-permute-done.3.p3), channel_id=1, source_target_pairs={{0,1},{1,0},{2,3},{3,2},{4,5},{5,4},{6,7},{7,6},{8,9},{9,8},{10,11... | collective-permute-start | bytes 1966088 | tf_op jit(solution)/shard_map/ppermute | solution.py:416
  35.5 5.9 %collective-permute-start.9 = (bf16[160,16,128]{2,1,0:T(8,128)(2,1)}, bf16[160,16,128]{2,1,0:T(8,128)(2,1)}, u32[]{:S(2)}, u32[]{:S(2)}) collective-permute-start(bf16[160,16,128]{2,1,0:T(8,128)(2,1)} %collective-permute-done.2.p2), channel_id=1, source_target_pairs={{0,1},{1,0},{2,3},{3,2},{4,5},{5,4},{6,7},{7,6},{8,9},{9,8},{10,11... | collective-permute-start | bytes 1966088 | tf_op jit(solution)/shard_map/ppermute | solution.py:416
  44.4 11.3 %collective-permute-start.13 = (s16[1040,128]{1,0:T(8,128)(2,1)S(1)}, s16[1040,128]{1,0:T(8,128)(2,1)S(1)}, u32[]{:S(2)}, u32[]{:S(2)}) collective-permute-start(s16[1040,128]{1,0:T(8,128)(2,1)S(1)} %get-tuple-element.40), channel_id=1, source_target_pairs={{0,224},{32,0},{64,32},{96,64},{128,96},{160,128},{192,160},{224,1... | collective-permute-start | bytes 798728 | tf_op jit(solution)/shard_map/ppermute | solution.py:401
  49.9 8.9 %collective-permute-start.12 = (s16[1040,128]{1,0:T(8,128)(2,1)S(1)}, s16[1040,128]{1,0:T(8,128)(2,1)S(1)}, u32[]{:S(2)}, u32[]{:S(2)}) collective-permute-start(s16[1040,128]{1,0:T(8,128)(2,1)S(1)} %get-tuple-element.39.refs_4_), channel_id=1, source_target_pairs={{0,32},{32,64},{64,96},{96,128},{128,160},{160,192},{192,224},{224... | collective-permute-start | bytes 798728 | tf_op jit(solution)/shard_map/ppermute | solution.py:401
  51.6 11.6 %collective-permute-start.17 = (s16[1040,128]{1,0:T(8,128)(2,1)S(1)}, s16[1040,128]{1,0:T(8,128)(2,1)S(1)}, u32[]{:S(2)}, u32[]{:S(2)}) collective-permute-start(s16[1040,128]{1,0:T(8,128)(2,1)S(1)} %get-tuple-element.44), channel_id=1, source_target_pairs={{0,224},{32,0},{64,32},{96,64},{128,96},{160,128},{192,160},{224,1... | collective-permute-start | bytes 798728 | tf_op jit(solution)/shard_map/ppermute | solution.py:401
  54.6 10.0 %collective-permute-start.16 = (s16[1040,128]{1,0:T(8,128)(2,1)S(1)}, s16[1040,128]{1,0:T(8,128)(2,1)S(1)}, u32[]{:S(2)}, u32[]{:S(2)}) collective-permute-start(s16[1040,128]{1,0:T(8,128)(2,1)S(1)} %get-tuple-element.41.refs_6_), channel_id=1, source_target_pairs={{0,32},{32,64},{64,96},{96,128},{128,160},{160,192},{192,224},{224... | collective-permute-start | bytes 798728 | tf_op jit(solution)/shard_map/ppermute | solution.py:401
  61.7 11.8 %collective-permute-start.15 = (s16[2064,128]{1,0:T(8,128)(2,1)S(1)}, s16[2064,128]{1,0:T(8,128)(2,1)S(1)}, u32[]{:S(2)}, u32[]{:S(2)}) collective-permute-start(s16[2064,128]{1,0:T(8,128)(2,1)S(1)} %get-tuple-element.43), channel_id=1, source_target_pairs={{0,224},{32,0},{64,32},{96,64},{128,96},{160,128},{192,160},{224,1... | collective-permute-start | bytes 1585160 | tf_op jit(solution)/shard_map/ppermute | solution.py:401
  62.1 13.1 %collective-permute-start.14 = (s16[2064,128]{1,0:T(8,128)(2,1)S(1)}, s16[2064,128]{1,0:T(8,128)(2,1)S(1)}, u32[]{:S(2)}, u32[]{:S(2)}) collective-permute-start(s16[2064,128]{1,0:T(8,128)(2,1)S(1)} %get-tuple-element.42.refs_6_), channel_id=1, source_target_pairs={{0,32},{32,64},{64,96},{96,128},{128,160},{160,192},{192,224},{224... | collective-permute-start | bytes 1585160 | tf_op jit(solution)/shard_map/ppermute | solution.py:401
  67.4 17.4 %collective-permute-start.21 = (s16[2064,128]{1,0:T(8,128)(2,1)S(1)}, s16[2064,128]{1,0:T(8,128)(2,1)S(1)}, u32[]{:S(2)}, u32[]{:S(2)}) collective-permute-start(s16[2064,128]{1,0:T(8,128)(2,1)S(1)} %get-tuple-element.48), channel_id=1, source_target_pairs={{0,224},{32,0},{64,32},{96,64},{128,96},{160,128},{192,160},{224,1... | collective-permute-start | bytes 1585160 | tf_op jit(solution)/shard_map/ppermute | solution.py:401
  67.8 18.8 %collective-permute-start.20 = (s16[2064,128]{1,0:T(8,128)(2,1)S(1)}, s16[2064,128]{1,0:T(8,128)(2,1)S(1)}, u32[]{:S(2)}, u32[]{:S(2)}) collective-permute-start(s16[2064,128]{1,0:T(8,128)(2,1)S(1)} %get-tuple-element.45.refs_6_), channel_id=1, source_target_pairs={{0,32},{32,64},{64,96},{96,128},{128,160},{160,192},{192,224},{224... | collective-permute-start | bytes 1585160 | tf_op jit(solution)/shard_map/ppermute | solution.py:401
  78.0 18.0 %collective-permute-start.19 = (s16[2064,128]{1,0:T(8,128)(2,1)S(1)}, s16[2064,128]{1,0:T(8,128)(2,1)S(1)}, u32[]{:S(2)}, u32[]{:S(2)}) collective-permute-start(s16[2064,128]{1,0:T(8,128)(2,1)S(1)} %get-tuple-element.47), channel_id=1, source_target_pairs={{0,224},{32,0},{64,32},{96,64},{128,96},{160,128},{192,160},{224,1... | collective-permute-start | bytes 1585160 | tf_op jit(solution)/shard_map/ppermute | solution.py:401
  78.5 19.4 %collective-permute-start.18 = (s16[2064,128]{1,0:T(8,128)(2,1)S(1)}, s16[2064,128]{1,0:T(8,128)(2,1)S(1)}, u32[]{:S(2)}, u32[]{:S(2)}) collective-permute-start(s16[2064,128]{1,0:T(8,128)(2,1)S(1)} %get-tuple-element.46.refs_6_), channel_id=1, source_target_pairs={{0,32},{32,64},{64,96},{96,128},{128,160},{160,192},{192,224},{224... | collective-permute-start | bytes 1585160 | tf_op jit(solution)/shard_map/ppermute | solution.py:401
  89.3 18.1 %collective-permute-start.25 = (s16[2064,128]{1,0:T(8,128)(2,1)S(1)}, s16[2064,128]{1,0:T(8,128)(2,1)S(1)}, u32[]{:S(2)}, u32[]{:S(2)}) collective-permute-start(s16[2064,128]{1,0:T(8,128)(2,1)S(1)} %get-tuple-element.52), channel_id=1, source_target_pairs={{0,224},{32,0},{64,32},{96,64},{128,96},{160,128},{192,160},{224,1... | collective-permute-start | bytes 1585160 | tf_op jit(solution)/shard_map/ppermute | solution.py:401
  89.8 19.4 %collective-permute-start.24 = (s16[2064,128]{1,0:T(8,128)(2,1)S(1)}, s16[2064,128]{1,0:T(8,128)(2,1)S(1)}, u32[]{:S(2)}, u32[]{:S(2)}) collective-permute-start(s16[2064,128]{1,0:T(8,128)(2,1)S(1)} %get-tuple-element.49.refs_6_), channel_id=1, source_target_pairs={{0,32},{32,64},{64,96},{96,128},{128,160},{160,192},{192,224},{224... | collective-permute-start | bytes 1585160 | tf_op jit(solution)/shard_map/ppermute | solution.py:401
  100.7 18.0 %collective-permute-start.23 = (s16[2064,128]{1,0:T(8,128)(2,1)S(1)}, s16[2064,128]{1,0:T(8,128)(2,1)S(1)}, u32[]{:S(2)}, u32[]{:S(2)}) collective-permute-start(s16[2064,128]{1,0:T(8,128)(2,1)S(1)} %get-tuple-element.51), channel_id=1, source_target_pairs={{0,224},{32,0},{64,32},{96,64},{128,96},{160,128},{192,160},{224,1... | collective-permute-start | bytes 1585160 | tf_op jit(solution)/shard_map/ppermute | solution.py:401
  101.1 19.4 %collective-permute-start.22 = (s16[2064,128]{1,0:T(8,128)(2,1)S(1)}, s16[2064,128]{1,0:T(8,128)(2,1)S(1)}, u32[]{:S(2)}, u32[]{:S(2)}) collective-permute-start(s16[2064,128]{1,0:T(8,128)(2,1)S(1)} %get-tuple-element.50.unused), channel_id=1, source_target_pairs={{0,32},{32,64},{64,96},{96,128},{128,160},{160,192},{192,224},{224... | collective-permute-start | bytes 1585160 | tf_op jit(solution)/shard_map/ppermute | solution.py:401
  112.0 18.1 %collective-permute-start.29 = (s16[2064,128]{1,0:T(8,128)(2,1)S(1)}, s16[2064,128]{1,0:T(8,128)(2,1)S(1)}, u32[]{:S(2)}, u32[]{:S(2)}) collective-permute-start(s16[2064,128]{1,0:T(8,128)(2,1)S(1)} %get-tuple-element.56), channel_id=1, source_target_pairs={{0,224},{32,0},{64,32},{96,64},{128,96},{160,128},{192,160},{224,1... | collective-permute-start | bytes 1585160 | tf_op jit(solution)/shard_map/ppermute | solution.py:401
  112.7 19.1 %collective-permute-start.28 = (s16[2064,128]{1,0:T(8,128)(2,1)S(1)}, s16[2064,128]{1,0:T(8,128)(2,1)S(1)}, u32[]{:S(2)}, u32[]{:S(2)}) collective-permute-start(s16[2064,128]{1,0:T(8,128)(2,1)S(1)} %get-tuple-element.53.unused), channel_id=1, source_target_pairs={{0,32},{32,64},{64,96},{96,128},{128,160},{160,192},{192,224},{224... | collective-permute-start | bytes 1585160 | tf_op jit(solution)/shard_map/ppermute | solution.py:401
  121.0 10.8 %collective-permute-start.30 = (s16[2,272,128]{2,1,0:T(8,128)(2,1)S(1)}, s16[2,272,128]{2,1,0:T(8,128)(2,1)S(1)}, u32[]{:S(2)}, u32[]{:S(2)}) collective-permute-start(s16[2,272,128]{2,1,0:T(8,128)(2,1)S(1)} %get-tuple-element.57), channel_id=1, source_target_pairs={{0,2},{1,3},{2,4},{3,5},{4,6},{5,7},{6,0},{7,1},{8,10},{9,11},{10,... | collective-permute-start | bytes 417800 | tf_op jit(solution)/shard_map/ppermute | solution.py:401
  121.1 14.0 %collective-permute-start.27 = (s16[2,272,128]{2,1,0:T(8,128)(2,1)S(1)}, s16[2,272,128]{2,1,0:T(8,128)(2,1)S(1)}, u32[]{:S(2)}, u32[]{:S(2)}) collective-permute-start(s16[2,272,128]{2,1,0:T(8,128)(2,1)S(1)} %get-tuple-element.55), channel_id=1, source_target_pairs={{0,6},{1,7},{2,0},{3,1},{4,2},{5,3},{6,4},{7,5},{8,14},{9,15},{10,... | collective-permute-start | bytes 417800 | tf_op jit(solution)/shard_map/ppermute | solution.py:401
  123.7 11.3 %collective-permute-start.26 = (s16[2,528,128]{2,1,0:T(8,128)(2,1)S(1)}, s16[2,528,128]{2,1,0:T(8,128)(2,1)S(1)}, u32[]{:S(2)}, u32[]{:S(2)}) collective-permute-start(s16[2,528,128]{2,1,0:T(8,128)(2,1)S(1)} %get-tuple-element.54), channel_id=1, source_target_pairs={{0,4},{1,5},{2,6},{3,7},{4,0},{5,1},{6,2},{7,3},{8,12},{9,13},{10,... | collective-permute-start | bytes 811016 | tf_op jit(solution)/shard_map/ppermute | solution.py:401
  132.3 6.3 %collective-permute-start.32 = (s16[2,272,128]{2,1,0:T(8,128)(2,1)S(1)}, s16[2,272,128]{2,1,0:T(8,128)(2,1)S(1)}, u32[]{:S(2)}, u32[]{:S(2)}) collective-permute-start(s16[2,272,128]{2,1,0:T(8,128)(2,1)S(1)} %get-tuple-element.62), channel_id=1, source_target_pairs={{0,2},{1,3},{2,4},{3,5},{4,6},{5,7},{6,0},{7,1},{8,10},{9,11},{10,... | collective-permute-start | bytes 417800 | tf_op jit(solution)/shard_map/ppermute | solution.py:401
  132.4 6.2 %collective-permute-start.33 = (s16[2,272,128]{2,1,0:T(8,128)(2,1)S(1)}, s16[2,272,128]{2,1,0:T(8,128)(2,1)S(1)}, u32[]{:S(2)}, u32[]{:S(2)}) collective-permute-start(s16[2,272,128]{2,1,0:T(8,128)(2,1)S(1)} %get-tuple-element.63), channel_id=1, source_target_pairs={{0,6},{1,7},{2,0},{3,1},{4,2},{5,3},{6,4},{7,5},{8,14},{9,15},{10,... | collective-permute-start | bytes 417800 | tf_op jit(solution)/shard_map/ppermute | solution.py:401
  135.1 6.2 %collective-permute-start.31 = (s16[1072,128]{1,0:T(8,128)(2,1)S(1)}, s16[1072,128]{1,0:T(8,128)(2,1)S(1)}, u32[]{:S(2)}, u32[]{:S(2)}) collective-permute-start(s16[1072,128]{1,0:T(8,128)(2,1)S(1)} %pad_add_fusion), channel_id=1, source_target_pairs={{0,1},{1,0},{2,3},{3,2},{4,5},{5,4},{6,7},{7,6},{8,9},{9,8},{10,11... | collective-permute-start | bytes 823304 | tf_op jit(solution)/shard_map/ppermute | solution.py:416
  138.6 4.4 %collective-permute-start.34 = (s16[544,128]{1,0:T(8,128)(2,1)S(1)}, s16[544,128]{1,0:T(8,128)(2,1)S(1)}, u32[]{:S(2)}, u32[]{:S(2)}) collective-permute-start(s16[544,128]{1,0:T(8,128)(2,1)S(1)} %pad_add_fusion.1), channel_id=1, source_target_pairs={{0,1},{1,0},{2,3},{3,2},{4,5},{5,4},{6,7},{7,6},{8,9},{9,8},{10,11... | collective-permute-start | bytes 417800 | tf_op jit(solution)/shard_map/ppermute | solution.py:416
  141.2 1.8 %collective-permute-start.35 = (s16[528,128]{1,0:T(8,128)(2,1)S(1)}, s16[528,128]{1,0:T(8,128)(2,1)S(1)}, u32[]{:S(2)}, u32[]{:S(2)}) collective-permute-start(s16[528,128]{1,0:T(8,128)(2,1)S(1)} %get-tuple-element.64), channel_id=1, source_target_pairs={{0,1},{1,0},{2,3},{3,2},{4,5},{5,4},{6,7},{7,6},{8,9},{9,8},{10,11... | collective-permute-start | bytes 405512 | tf_op jit(solution)/shard_map/ppermute | solution.py:416

commit v5 on v4

--- a/solution.py
+++ b/solution.py
@@ -159,8 +159,8 @@
 
 
 def second_kernel(h, pos, tab, a, b, in_r, in_l, out_r, out_l, code_r, code_l, scale_r, scale_l):
-    base_r = (pos[0] + 3) % 8 * 32 + h * SUB
-    base_l = (pos[0] + 5) % 8 * 32 + h * SUB
+    base_r = (pos[0] + 5) % 8 * 32 + h * SUB
+    base_l = (pos[0] + 3) % 8 * 32 + h * SUB
     read_codes(in_r, HALF_ROWS, scale_r)
     read_codes(in_l, HALF_ROWS, scale_l)
 
@@ -184,8 +184,8 @@
 
 
 def middle_kernel(h, away, pos, tab, a, b, in_r, in_l, out_r, out_l, code_r, code_l, scale_r, scale_l):
-    base_r = (pos[0] + away) % 8 * 32 + h * SUB
-    base_l = (pos[0] + 8 - away) % 8 * 32 + h * SUB
+    base_r = (pos[0] + 8 - away) % 8 * 32 + h * SUB
+    base_l = (pos[0] + away) % 8 * 32 + h * SUB
     read_codes(in_r, ROWS, scale_r)
     read_codes(in_l, ROWS, scale_l)
 
@@ -410,7 +410,7 @@
                 pairs.append((r * col + c, (r + 1 - 2 * (c % 2)) % row * col + c))
         return lax.ppermute(x, ("row", "col"), pairs)
 
-    z_up, z_down = shift("depth", depth, 1), shift("depth", depth, -1)
+    z_up, z_down = shift("depth", depth, -1), shift("depth", depth, 1)
 
     def swap(x):
         return lax.ppermute(x, "col", [(i, i ^ 1) for i in range(col)])

time: 145 us -> 145 us (level); the launches traced: 145 us -> 142 us
  waiting for transfers between devices: 60.5 us -> 51.6 us
  starting transfers between devices: 45.7 us -> 52.1 us
    ppermute x21, waiting for transfers between devices: 44.9 us -> 35.9 us  [shift(): return lambda x: lax.ppermute(x, axis, pairs)]
    ppermute x21, starting transfers between devices: 23.4 us -> 30.7 us  [shift(): return lambda x: lax.ppermute(x, axis, pairs)]
  transfers between devices with their start and end apart: 36 -> 36, of which waited for: 19 -> 13; matrix products, arithmetic and copies ran while one was open for 4% -> 5% of each run, Pallas kernels for 19% -> 19%
where the time goes in v5:
time: 145 us; the launch traced here: 142 us
  starting transfers between devices  52.1 us (36%)
  waiting for transfers between devices  51.6 us (36%)
  Pallas kernels  31.5 us (22%)
  other arithmetic  4.21 us (3%)
  local copies, waits for them, and re-layouts  2.29 us (2%)
    ppermute x21, waiting for transfers between devices, shift(): return lambda x: lax.ppermute(x, axis, pairs)  35.9 us
    ppermute x21, starting transfers between devices, shift(): return lambda x: lax.ppermute(x, axis, pairs)  30.7 us
    pallas_call x7, Pallas kernels, step(): pl.pallas_call(body, out_shape=out_shape, in_specs=ins, out_specs=jax.tre...  18.7 us
    ppermute x9, starting transfers between devices, swap(): return lax.ppermute(x, 'col', [(i, i ^ 1) for i in range(col)])  13.2 us
    ppermute x3, waiting for transfers between devices, y_split(): return lax.ppermute(x, ('row', 'col'), pairs)  7.15 us
    ppermute x3, waiting for transfers between devices, x_split(): lax.ppermute(x, 'col', [(i, (i + 2 - 4 * (i % 2)) % col) for i in range(c...  6.86 us
    ppermute x3, starting transfers between devices, x_split(): lax.ppermute(x, 'col', [(i, (i + 2 - 4 * (i % 2)) % col) for i in range(c...  5.92 us
    pallas_call x2, Pallas kernels, deliver(): pl.pallas_call(kernel, out_shape=jax.ShapeDtypeStruct((tiles, TILE, TILE)...  3.16 us
  transfers between devices with their start and end apart: 36, of which 13 were waited for; matrix products, arithmetic and copies ran while one was open for 5% of the time, Pallas kernels for 19%

profile of v5, /device:TPU:1, one launch (start us, length us, event | category | flops | bytes accessed | tf_op | source)
XLA Modules:
  0.0 142.3 jit_solution(16901935922418851980)
XLA Ops:
  0.0 3.2 %collective-permute-start.6 = (bf16[128,32,128]{2,1,0:T(8,128)(2,1)}, bf16[128,32,128]{2,1,0:T(8,128)(2,1)}, u32[]{:S(2)}, u32[]{:S(2)}) collective-permute-start(bf16[128,32,128]{2,1,0:T(8,128)(2,1)} %bitcast.21), channel_id=1, source_target_pairs={{0,1},{1,0},{2,3},{3,2},{4,5},{5,4},{6,7},{7,6},{8,9},{9,8},{10,11... | collective-permute-start | bytes 3145736 | tf_op jit(solution)/shard_map/ppermute | solution.py:416
  3.2 1.0 collective-permute-start.5
  4.2 1.6 %collective-permute-done.6 = bf16[128,32,128]{2,1,0:T(8,128)(2,1)} collective-permute-done((bf16[128,32,128]{2,1,0:T(8,128)(2,1)}, bf16[128,32,128]{2,1,0:T(8,128)(2,1)}, u32[]{:S(2)}, u32[]{:S(2)}) %collective-permute-start.6) | collective-permute-done | bytes 1048608 | tf_op jit(solution)/shard_map/ppermute | solution.py:416
  5.9 1.0 collective-permute-start.7
  6.9 2.5 %collective-permute-start.1 = (bf16[160,16,128]{2,1,0:T(8,128)(2,1)}, bf16[160,16,128]{2,1,0:T(8,128)(2,1)}, u32[]{:S(2)}, u32[]{:S(2)}) collective-permute-start(bf16[160,16,128]{2,1,0:T(8,128)(2,1)} %bitcast.24), channel_id=1, source_target_pairs={{0,2},{1,7},{2,4},{3,1},{4,6},{5,3},{6,0},{7,5},{8,10},{9,15},{10,... | collective-permute-start | bytes 1966088 | tf_op jit(solution)/shard_map/ppermute | solution.py:404
  9.4 0.8 copy.37
  10.9 0.7 fusion
  12.4 4.8 %collective-permute-done.1.p1 = bf16[160,16,128]{2,1,0:T(8,128)(2,1)} collective-permute-done((bf16[160,16,128]{2,1,0:T(8,128)(2,1)}, bf16[160,16,128]{2,1,0:T(8,128)(2,1)}, u32[]{:S(2)}, u32[]{:S(2)}) %collective-permute-start.1) | collective-permute-done | bytes 655392 | tf_op jit(solution)/shard_map/ppermute | solution.py:404
  17.2 3.4 %collective-permute-start.3 = (bf16[160,16,128]{2,1,0:T(8,128)(2,1)}, bf16[160,16,128]{2,1,0:T(8,128)(2,1)}, u32[]{:S(2)}, u32[]{:S(2)}) collective-permute-start(bf16[160,16,128]{2,1,0:T(8,128)(2,1)} %collective-permute-done.1.p1), channel_id=1, source_target_pairs={{0,2},{1,7},{2,4},{3,1},{4,6},{5,3},{6,0},{7,5},{8,10},{9,15},{10,... | collective-permute-start | bytes 1966088 | tf_op jit(solution)/shard_map/ppermute | solution.py:404
  21.6 7.1 %collective-permute-done.7 = bf16[128,32,128]{2,1,0:T(8,128)(2,1)} collective-permute-done((bf16[128,32,128]{2,1,0:T(8,128)(2,1)}, bf16[128,32,128]{2,1,0:T(8,128)(2,1)}, u32[]{:S(2)}, u32[]{:S(2)}) %collective-permute-start.7) | collective-permute-done | bytes 1048608 | tf_op jit(solution)/shard_map/ppermute | solution.py:411
  28.7 2.1 %collective-permute-start.8 = (bf16[128,32,128]{2,1,0:T(8,128)(2,1)}, bf16[128,32,128]{2,1,0:T(8,128)(2,1)S(1)}, u32[]{:S(2)}, u32[]{:S(2)}) collective-permute-start(bf16[128,32,128]{2,1,0:T(8,128)(2,1)} %collective-permute-done.7), channel_id=1, source_target_pairs={{0,1},{1,0},{2,3},{3,2},{4,5},{5,4},{6,7},{7,6},{8,9},{9,8},{10,11... | collective-permute-start | bytes 3145736 | tf_op jit(solution)/shard_map/ppermute | solution.py:416
  30.8 0.8 compare_reduce_fusion
  31.7 0.8 copy.36
  33.5 2.0 %collective-permute-done.2.p2 = bf16[160,16,128]{2,1,0:T(8,128)(2,1)} collective-permute-done((bf16[160,16,128]{2,1,0:T(8,128)(2,1)}, bf16[160,16,128]{2,1,0:T(8,128)(2,1)}, u32[]{:S(2)}, u32[]{:S(2)}) %collective-permute-start.2) | collective-permute-done | bytes 655392 | tf_op jit(solution)/shard_map/ppermute | solution.py:404
  35.5 2.0 %collective-permute-start.9 = (bf16[160,16,128]{2,1,0:T(8,128)(2,1)}, bf16[160,16,128]{2,1,0:T(8,128)(2,1)}, u32[]{:S(2)}, u32[]{:S(2)}) collective-permute-start(bf16[160,16,128]{2,1,0:T(8,128)(2,1)} %collective-permute-done.2.p2), channel_id=1, source_target_pairs={{0,1},{1,0},{2,3},{3,2},{4,5},{5,4},{6,7},{7,6},{8,9},{9,8},{10,11... | collective-permute-start | bytes 1966088 | tf_op jit(solution)/shard_map/ppermute | solution.py:416
  38.3 3.1 %assemble.1 = (bf16[160,128,128]{2,1,0:T(8,128)(2,1)S(1)}, bf16[129,128,128]{2,1,0:T(8,128)(2,1)S(1)}) custom-call(s32[3]{0:T(128)S(1)} %pad_add_fusion.3.pos.refs_0_, bf16[160,16,128]{2,1,0:T(8,128)(2,1)} %bitcast.26, bf16[160,16,128]{2,1,0:T(8,128)(2,1)} %collective-permute-done.ap, bf16[160,16,128]{2,1,0:T(8,128)(2,1)} %collective-permute-done.1.p1, ...), custom_call_target="tpu_custom_call" | custom-call | tf_op jit(solution)/shard_map/assemble/pallas_call | solution.py:428
  41.4 3.0 %first0.1 = (s16[1040,128]{1,0:T(8,128)(2,1)S(1)}, s16[1040,128]{1,0:T(8,128)(2,1)S(1)}, bf16[160,128,128]{2,1,0:T(8,128)(2,1)S(1)}, bf16[129,128,128]{2,1,0:T(8,128)(2,1)S(1)}) custom-call(s32[3]{0:T(128)S(1)} %pad_add_fusion.3.pos.refs_0_, s32[1536]{0:T(1024)S(1)} %reshape.107.tab.refs_1_, ...), custom_call_target="tpu_custom_call", output_to_operand_aliasing={{2}: (2, {}), {3}: (3, {})} | custom-call | flops 2000000000 | bytes 6000000 | tf_op jit(solution)/shard_map/first0/pallas_call | solution.py:444
  44.4 1.6 %collective-permute-start.13 = (s16[1040,128]{1,0:T(8,128)(2,1)S(1)}, s16[1040,128]{1,0:T(8,128)(2,1)S(1)}, u32[]{:S(2)}, u32[]{:S(2)}) collective-permute-start(s16[1040,128]{1,0:T(8,128)(2,1)S(1)} %get-tuple-element.40), channel_id=1, source_target_pairs={{0,32},{32,64},{64,96},{96,128},{128,160},{160,192},{192,224},{224... | collective-permute-start | bytes 798728 | tf_op jit(solution)/shard_map/ppermute | solution.py:401
  46.0 4.0 %collective-permute-start.12 = (s16[1040,128]{1,0:T(8,128)(2,1)S(1)}, s16[1040,128]{1,0:T(8,128)(2,1)S(1)}, u32[]{:S(2)}, u32[]{:S(2)}) collective-permute-start(s16[1040,128]{1,0:T(8,128)(2,1)S(1)} %get-tuple-element.39.refs_4_), channel_id=1, source_target_pairs={{0,224},{32,0},{64,32},{96,64},{128,96},{160,128},{192,160},{224,1... | collective-permute-start | bytes 798728 | tf_op jit(solution)/shard_map/ppermute | solution.py:401
  50.0 1.7 %first1.1 = (s16[1040,128]{1,0:T(8,128)(2,1)S(1)}, s16[1040,128]{1,0:T(8,128)(2,1)S(1)}) custom-call(s32[3]{0:T(128)S(1)} %pad_add_fusion.3.pos.refs_0_, s32[1536]{0:T(1024)S(1)} %reshape.107.tab.refs_1_, bf16[160,128,128]{2,1,0:T(8,128)(2,1)S(1)} %get-tuple-element.37.refs_2_.a, bf16[129,128,128]{2,1,0:T(8,128)(2,1)S(1)} %get-tuple-element.38.refs_3_.b, ...), custom_call_target="tpu_custom_call" | custom-call | flops 2000000000 | bytes 6000000 | tf_op jit(solution)/shard_map/first1/pallas_call | solution.py:334
  52.0 2.7 %collective-permute-start.16 = (s16[1040,128]{1,0:T(8,128)(2,1)S(1)}, s16[1040,128]{1,0:T(8,128)(2,1)S(1)}, u32[]{:S(2)}, u32[]{:S(2)}) collective-permute-start(s16[1040,128]{1,0:T(8,128)(2,1)S(1)} %get-tuple-element.41.refs_6_), channel_id=1, source_target_pairs={{0,224},{32,0},{64,32},{96,64},{128,96},{160,128},{192,160},{224,1... | collective-permute-start | bytes 798728 | tf_op jit(solution)/shard_map/ppermute | solution.py:401
  54.7 2.0 %collective-permute-done.13.refs_5_ = s16[1040,128]{1,0:T(8,128)(2,1)S(1)} collective-permute-done((s16[1040,128]{1,0:T(8,128)(2,1)S(1)}, s16[1040,128]{1,0:T(8,128)(2,1)S(1)}, u32[]{:S(2)}, u32[]{:S(2)}) %collective-permute-start.13) | collective-permute-done | bytes 266272 | tf_op jit(solution)/shard_map/ppermute | solution.py:401
  56.7 2.8 %second0.1 = (s16[2064,128]{1,0:T(8,128)(2,1)S(1)}, s16[2064,128]{1,0:T(8,128)(2,1)S(1)}) custom-call(s32[3]{0:T(128)S(1)} %pad_add_fusion.3.pos.refs_0_, s32[1536]{0:T(1024)S(1)} %reshape.107.tab.refs_1_, bf16[160,128,128]{2,1,0:T(8,128)(2,1)S(1)} %get-tuple-element.37.refs_2_.a, bf16[129,128,128]{2,1,0:T(8,128)(2,1)S(1)} %get-tuple-element.38.refs_3_.b, ...), custom_call_target="tpu_custom_call" | custom-call | flops 3000000000 | bytes 9000000 | tf_op jit(solution)/shard_map/second0/pallas_call | solution.py:334
  59.6 2.7 %collective-permute-start.14 = (s16[2064,128]{1,0:T(8,128)(2,1)S(1)}, s16[2064,128]{1,0:T(8,128)(2,1)S(1)}, u32[]{:S(2)}, u32[]{:S(2)}) collective-permute-start(s16[2064,128]{1,0:T(8,128)(2,1)S(1)} %get-tuple-element.42.refs_6_), channel_id=1, source_target_pairs={{0,224},{32,0},{64,32},{96,64},{128,96},{160,128},{192,160},{224,1... | collective-permute-start | bytes 1585160 | tf_op jit(solution)/shard_map/ppermute | solution.py:401
  62.4 2.8 %second1.1 = (s16[2064,128]{1,0:T(8,128)(2,1)S(1)}, s16[2064,128]{1,0:T(8,128)(2,1)S(1)}) custom-call(s32[3]{0:T(128)S(1)} %pad_add_fusion.3.pos.refs_0_, s32[1536]{0:T(1024)S(1)} %reshape.107.tab.refs_1_, bf16[160,128,128]{2,1,0:T(8,128)(2,1)S(1)} %get-tuple-element.37.refs_2_.a, bf16[129,128,128]{2,1,0:T(8,128)(2,1)S(1)} %get-tuple-element.38.refs_3_.b, ...), custom_call_target="tpu_custom_call" | custom-call | flops 3000000000 | bytes 9000000 | tf_op jit(solution)/shard_map/second1/pallas_call | solution.py:334
  65.3 2.7 %collective-permute-start.20 = (s16[2064,128]{1,0:T(8,128)(2,1)S(1)}, s16[2064,128]{1,0:T(8,128)(2,1)S(1)}, u32[]{:S(2)}, u32[]{:S(2)}) collective-permute-start(s16[2064,128]{1,0:T(8,128)(2,1)S(1)} %get-tuple-element.45.refs_6_), channel_id=1, source_target_pairs={{0,224},{32,0},{64,32},{96,64},{128,96},{160,128},{192,160},{224,1... | collective-permute-start | bytes 1585160 | tf_op jit(solution)/shard_map/ppermute | solution.py:401
  68.0 5.6 %collective-permute-done.15.refs_5_ = s16[2064,128]{1,0:T(8,128)(2,1)S(1)} collective-permute-done((s16[2064,128]{1,0:T(8,128)(2,1)S(1)}, s16[2064,128]{1,0:T(8,128)(2,1)S(1)}, u32[]{:S(2)}, u32[]{:S(2)}) %collective-permute-start.15) | collective-permute-done | bytes 528416 | tf_op jit(solution)/shard_map/ppermute | solution.py:401
  73.6 2.8 %middle10.1 = (s16[2064,128]{1,0:T(8,128)(2,1)S(1)}, s16[2064,128]{1,0:T(8,128)(2,1)S(1)}) custom-call(s32[3]{0:T(128)S(1)} %pad_add_fusion.3.pos.refs_0_, s32[1536]{0:T(1024)S(1)} %reshape.107.tab.refs_1_, bf16[160,128,128]{2,1,0:T(8,128)(2,1)S(1)} %get-tuple-element.37.refs_2_.a, bf16[129,128,128]{2,1,0:T(8,128)(2,1)S(1)} %get-tuple-element.38.refs_3_.b, ...), custom_call_target="tpu_custom_call" | custom-call | flops 3000000000 | bytes 9000000 | tf_op jit(solution)/shard_map/middle10/pallas_call | solution.py:334
  77.1 2.1 %collective-permute-start.18 = (s16[2064,128]{1,0:T(8,128)(2,1)S(1)}, s16[2064,128]{1,0:T(8,128)(2,1)S(1)}, u32[]{:S(2)}, u32[]{:S(2)}) collective-permute-start(s16[2064,128]{1,0:T(8,128)(2,1)S(1)} %get-tuple-element.46.refs_6_), channel_id=1, source_target_pairs={{0,224},{32,0},{64,32},{96,64},{128,96},{160,128},{192,160},{224,1... | collective-permute-start | bytes 1585160 | tf_op jit(solution)/shard_map/ppermute | solution.py:401
  79.2 5.7 %collective-permute-done.21.refs_5_ = s16[2064,128]{1,0:T(8,128)(2,1)S(1)} collective-permute-done((s16[2064,128]{1,0:T(8,128)(2,1)S(1)}, s16[2064,128]{1,0:T(8,128)(2,1)S(1)}, u32[]{:S(2)}, u32[]{:S(2)}) %collective-permute-start.21) | collective-permute-done | bytes 528416 | tf_op jit(solution)/shard_map/ppermute | solution.py:401
  84.9 2.8 %middle11.1 = (s16[2064,128]{1,0:T(8,128)(2,1)S(1)}, s16[2064,128]{1,0:T(8,128)(2,1)S(1)}) custom-call(s32[3]{0:T(128)S(1)} %pad_add_fusion.3.pos.refs_0_, s32[1536]{0:T(1024)S(1)} %reshape.107.tab.refs_1_, bf16[160,128,128]{2,1,0:T(8,128)(2,1)S(1)} %get-tuple-element.37.refs_2_.a, bf16[129,128,128]{2,1,0:T(8,128)(2,1)S(1)} %get-tuple-element.38.refs_3_.b, ...), custom_call_target="tpu_custom_call" | custom-call | flops 3000000000 | bytes 9000000 | tf_op jit(solution)/shard_map/middle11/pallas_call | solution.py:334
  88.4 2.1 %collective-permute-start.24 = (s16[2064,128]{1,0:T(8,128)(2,1)S(1)}, s16[2064,128]{1,0:T(8,128)(2,1)S(1)}, u32[]{:S(2)}, u32[]{:S(2)}) collective-permute-start(s16[2064,128]{1,0:T(8,128)(2,1)S(1)} %get-tuple-element.49.refs_6_), channel_id=1, source_target_pairs={{0,224},{32,0},{64,32},{96,64},{128,96},{160,128},{192,160},{224,1... | collective-permute-start | bytes 1585160 | tf_op jit(solution)/shard_map/ppermute | solution.py:401
  90.5 5.7 %collective-permute-done.19.refs_5_ = s16[2064,128]{1,0:T(8,128)(2,1)S(1)} collective-permute-done((s16[2064,128]{1,0:T(8,128)(2,1)S(1)}, s16[2064,128]{1,0:T(8,128)(2,1)S(1)}, u32[]{:S(2)}, u32[]{:S(2)}) %collective-permute-start.19) | collective-permute-done | bytes 528416 | tf_op jit(solution)/shard_map/ppermute | solution.py:401
  96.2 2.8 %middle20.1 = (s16[2064,128]{1,0:T(8,128)(2,1)S(1)}, s16[2064,128]{1,0:T(8,128)(2,1)S(1)}) custom-call(s32[3]{0:T(128)S(1)} %pad_add_fusion.3.pos.refs_0_, s32[1536]{0:T(1024)S(1)} %reshape.107.tab.refs_1_, bf16[160,128,128]{2,1,0:T(8,128)(2,1)S(1)} %get-tuple-element.37.refs_2_.a, bf16[129,128,128]{2,1,0:T(8,128)(2,1)S(1)} %get-tuple-element.38.refs_3_.b, ...), custom_call_target="tpu_custom_call" | custom-call | flops 3000000000 | bytes 9000000 | tf_op jit(solution)/shard_map/middle20/pallas_call | solution.py:334
  99.7 2.1 %collective-permute-start.22 = (s16[2064,128]{1,0:T(8,128)(2,1)S(1)}, s16[2064,128]{1,0:T(8,128)(2,1)S(1)}, u32[]{:S(2)}, u32[]{:S(2)}) collective-permute-start(s16[2064,128]{1,0:T(8,128)(2,1)S(1)} %get-tuple-element.50.unused), channel_id=1, source_target_pairs={{0,224},{32,0},{64,32},{96,64},{128,96},{160,128},{192,160},{224,1... | collective-permute-start | bytes 1585160 | tf_op jit(solution)/shard_map/ppermute | solution.py:401
  101.8 2.6 %own.1.refs_6_ = f32[32,128,128]{2,1,0:T(8,128)S(1)} custom-call(s32[3]{0:T(128)S(1)} %pad_add_fusion.3.pos.refs_0_, s32[1536]{0:T(1024)S(1)} %reshape.107.tab.refs_1_, bf16[160,128,128]{2,1,0:T(8,128)(2,1)S(1)} %get-tuple-element.37.refs_2_.a, bf16[129,128,128]{2,1,0:T(8,128)(2,1)S(1)} %get-tuple-element.38.refs_3_.b, ...), custom_call_target="tpu_custom_call" | custom-call | flops 3000000000 | bytes 9000000 | tf_op jit(solution)/shard_map/own/pallas_call | solution.py:350
  104.5 3.1 %collective-permute-done.25.refs_5_ = s16[2064,128]{1,0:T(8,128)(2,1)S(1)} collective-permute-done((s16[2064,128]{1,0:T(8,128)(2,1)S(1)}, s16[2064,128]{1,0:T(8,128)(2,1)S(1)}, u32[]{:S(2)}, u32[]{:S(2)}) %collective-permute-start.25) | collective-permute-done | bytes 528416 | tf_op jit(solution)/shard_map/ppermute | solution.py:401
  107.5 2.8 %middle21.1 = (s16[2064,128]{1,0:T(8,128)(2,1)S(1)}, s16[2064,128]{1,0:T(8,128)(2,1)S(1)}) custom-call(s32[3]{0:T(128)S(1)} %pad_add_fusion.3.pos.refs_0_, s32[1536]{0:T(1024)S(1)} %reshape.107.tab.refs_1_, bf16[160,128,128]{2,1,0:T(8,128)(2,1)S(1)} %get-tuple-element.37.refs_2_.a, bf16[129,128,128]{2,1,0:T(8,128)(2,1)S(1)} %get-tuple-element.38.refs_3_.b, ...), custom_call_target="tpu_custom_call" | custom-call | flops 3000000000 | bytes 9000000 | tf_op jit(solution)/shard_map/middle21/pallas_call | solution.py:334
  110.4 0.9 collective-permute-start.29
  111.2 2.1 %collective-permute-start.28 = (s16[2064,128]{1,0:T(8,128)(2,1)S(1)}, s16[2064,128]{1,0:T(8,128)(2,1)S(1)}, u32[]{:S(2)}, u32[]{:S(2)}) collective-permute-start(s16[2064,128]{1,0:T(8,128)(2,1)S(1)} %get-tuple-element.53.unused), channel_id=1, source_target_pairs={{0,224},{32,0},{64,32},{96,64},{128,96},{160,128},{192,160},{224,1... | collective-permute-start | bytes 1585160 | tf_op jit(solution)/shard_map/ppermute | solution.py:401
  113.3 5.5 %collective-permute-done.23.in_l = s16[2064,128]{1,0:T(8,128)(2,1)S(1)} collective-permute-done((s16[2064,128]{1,0:T(8,128)(2,1)S(1)}, s16[2064,128]{1,0:T(8,128)(2,1)S(1)}, u32[]{:S(2)}, u32[]{:S(2)}) %collective-permute-start.23) | collective-permute-done | bytes 528416 | tf_op jit(solution)/shard_map/ppermute | solution.py:401
  119.4 2.7 %collective-permute-start.27 = (s16[2,272,128]{2,1,0:T(8,128)(2,1)S(1)}, s16[2,272,128]{2,1,0:T(8,128)(2,1)S(1)}, u32[]{:S(2)}, u32[]{:S(2)}) collective-permute-start(s16[2,272,128]{2,1,0:T(8,128)(2,1)S(1)} %get-tuple-element.55), channel_id=1, source_target_pairs={{0,6},{1,7},{2,0},{3,1},{4,2},{5,3},{6,4},{7,5},{8,14},{9,15},{10,... | collective-permute-start | bytes 417800 | tf_op jit(solution)/shard_map/ppermute | solution.py:401
  122.1 8.1 %collective-permute-done.29.in_l = s16[2064,128]{1,0:T(8,128)(2,1)S(1)} collective-permute-done((s16[2064,128]{1,0:T(8,128)(2,1)S(1)}, s16[2064,128]{1,0:T(8,128)(2,1)S(1)}, u32[]{:S(2)}, u32[]{:S(2)}) %collective-permute-start.29) | collective-permute-done | bytes 528416 | tf_op jit(solution)/shard_map/ppermute | solution.py:401
  130.7 2.7 %collective-permute-start.33 = (s16[2,272,128]{2,1,0:T(8,128)(2,1)S(1)}, s16[2,272,128]{2,1,0:T(8,128)(2,1)S(1)}, u32[]{:S(2)}, u32[]{:S(2)}) collective-permute-start(s16[2,272,128]{2,1,0:T(8,128)(2,1)S(1)} %get-tuple-element.63), channel_id=1, source_target_pairs={{0,6},{1,7},{2,0},{3,1},{4,2},{5,3},{6,4},{7,5},{8,14},{9,15},{10,... | collective-permute-start | bytes 417800 | tf_op jit(solution)/shard_map/ppermute | solution.py:401
  133.5 2.3 %collective-permute-start.31 = (s16[1072,128]{1,0:T(8,128)(2,1)S(1)}, s16[1072,128]{1,0:T(8,128)(2,1)S(1)}, u32[]{:S(2)}, u32[]{:S(2)}) collective-permute-start(s16[1072,128]{1,0:T(8,128)(2,1)S(1)} %pad_add_fusion), channel_id=1, source_target_pairs={{0,1},{1,0},{2,3},{3,2},{4,5},{5,4},{6,7},{7,6},{8,9},{9,8},{10,11... | collective-permute-start | bytes 823304 | tf_op jit(solution)/shard_map/ppermute | solution.py:416
  135.9 2.9 %collective-permute-start.34 = (s16[544,128]{1,0:T(8,128)(2,1)S(1)}, s16[544,128]{1,0:T(8,128)(2,1)S(1)}, u32[]{:S(2)}, u32[]{:S(2)}) collective-permute-start(s16[544,128]{1,0:T(8,128)(2,1)S(1)} %pad_add_fusion.1), channel_id=1, source_target_pairs={{0,1},{1,0},{2,3},{3,2},{4,5},{5,4},{6,7},{7,6},{8,9},{9,8},{10,11... | collective-permute-start | bytes 417800 | tf_op jit(solution)/shard_map/ppermute | solution.py:416
  138.9 1.6 %deliver0.1.early = f32[32,128,128]{2,1,0:T(8,128)} custom-call(s32[3]{0:T(128)S(1)} %pad_add_fusion.3.pos.refs_0_, s16[2,528,128]{2,1,0:T(8,128)(2,1)S(1)} %collective-permute-done.26.far, s16[2,272,128]{2,1,0:T(8,128)(2,1)S(1)} %collective-permute-done.30.unused.up, s16[2,272,128]{2,1,0:T(8,128)(2,1)S(1)} %collective-permute-done.27.down, ...), custom_call_target="tpu_custom_call" | custom-call | flops 1000000000 | bytes 3000000 | tf_op jit(solution)/shard_map/deliver0/pallas_call | solution.py:379
  140.6 1.5 %deliver1.1 = f32[32,128,128]{2,1,0:T(8,128)} custom-call(s32[3]{0:T(128)S(1)} %pad_add_fusion.3.pos.refs_0_, f32[32,128,128]{2,1,0:T(8,128)} %deliver0.1.early, s16[2,272,128]{2,1,0:T(8,128)(2,1)S(1)} %collective-permute-done.32.up, s16[2,272,128]{2,1,0:T(8,128)(2,1)S(1)} %collective-permute-done.33.down, ...), custom_call_target="tpu_custom_call", output_to_operand_aliasing={{}: (1, {})} | custom-call | flops 1000000000 | bytes 3000000 | tf_op jit(solution)/shard_map/deliver1/pallas_call | solution.py:379
  (69 shorter events, 8.2 us)
Async XLA Ops:
  0.0 5.9 %collective-permute-start.6 = (bf16[128,32,128]{2,1,0:T(8,128)(2,1)}, bf16[128,32,128]{2,1,0:T(8,128)(2,1)}, u32[]{:S(2)}, u32[]{:S(2)}) collective-permute-start(bf16[128,32,128]{2,1,0:T(8,128)(2,1)} %bitcast.21), channel_id=1, source_target_pairs={{0,1},{1,0},{2,3},{3,2},{4,5},{5,4},{6,7},{7,6},{8,9},{9,8},{10,11... | collective-permute-start | bytes 3145736 | tf_op jit(solution)/shard_map/ppermute | solution.py:416
  3.2 18.1 %collective-permute-start.5 = (bf16[128,32,128]{2,1,0:T(8,128)(2,1)}, bf16[128,32,128]{2,1,0:T(8,128)(2,1)S(1)}, u32[]{:S(2)}, u32[]{:S(2)}) collective-permute-start(bf16[128,32,128]{2,1,0:T(8,128)(2,1)} %bitcast.22), channel_id=1, source_target_pairs={{0,8},{1,25},{2,10},{3,27},{4,12},{5,29},{6,14},{7,31},{8,16},{9,1... | collective-permute-start | bytes 3145736 | tf_op jit(solution)/shard_map/ppermute | solution.py:411
  5.9 22.9 %collective-permute-start.7 = (bf16[128,32,128]{2,1,0:T(8,128)(2,1)}, bf16[128,32,128]{2,1,0:T(8,128)(2,1)}, u32[]{:S(2)}, u32[]{:S(2)}) collective-permute-start(bf16[128,32,128]{2,1,0:T(8,128)(2,1)} %collective-permute-done.6), channel_id=1, source_target_pairs={{0,8},{1,25},{2,10},{3,27},{4,12},{5,29},{6,14},{7,31},{8,16},{9,1... | collective-permute-start | bytes 3145736 | tf_op jit(solution)/shard_map/ppermute | solution.py:411
  6.9 10.3 %collective-permute-start.1 = (bf16[160,16,128]{2,1,0:T(8,128)(2,1)}, bf16[160,16,128]{2,1,0:T(8,128)(2,1)}, u32[]{:S(2)}, u32[]{:S(2)}) collective-permute-start(bf16[160,16,128]{2,1,0:T(8,128)(2,1)} %bitcast.24), channel_id=1, source_target_pairs={{0,2},{1,7},{2,4},{3,1},{4,6},{5,3},{6,0},{7,5},{8,10},{9,15},{10,... | collective-permute-start | bytes 1966088 | tf_op jit(solution)/shard_map/ppermute | solution.py:404
  9.3 11.3 %collective-permute-start = (bf16[160,16,128]{2,1,0:T(8,128)(2,1)}, bf16[160,16,128]{2,1,0:T(8,128)(2,1)}, u32[]{:S(2)}, u32[]{:S(2)}) collective-permute-start(bf16[160,16,128]{2,1,0:T(8,128)(2,1)} %bitcast.25), channel_id=1, source_target_pairs={{0,1},{1,0},{2,3},{3,2},{4,5},{5,4},{6,7},{7,6},{8,9},{9,8},{10,11... | collective-permute-start | bytes 1966088 | tf_op jit(solution)/shard_map/ppermute | solution.py:416
  17.2 15.8 %collective-permute-start.3 = (bf16[160,16,128]{2,1,0:T(8,128)(2,1)}, bf16[160,16,128]{2,1,0:T(8,128)(2,1)}, u32[]{:S(2)}, u32[]{:S(2)}) collective-permute-start(bf16[160,16,128]{2,1,0:T(8,128)(2,1)} %collective-permute-done.1.p1), channel_id=1, source_target_pairs={{0,2},{1,7},{2,4},{3,1},{4,6},{5,3},{6,0},{7,5},{8,10},{9,15},{10,... | collective-permute-start | bytes 1966088 | tf_op jit(solution)/shard_map/ppermute | solution.py:404
  20.6 14.9 %collective-permute-start.2 = (bf16[160,16,128]{2,1,0:T(8,128)(2,1)}, bf16[160,16,128]{2,1,0:T(8,128)(2,1)}, u32[]{:S(2)}, u32[]{:S(2)}) collective-permute-start(bf16[160,16,128]{2,1,0:T(8,128)(2,1)} %collective-permute-done.ap), channel_id=1, source_target_pairs={{0,2},{1,7},{2,4},{3,1},{4,6},{5,3},{6,0},{7,5},{8,10},{9,15},{10,... | collective-permute-start | bytes 1966088 | tf_op jit(solution)/shard_map/ppermute | solution.py:404
  21.4 20.0 %collective-permute-start.11 = (bf16[128,32,128]{2,1,0:T(8,128)(2,1)S(1)}, bf16[128,32,128]{2,1,0:T(8,128)(2,1)S(1)}, u32[]{:S(2)}, u32[]{:S(2)}) collective-permute-start(bf16[128,32,128]{2,1,0:T(8,128)(2,1)S(1)} %collective-permute-done.5.q1), channel_id=1, source_target_pairs={{0,8},{1,25},{2,10},{3,27},{4,12},{5,29},{6,14},{7,31},{8,16},{9,1... | collective-permute-start | bytes 3145736 | tf_op jit(solution)/shard_map/ppermute | solution.py:411
  28.7 9.5 %collective-permute-start.8 = (bf16[128,32,128]{2,1,0:T(8,128)(2,1)}, bf16[128,32,128]{2,1,0:T(8,128)(2,1)S(1)}, u32[]{:S(2)}, u32[]{:S(2)}) collective-permute-start(bf16[128,32,128]{2,1,0:T(8,128)(2,1)} %collective-permute-done.7), channel_id=1, source_target_pairs={{0,1},{1,0},{2,3},{3,2},{4,5},{5,4},{6,7},{7,6},{8,9},{9,8},{10,11... | collective-permute-start | bytes 3145736 | tf_op jit(solution)/shard_map/ppermute | solution.py:416
  32.9 5.4 %collective-permute-start.4 = (bf16[160,16,128]{2,1,0:T(8,128)(2,1)}, bf16[160,16,128]{2,1,0:T(8,128)(2,1)}, u32[]{:S(2)}, u32[]{:S(2)}) collective-permute-start(bf16[160,16,128]{2,1,0:T(8,128)(2,1)} %collective-permute-done.1.p1), channel_id=1, source_target_pairs={{0,1},{1,0},{2,3},{3,2},{4,5},{5,4},{6,7},{7,6},{8,9},{9,8},{10,11... | collective-permute-start | bytes 1966088 | tf_op jit(solution)/shard_map/ppermute | solution.py:416
  33.0 8.4 %collective-permute-start.10 = (bf16[160,16,128]{2,1,0:T(8,128)(2,1)}, bf16[160,16,128]{2,1,0:T(8,128)(2,1)}, u32[]{:S(2)}, u32[]{:S(2)}) collective-permute-start(bf16[160,16,128]{2,1,0:T(8,128)(2,1)} %collective-permute-done.3.p3), channel_id=1, source_target_pairs={{0,1},{1,0},{2,3},{3,2},{4,5},{5,4},{6,7},{7,6},{8,9},{9,8},{10,11... | collective-permute-start | bytes 1966088 | tf_op jit(solution)/shard_map/ppermute | solution.py:416
  35.5 5.9 %collective-permute-start.9 = (bf16[160,16,128]{2,1,0:T(8,128)(2,1)}, bf16[160,16,128]{2,1,0:T(8,128)(2,1)}, u32[]{:S(2)}, u32[]{:S(2)}) collective-permute-start(bf16[160,16,128]{2,1,0:T(8,128)(2,1)} %collective-permute-done.2.p2), channel_id=1, source_target_pairs={{0,1},{1,0},{2,3},{3,2},{4,5},{5,4},{6,7},{7,6},{8,9},{9,8},{10,11... | collective-permute-start | bytes 1966088 | tf_op jit(solution)/shard_map/ppermute | solution.py:416
  44.4 12.3 %collective-permute-start.13 = (s16[1040,128]{1,0:T(8,128)(2,1)S(1)}, s16[1040,128]{1,0:T(8,128)(2,1)S(1)}, u32[]{:S(2)}, u32[]{:S(2)}) collective-permute-start(s16[1040,128]{1,0:T(8,128)(2,1)S(1)} %get-tuple-element.40), channel_id=1, source_target_pairs={{0,32},{32,64},{64,96},{96,128},{128,160},{160,192},{192,224},{224... | collective-permute-start | bytes 798728 | tf_op jit(solution)/shard_map/ppermute | solution.py:401
  46.0 10.7 %collective-permute-start.12 = (s16[1040,128]{1,0:T(8,128)(2,1)S(1)}, s16[1040,128]{1,0:T(8,128)(2,1)S(1)}, u32[]{:S(2)}, u32[]{:S(2)}) collective-permute-start(s16[1040,128]{1,0:T(8,128)(2,1)S(1)} %get-tuple-element.39.refs_4_), channel_id=1, source_target_pairs={{0,224},{32,0},{64,32},{96,64},{128,96},{160,128},{192,160},{224,1... | collective-permute-start | bytes 798728 | tf_op jit(solution)/shard_map/ppermute | solution.py:401
  51.7 10.7 %collective-permute-start.17 = (s16[1040,128]{1,0:T(8,128)(2,1)S(1)}, s16[1040,128]{1,0:T(8,128)(2,1)S(1)}, u32[]{:S(2)}, u32[]{:S(2)}) collective-permute-start(s16[1040,128]{1,0:T(8,128)(2,1)S(1)} %get-tuple-element.44), channel_id=1, source_target_pairs={{0,32},{32,64},{64,96},{96,128},{128,160},{160,192},{192,224},{224... | collective-permute-start | bytes 798728 | tf_op jit(solution)/shard_map/ppermute | solution.py:401
  52.0 10.4 %collective-permute-start.16 = (s16[1040,128]{1,0:T(8,128)(2,1)S(1)}, s16[1040,128]{1,0:T(8,128)(2,1)S(1)}, u32[]{:S(2)}, u32[]{:S(2)}) collective-permute-start(s16[1040,128]{1,0:T(8,128)(2,1)S(1)} %get-tuple-element.41.refs_6_), channel_id=1, source_target_pairs={{0,224},{32,0},{64,32},{96,64},{128,96},{160,128},{192,160},{224,1... | collective-permute-start | bytes 798728 | tf_op jit(solution)/shard_map/ppermute | solution.py:401
  59.5 14.1 %collective-permute-start.15 = (s16[2064,128]{1,0:T(8,128)(2,1)S(1)}, s16[2064,128]{1,0:T(8,128)(2,1)S(1)}, u32[]{:S(2)}, u32[]{:S(2)}) collective-permute-start(s16[2064,128]{1,0:T(8,128)(2,1)S(1)} %get-tuple-element.43), channel_id=1, source_target_pairs={{0,32},{32,64},{64,96},{96,128},{128,160},{160,192},{192,224},{224... | collective-permute-start | bytes 1585160 | tf_op jit(solution)/shard_map/ppermute | solution.py:401
  59.6 14.0 %collective-permute-start.14 = (s16[2064,128]{1,0:T(8,128)(2,1)S(1)}, s16[2064,128]{1,0:T(8,128)(2,1)S(1)}, u32[]{:S(2)}, u32[]{:S(2)}) collective-permute-start(s16[2064,128]{1,0:T(8,128)(2,1)S(1)} %get-tuple-element.42.refs_6_), channel_id=1, source_target_pairs={{0,224},{32,0},{64,32},{96,64},{128,96},{160,128},{192,160},{224,1... | collective-permute-start | bytes 1585160 | tf_op jit(solution)/shard_map/ppermute | solution.py:401
  65.2 19.7 %collective-permute-start.21 = (s16[2064,128]{1,0:T(8,128)(2,1)S(1)}, s16[2064,128]{1,0:T(8,128)(2,1)S(1)}, u32[]{:S(2)}, u32[]{:S(2)}) collective-permute-start(s16[2064,128]{1,0:T(8,128)(2,1)S(1)} %get-tuple-element.48), channel_id=1, source_target_pairs={{0,32},{32,64},{64,96},{96,128},{128,160},{160,192},{192,224},{224... | collective-permute-start | bytes 1585160 | tf_op jit(solution)/shard_map/ppermute | solution.py:401
  65.3 19.6 %collective-permute-start.20 = (s16[2064,128]{1,0:T(8,128)(2,1)S(1)}, s16[2064,128]{1,0:T(8,128)(2,1)S(1)}, u32[]{:S(2)}, u32[]{:S(2)}) collective-permute-start(s16[2064,128]{1,0:T(8,128)(2,1)S(1)} %get-tuple-element.45.refs_6_), channel_id=1, source_target_pairs={{0,224},{32,0},{64,32},{96,64},{128,96},{160,128},{192,160},{224,1... | collective-permute-start | bytes 1585160 | tf_op jit(solution)/shard_map/ppermute | solution.py:401
  76.4 19.8 %collective-permute-start.19 = (s16[2064,128]{1,0:T(8,128)(2,1)S(1)}, s16[2064,128]{1,0:T(8,128)(2,1)S(1)}, u32[]{:S(2)}, u32[]{:S(2)}) collective-permute-start(s16[2064,128]{1,0:T(8,128)(2,1)S(1)} %get-tuple-element.47), channel_id=1, source_target_pairs={{0,32},{32,64},{64,96},{96,128},{128,160},{160,192},{192,224},{224... | collective-permute-start | bytes 1585160 | tf_op jit(solution)/shard_map/ppermute | solution.py:401
  77.1 19.1 %collective-permute-start.18 = (s16[2064,128]{1,0:T(8,128)(2,1)S(1)}, s16[2064,128]{1,0:T(8,128)(2,1)S(1)}, u32[]{:S(2)}, u32[]{:S(2)}) collective-permute-start(s16[2064,128]{1,0:T(8,128)(2,1)S(1)} %get-tuple-element.46.refs_6_), channel_id=1, source_target_pairs={{0,224},{32,0},{64,32},{96,64},{128,96},{160,128},{192,160},{224,1... | collective-permute-start | bytes 1585160 | tf_op jit(solution)/shard_map/ppermute | solution.py:401
  87.7 19.8 %collective-permute-start.25 = (s16[2064,128]{1,0:T(8,128)(2,1)S(1)}, s16[2064,128]{1,0:T(8,128)(2,1)S(1)}, u32[]{:S(2)}, u32[]{:S(2)}) collective-permute-start(s16[2064,128]{1,0:T(8,128)(2,1)S(1)} %get-tuple-element.52), channel_id=1, source_target_pairs={{0,32},{32,64},{64,96},{96,128},{128,160},{160,192},{192,224},{224... | collective-permute-start | bytes 1585160 | tf_op jit(solution)/shard_map/ppermute | solution.py:401
  88.4 19.2 %collective-permute-start.24 = (s16[2064,128]{1,0:T(8,128)(2,1)S(1)}, s16[2064,128]{1,0:T(8,128)(2,1)S(1)}, u32[]{:S(2)}, u32[]{:S(2)}) collective-permute-start(s16[2064,128]{1,0:T(8,128)(2,1)S(1)} %get-tuple-element.49.refs_6_), channel_id=1, source_target_pairs={{0,224},{32,0},{64,32},{96,64},{128,96},{160,128},{192,160},{224,1... | collective-permute-start | bytes 1585160 | tf_op jit(solution)/shard_map/ppermute | solution.py:401
  99.1 19.8 %collective-permute-start.23 = (s16[2064,128]{1,0:T(8,128)(2,1)S(1)}, s16[2064,128]{1,0:T(8,128)(2,1)S(1)}, u32[]{:S(2)}, u32[]{:S(2)}) collective-permute-start(s16[2064,128]{1,0:T(8,128)(2,1)S(1)} %get-tuple-element.51), channel_id=1, source_target_pairs={{0,32},{32,64},{64,96},{96,128},{128,160},{160,192},{192,224},{224... | collective-permute-start | bytes 1585160 | tf_op jit(solution)/shard_map/ppermute | solution.py:401
  99.7 19.1 %collective-permute-start.22 = (s16[2064,128]{1,0:T(8,128)(2,1)S(1)}, s16[2064,128]{1,0:T(8,128)(2,1)S(1)}, u32[]{:S(2)}, u32[]{:S(2)}) collective-permute-start(s16[2064,128]{1,0:T(8,128)(2,1)S(1)} %get-tuple-element.50.unused), channel_id=1, source_target_pairs={{0,224},{32,0},{64,32},{96,64},{128,96},{160,128},{192,160},{224,1... | collective-permute-start | bytes 1585160 | tf_op jit(solution)/shard_map/ppermute | solution.py:401
  110.4 19.8 %collective-permute-start.29 = (s16[2064,128]{1,0:T(8,128)(2,1)S(1)}, s16[2064,128]{1,0:T(8,128)(2,1)S(1)}, u32[]{:S(2)}, u32[]{:S(2)}) collective-permute-start(s16[2064,128]{1,0:T(8,128)(2,1)S(1)} %get-tuple-element.56), channel_id=1, source_target_pairs={{0,32},{32,64},{64,96},{96,128},{128,160},{160,192},{192,224},{224... | collective-permute-start | bytes 1585160 | tf_op jit(solution)/shard_map/ppermute | solution.py:401
  111.2 18.9 %collective-permute-start.28 = (s16[2064,128]{1,0:T(8,128)(2,1)S(1)}, s16[2064,128]{1,0:T(8,128)(2,1)S(1)}, u32[]{:S(2)}, u32[]{:S(2)}) collective-permute-start(s16[2064,128]{1,0:T(8,128)(2,1)S(1)} %get-tuple-element.53.unused), channel_id=1, source_target_pairs={{0,224},{32,0},{64,32},{96,64},{128,96},{160,128},{192,160},{224,1... | collective-permute-start | bytes 1585160 | tf_op jit(solution)/shard_map/ppermute | solution.py:401
  119.3 10.8 %collective-permute-start.30 = (s16[2,272,128]{2,1,0:T(8,128)(2,1)S(1)}, s16[2,272,128]{2,1,0:T(8,128)(2,1)S(1)}, u32[]{:S(2)}, u32[]{:S(2)}) collective-permute-start(s16[2,272,128]{2,1,0:T(8,128)(2,1)S(1)} %get-tuple-element.57), channel_id=1, source_target_pairs={{0,2},{1,3},{2,4},{3,5},{4,6},{5,7},{6,0},{7,1},{8,10},{9,11},{10,... | collective-permute-start | bytes 417800 | tf_op jit(solution)/shard_map/ppermute | solution.py:401
  119.4 14.0 %collective-permute-start.27 = (s16[2,272,128]{2,1,0:T(8,128)(2,1)S(1)}, s16[2,272,128]{2,1,0:T(8,128)(2,1)S(1)}, u32[]{:S(2)}, u32[]{:S(2)}) collective-permute-start(s16[2,272,128]{2,1,0:T(8,128)(2,1)S(1)} %get-tuple-element.55), channel_id=1, source_target_pairs={{0,6},{1,7},{2,0},{3,1},{4,2},{5,3},{6,4},{7,5},{8,14},{9,15},{10,... | collective-permute-start | bytes 417800 | tf_op jit(solution)/shard_map/ppermute | solution.py:401
  122.1 11.3 %collective-permute-start.26 = (s16[2,528,128]{2,1,0:T(8,128)(2,1)S(1)}, s16[2,528,128]{2,1,0:T(8,128)(2,1)S(1)}, u32[]{:S(2)}, u32[]{:S(2)}) collective-permute-start(s16[2,528,128]{2,1,0:T(8,128)(2,1)S(1)} %get-tuple-element.54), channel_id=1, source_target_pairs={{0,4},{1,5},{2,6},{3,7},{4,0},{5,1},{6,2},{7,3},{8,12},{9,13},{10,... | collective-permute-start | bytes 811016 | tf_op jit(solution)/shard_map/ppermute | solution.py:401
  130.6 5.2 %collective-permute-start.32 = (s16[2,272,128]{2,1,0:T(8,128)(2,1)S(1)}, s16[2,272,128]{2,1,0:T(8,128)(2,1)S(1)}, u32[]{:S(2)}, u32[]{:S(2)}) collective-permute-start(s16[2,272,128]{2,1,0:T(8,128)(2,1)S(1)} %get-tuple-element.62), channel_id=1, source_target_pairs={{0,2},{1,3},{2,4},{3,5},{4,6},{5,7},{6,0},{7,1},{8,10},{9,11},{10,... | collective-permute-start | bytes 417800 | tf_op jit(solution)/shard_map/ppermute | solution.py:401
  130.7 5.1 %collective-permute-start.33 = (s16[2,272,128]{2,1,0:T(8,128)(2,1)S(1)}, s16[2,272,128]{2,1,0:T(8,128)(2,1)S(1)}, u32[]{:S(2)}, u32[]{:S(2)}) collective-permute-start(s16[2,272,128]{2,1,0:T(8,128)(2,1)S(1)} %get-tuple-element.63), channel_id=1, source_target_pairs={{0,6},{1,7},{2,0},{3,1},{4,2},{5,3},{6,4},{7,5},{8,14},{9,15},{10,... | collective-permute-start | bytes 417800 | tf_op jit(solution)/shard_map/ppermute | solution.py:401
  133.5 5.4 %collective-permute-start.31 = (s16[1072,128]{1,0:T(8,128)(2,1)S(1)}, s16[1072,128]{1,0:T(8,128)(2,1)S(1)}, u32[]{:S(2)}, u32[]{:S(2)}) collective-permute-start(s16[1072,128]{1,0:T(8,128)(2,1)S(1)} %pad_add_fusion), channel_id=1, source_target_pairs={{0,1},{1,0},{2,3},{3,2},{4,5},{5,4},{6,7},{7,6},{8,9},{9,8},{10,11... | collective-permute-start | bytes 823304 | tf_op jit(solution)/shard_map/ppermute | solution.py:416
  135.9 4.7 %collective-permute-start.34 = (s16[544,128]{1,0:T(8,128)(2,1)S(1)}, s16[544,128]{1,0:T(8,128)(2,1)S(1)}, u32[]{:S(2)}, u32[]{:S(2)}) collective-permute-start(s16[544,128]{1,0:T(8,128)(2,1)S(1)} %pad_add_fusion.1), channel_id=1, source_target_pairs={{0,1},{1,0},{2,3},{3,2},{4,5},{5,4},{6,7},{7,6},{8,9},{9,8},{10,11... | collective-permute-start | bytes 417800 | tf_op jit(solution)/shard_map/ppermute | solution.py:416
  138.8 1.8 %collective-permute-start.35 = (s16[528,128]{1,0:T(8,128)(2,1)S(1)}, s16[528,128]{1,0:T(8,128)(2,1)S(1)}, u32[]{:S(2)}, u32[]{:S(2)}) collective-permute-start(s16[528,128]{1,0:T(8,128)(2,1)S(1)} %get-tuple-element.64), channel_id=1, source_target_pairs={{0,1},{1,0},{2,3},{3,2},{4,5},{5,4},{6,7},{7,6},{8,9},{9,8},{10,11... | collective-permute-start | bytes 405512 | tf_op jit(solution)/shard_map/ppermute | solution.py:416

commit v6 on v5

--- a/solution.py
+++ b/solution.py
@@ -264,32 +264,36 @@
 WIDE, SLIM = 4 * TILE + CODE_ROWS, 2 * TILE + CODE_ROWS
 
 
-def deliver_early_kernel(pos, far, up, down, swapped, home, out, tiles, scale, sem):
+def deliver_first_kernel(pos, far, up, down, home, out, tiles, scale, sem):
+    col = pos[2]
+    blocks = [(far.at[0], 0, col + 4, 0, 4), (up.at[0], 0, col - 2, 0, 2), (down.at[0], 0, col + 2, 0, 2)]
+    kept = pltpu.make_async_copy(home, out.at[pl.ds(col * 4, 4)], sem.at[len(blocks)])
+    kept.start()
+    for one in deliver_blocks(blocks, out, tiles, scale, sem) + [kept]:
+        one.wait()
+
+
+def deliver_second_kernel(pos, before, swapped, out, tiles, scale, sem):
     col = pos[2]
     other = col + 1 - 2 * (col % 2)
     blocks = [
-        (far.at[0], 0, col + 4, 0, 4),
-        (up.at[0], 0, col - 2, 0, 2),
-        (down.at[0], 0, col + 2, 0, 2),
         (swapped, 0, other + 4, 0, 4),
         (swapped, WIDE, other - 2, 0, 2),
         (swapped, WIDE + SLIM, other + 2, 0, 2),
     ]
-    kept = pltpu.make_async_copy(home, out.at[pl.ds(col * 4, 4)], sem.at[len(blocks)])
-    kept.start()
-    for one in deliver_blocks(blocks, out, tiles, scale, sem) + [kept]:
+    for one in deliver_blocks(blocks, out, tiles, scale, sem):
         one.wait()
 
 
-def deliver_late_kernel(pos, early, up, down, swapped, cross, out, tiles, scale, sem):
+def deliver_last_kernel(pos, before, up, down, swapped, cross, out, tiles, scale, sem):
     col = pos[2]
     other = col + 1 - 2 * (col % 2)
     blocks = [
-        (cross, 0, other, 0, 4),
         (up.at[0], 0, col - 2, 2, 2),
         (down.at[0], 0, col + 2, 2, 2),
         (swapped, 0, other - 2, 2, 2),
         (swapped, SLIM, other + 2, 2, 2),
+        (cross, 0, other, 0, 4),
     ]
     for one in deliver_blocks(blocks, out, tiles, scale, sem):
         one.wait()
@@ -478,27 +482,16 @@
         own,
         *flying[1],
     )
-    up1, down1, cross = x_up(up1), x_down(down1), swap(cross)
+    up1, down1 = x_up(up1), x_down(down1)
     far, down, home = lax.optimization_barrier((far, down, home))
     swapped = swap(jnp.concatenate([far[1], up[1], down[1]]))
-    early = deliver(
-        deliver_early_kernel, "deliver0", [VMEM_SPEC] * 5, col * 4, 16, {}, pos, far, up, down, swapped, home
-    )
+    done = deliver(deliver_first_kernel, "deliver0", [VMEM_SPEC] * 4, col * 4, 8, {}, pos, far, up, down, home)
+    done, up1, down1, cross = lax.optimization_barrier((done, up1, down1, cross))
+    cross = swap(cross)
     swapped1 = swap(jnp.concatenate([up1[1], down1[1]]))
-    return deliver(
-        deliver_late_kernel,
-        "deliver1",
-        [ANY_SPEC] + [VMEM_SPEC] * 4,
-        col * 4,
-        12,
-        {1: 0},
-        pos,
-        early,
-        up1,
-        down1,
-        swapped1,
-        cross,
-    )
+    specs = [ANY_SPEC] + [VMEM_SPEC] * 4
+    done = deliver(deliver_second_kernel, "deliver1", specs[:2], col * 4, 8, {1: 0}, pos, done, swapped)
+    return deliver(deliver_last_kernel, "deliver2", specs, col * 4, 12, {1: 0}, pos, done, up1, down1, swapped1, cross)
 
 
 def solution(mesh):

time: 145 us -> 144 us (level)
  starting transfers between devices: 52.1 us -> 50.6 us
    ppermute x9, starting transfers between devices: 13.2 us -> 11.8 us  [swap(): return lax.ppermute(x, 'col', [(i, i ^ 1) for i in range(col)])]
    pallas_call x2 -> x3, Pallas kernels: 3.16 us -> 4.4 us  [deliver(): pl.pallas_call(kernel, out_shape=jax.ShapeDtypeStruct((tiles, TILE, TILE)...]
  transfers between devices with their start and end apart: 36 -> 36, of which waited for: 13 -> 12; matrix products, arithmetic and copies ran while one was open for 5% -> 5% of each run, Pallas kernels for 19% -> 20%
where the time goes in v6:
time: 144 us; the launch traced here: 142 us
  waiting for transfers between devices  51.5 us (36%)
  starting transfers between devices  50.6 us (35%)
  Pallas kernels  32.7 us (23%)
  other arithmetic  4.21 us (3%)
  local copies, waits for them, and re-layouts  2.29 us (2%)
    ppermute x21, waiting for transfers between devices, shift(): return lambda x: lax.ppermute(x, axis, pairs)  35.9 us
    ppermute x21, starting transfers between devices, shift(): return lambda x: lax.ppermute(x, axis, pairs)  30.7 us
    pallas_call x7, Pallas kernels, step(): pl.pallas_call(body, out_shape=out_shape, in_specs=ins, out_specs=jax.tre...  18.7 us
    ppermute x9, starting transfers between devices, swap(): return lax.ppermute(x, 'col', [(i, i ^ 1) for i in range(col)])  11.8 us
    ppermute x3, waiting for transfers between devices, y_split(): return lax.ppermute(x, ('row', 'col'), pairs)  7.15 us
    ppermute x3, waiting for transfers between devices, x_split(): lax.ppermute(x, 'col', [(i, (i + 2 - 4 * (i % 2)) % col) for i in range(c...  6.86 us
    ppermute x3, starting transfers between devices, x_split(): lax.ppermute(x, 'col', [(i, (i + 2 - 4 * (i % 2)) % col) for i in range(c...  5.92 us
    pallas_call x3, Pallas kernels, deliver(): pl.pallas_call(kernel, out_shape=jax.ShapeDtypeStruct((tiles, TILE, TILE)...  4.4 us
  transfers between devices with their start and end apart: 36, of which 12 were waited for; matrix products, arithmetic and copies ran while one was open for 5% of the time, Pallas kernels for 20%

profile of v6, /device:TPU:1, one launch (start us, length us, event | category | flops | bytes accessed | tf_op | source)
XLA Modules:
  0.0 142.0 jit_solution(9406729109724546032)
XLA Ops:
  0.0 3.2 %collective-permute-start.6 = (bf16[128,32,128]{2,1,0:T(8,128)(2,1)}, bf16[128,32,128]{2,1,0:T(8,128)(2,1)}, u32[]{:S(2)}, u32[]{:S(2)}) collective-permute-start(bf16[128,32,128]{2,1,0:T(8,128)(2,1)} %bitcast.21), channel_id=1, source_target_pairs={{0,1},{1,0},{2,3},{3,2},{4,5},{5,4},{6,7},{7,6},{8,9},{9,8},{10,11... | collective-permute-start | bytes 3145736 | tf_op jit(solution)/shard_map/ppermute | solution.py:420
  3.2 1.0 collective-permute-start.5
  4.2 1.6 %collective-permute-done.6 = bf16[128,32,128]{2,1,0:T(8,128)(2,1)} collective-permute-done((bf16[128,32,128]{2,1,0:T(8,128)(2,1)}, bf16[128,32,128]{2,1,0:T(8,128)(2,1)}, u32[]{:S(2)}, u32[]{:S(2)}) %collective-permute-start.6) | collective-permute-done | bytes 1048608 | tf_op jit(solution)/shard_map/ppermute | solution.py:420
  5.9 1.0 collective-permute-start.7
  6.9 2.5 %collective-permute-start.1 = (bf16[160,16,128]{2,1,0:T(8,128)(2,1)}, bf16[160,16,128]{2,1,0:T(8,128)(2,1)}, u32[]{:S(2)}, u32[]{:S(2)}) collective-permute-start(bf16[160,16,128]{2,1,0:T(8,128)(2,1)} %bitcast.24), channel_id=1, source_target_pairs={{0,2},{1,7},{2,4},{3,1},{4,6},{5,3},{6,0},{7,5},{8,10},{9,15},{10,... | collective-permute-start | bytes 1966088 | tf_op jit(solution)/shard_map/ppermute | solution.py:408
  9.4 0.8 copy.38
  12.4 4.8 %collective-permute-done.1.p1 = bf16[160,16,128]{2,1,0:T(8,128)(2,1)} collective-permute-done((bf16[160,16,128]{2,1,0:T(8,128)(2,1)}, bf16[160,16,128]{2,1,0:T(8,128)(2,1)}, u32[]{:S(2)}, u32[]{:S(2)}) %collective-permute-start.1) | collective-permute-done | bytes 655392 | tf_op jit(solution)/shard_map/ppermute | solution.py:408
  17.2 3.4 %collective-permute-start.3 = (bf16[160,16,128]{2,1,0:T(8,128)(2,1)}, bf16[160,16,128]{2,1,0:T(8,128)(2,1)}, u32[]{:S(2)}, u32[]{:S(2)}) collective-permute-start(bf16[160,16,128]{2,1,0:T(8,128)(2,1)} %collective-permute-done.1.p1), channel_id=1, source_target_pairs={{0,2},{1,7},{2,4},{3,1},{4,6},{5,3},{6,0},{7,5},{8,10},{9,15},{10,... | collective-permute-start | bytes 1966088 | tf_op jit(solution)/shard_map/ppermute | solution.py:408
  21.6 7.1 %collective-permute-done.7 = bf16[128,32,128]{2,1,0:T(8,128)(2,1)} collective-permute-done((bf16[128,32,128]{2,1,0:T(8,128)(2,1)}, bf16[128,32,128]{2,1,0:T(8,128)(2,1)}, u32[]{:S(2)}, u32[]{:S(2)}) %collective-permute-start.7) | collective-permute-done | bytes 1048608 | tf_op jit(solution)/shard_map/ppermute | solution.py:415
  28.7 2.1 %collective-permute-start.8 = (bf16[128,32,128]{2,1,0:T(8,128)(2,1)}, bf16[128,32,128]{2,1,0:T(8,128)(2,1)S(1)}, u32[]{:S(2)}, u32[]{:S(2)}) collective-permute-start(bf16[128,32,128]{2,1,0:T(8,128)(2,1)} %collective-permute-done.7), channel_id=1, source_target_pairs={{0,1},{1,0},{2,3},{3,2},{4,5},{5,4},{6,7},{7,6},{8,9},{9,8},{10,11... | collective-permute-start | bytes 3145736 | tf_op jit(solution)/shard_map/ppermute | solution.py:420
  30.8 0.8 compare_reduce_fusion
  31.7 0.8 copy.37
  33.5 2.0 %collective-permute-done.2.p2 = bf16[160,16,128]{2,1,0:T(8,128)(2,1)} collective-permute-done((bf16[160,16,128]{2,1,0:T(8,128)(2,1)}, bf16[160,16,128]{2,1,0:T(8,128)(2,1)}, u32[]{:S(2)}, u32[]{:S(2)}) %collective-permute-start.2) | collective-permute-done | bytes 655392 | tf_op jit(solution)/shard_map/ppermute | solution.py:408
  35.5 2.0 %collective-permute-start.9 = (bf16[160,16,128]{2,1,0:T(8,128)(2,1)}, bf16[160,16,128]{2,1,0:T(8,128)(2,1)}, u32[]{:S(2)}, u32[]{:S(2)}) collective-permute-start(bf16[160,16,128]{2,1,0:T(8,128)(2,1)} %collective-permute-done.2.p2), channel_id=1, source_target_pairs={{0,1},{1,0},{2,3},{3,2},{4,5},{5,4},{6,7},{7,6},{8,9},{9,8},{10,11... | collective-permute-start | bytes 1966088 | tf_op jit(solution)/shard_map/ppermute | solution.py:420
  38.3 3.1 %assemble.1 = (bf16[160,128,128]{2,1,0:T(8,128)(2,1)S(1)}, bf16[129,128,128]{2,1,0:T(8,128)(2,1)S(1)}) custom-call(s32[3]{0:T(128)S(1)} %pad_add_fusion.3.pos.refs_0_, bf16[160,16,128]{2,1,0:T(8,128)(2,1)} %bitcast.26, bf16[160,16,128]{2,1,0:T(8,128)(2,1)} %collective-permute-done.ap, bf16[160,16,128]{2,1,0:T(8,128)(2,1)} %collective-permute-done.1.p1, ...), custom_call_target="tpu_custom_call" | custom-call | tf_op jit(solution)/shard_map/assemble/pallas_call | solution.py:432
  41.4 3.0 %first0.1 = (s16[1040,128]{1,0:T(8,128)(2,1)S(1)}, s16[1040,128]{1,0:T(8,128)(2,1)S(1)}, bf16[160,128,128]{2,1,0:T(8,128)(2,1)S(1)}, bf16[129,128,128]{2,1,0:T(8,128)(2,1)S(1)}) custom-call(s32[3]{0:T(128)S(1)} %pad_add_fusion.3.pos.refs_0_, s32[1536]{0:T(1024)S(1)} %reshape.107.tab.refs_1_, ...), custom_call_target="tpu_custom_call", output_to_operand_aliasing={{2}: (2, {}), {3}: (3, {})} | custom-call | flops 2000000000 | bytes 6000000 | tf_op jit(solution)/shard_map/first0/pallas_call | solution.py:448
  44.4 1.6 %collective-permute-start.13 = (s16[1040,128]{1,0:T(8,128)(2,1)S(1)}, s16[1040,128]{1,0:T(8,128)(2,1)S(1)}, u32[]{:S(2)}, u32[]{:S(2)}) collective-permute-start(s16[1040,128]{1,0:T(8,128)(2,1)S(1)} %get-tuple-element.44), channel_id=1, source_target_pairs={{0,32},{32,64},{64,96},{96,128},{128,160},{160,192},{192,224},{224... | collective-permute-start | bytes 798728 | tf_op jit(solution)/shard_map/ppermute | solution.py:405
  46.0 4.0 %collective-permute-start.12 = (s16[1040,128]{1,0:T(8,128)(2,1)S(1)}, s16[1040,128]{1,0:T(8,128)(2,1)S(1)}, u32[]{:S(2)}, u32[]{:S(2)}) collective-permute-start(s16[1040,128]{1,0:T(8,128)(2,1)S(1)} %get-tuple-element.43.refs_4_), channel_id=1, source_target_pairs={{0,224},{32,0},{64,32},{96,64},{128,96},{160,128},{192,160},{224,1... | collective-permute-start | bytes 798728 | tf_op jit(solution)/shard_map/ppermute | solution.py:405
  50.0 1.7 %first1.1 = (s16[1040,128]{1,0:T(8,128)(2,1)S(1)}, s16[1040,128]{1,0:T(8,128)(2,1)S(1)}) custom-call(s32[3]{0:T(128)S(1)} %pad_add_fusion.3.pos.refs_0_, s32[1536]{0:T(1024)S(1)} %reshape.107.tab.refs_1_, bf16[160,128,128]{2,1,0:T(8,128)(2,1)S(1)} %get-tuple-element.41.refs_2_.a, bf16[129,128,128]{2,1,0:T(8,128)(2,1)S(1)} %get-tuple-element.42.refs_3_.b, ...), custom_call_target="tpu_custom_call" | custom-call | flops 2000000000 | bytes 6000000 | tf_op jit(solution)/shard_map/first1/pallas_call | solution.py:338
  52.0 2.7 %collective-permute-start.16 = (s16[1040,128]{1,0:T(8,128)(2,1)S(1)}, s16[1040,128]{1,0:T(8,128)(2,1)S(1)}, u32[]{:S(2)}, u32[]{:S(2)}) collective-permute-start(s16[1040,128]{1,0:T(8,128)(2,1)S(1)} %get-tuple-element.45.refs_6_), channel_id=1, source_target_pairs={{0,224},{32,0},{64,32},{96,64},{128,96},{160,128},{192,160},{224,1... | collective-permute-start | bytes 798728 | tf_op jit(solution)/shard_map/ppermute | solution.py:405
  54.7 2.0 %collective-permute-done.13.refs_5_ = s16[1040,128]{1,0:T(8,128)(2,1)S(1)} collective-permute-done((s16[1040,128]{1,0:T(8,128)(2,1)S(1)}, s16[1040,128]{1,0:T(8,128)(2,1)S(1)}, u32[]{:S(2)}, u32[]{:S(2)}) %collective-permute-start.13) | collective-permute-done | bytes 266272 | tf_op jit(solution)/shard_map/ppermute | solution.py:405
  56.7 2.8 %second0.1 = (s16[2064,128]{1,0:T(8,128)(2,1)S(1)}, s16[2064,128]{1,0:T(8,128)(2,1)S(1)}) custom-call(s32[3]{0:T(128)S(1)} %pad_add_fusion.3.pos.refs_0_, s32[1536]{0:T(1024)S(1)} %reshape.107.tab.refs_1_, bf16[160,128,128]{2,1,0:T(8,128)(2,1)S(1)} %get-tuple-element.41.refs_2_.a, bf16[129,128,128]{2,1,0:T(8,128)(2,1)S(1)} %get-tuple-element.42.refs_3_.b, ...), custom_call_target="tpu_custom_call" | custom-call | flops 3000000000 | bytes 9000000 | tf_op jit(solution)/shard_map/second0/pallas_call | solution.py:338
  59.6 2.7 %collective-permute-start.14 = (s16[2064,128]{1,0:T(8,128)(2,1)S(1)}, s16[2064,128]{1,0:T(8,128)(2,1)S(1)}, u32[]{:S(2)}, u32[]{:S(2)}) collective-permute-start(s16[2064,128]{1,0:T(8,128)(2,1)S(1)} %get-tuple-element.46.refs_6_), channel_id=1, source_target_pairs={{0,224},{32,0},{64,32},{96,64},{128,96},{160,128},{192,160},{224,1... | collective-permute-start | bytes 1585160 | tf_op jit(solution)/shard_map/ppermute | solution.py:405
  62.4 2.8 %second1.1 = (s16[2064,128]{1,0:T(8,128)(2,1)S(1)}, s16[2064,128]{1,0:T(8,128)(2,1)S(1)}) custom-call(s32[3]{0:T(128)S(1)} %pad_add_fusion.3.pos.refs_0_, s32[1536]{0:T(1024)S(1)} %reshape.107.tab.refs_1_, bf16[160,128,128]{2,1,0:T(8,128)(2,1)S(1)} %get-tuple-element.41.refs_2_.a, bf16[129,128,128]{2,1,0:T(8,128)(2,1)S(1)} %get-tuple-element.42.refs_3_.b, ...), custom_call_target="tpu_custom_call" | custom-call | flops 3000000000 | bytes 9000000 | tf_op jit(solution)/shard_map/second1/pallas_call | solution.py:338
  65.3 2.7 %collective-permute-start.20 = (s16[2064,128]{1,0:T(8,128)(2,1)S(1)}, s16[2064,128]{1,0:T(8,128)(2,1)S(1)}, u32[]{:S(2)}, u32[]{:S(2)}) collective-permute-start(s16[2064,128]{1,0:T(8,128)(2,1)S(1)} %get-tuple-element.49.refs_6_), channel_id=1, source_target_pairs={{0,224},{32,0},{64,32},{96,64},{128,96},{160,128},{192,160},{224,1... | collective-permute-start | bytes 1585160 | tf_op jit(solution)/shard_map/ppermute | solution.py:405
  68.0 5.6 %collective-permute-done.15.refs_5_ = s16[2064,128]{1,0:T(8,128)(2,1)S(1)} collective-permute-done((s16[2064,128]{1,0:T(8,128)(2,1)S(1)}, s16[2064,128]{1,0:T(8,128)(2,1)S(1)}, u32[]{:S(2)}, u32[]{:S(2)}) %collective-permute-start.15) | collective-permute-done | bytes 528416 | tf_op jit(solution)/shard_map/ppermute | solution.py:405
  73.6 2.8 %middle10.1 = (s16[2064,128]{1,0:T(8,128)(2,1)S(1)}, s16[2064,128]{1,0:T(8,128)(2,1)S(1)}) custom-call(s32[3]{0:T(128)S(1)} %pad_add_fusion.3.pos.refs_0_, s32[1536]{0:T(1024)S(1)} %reshape.107.tab.refs_1_, bf16[160,128,128]{2,1,0:T(8,128)(2,1)S(1)} %get-tuple-element.41.refs_2_.a, bf16[129,128,128]{2,1,0:T(8,128)(2,1)S(1)} %get-tuple-element.42.refs_3_.b, ...), custom_call_target="tpu_custom_call" | custom-call | flops 3000000000 | bytes 9000000 | tf_op jit(solution)/shard_map/middle10/pallas_call | solution.py:338
  77.1 2.1 %collective-permute-start.18 = (s16[2064,128]{1,0:T(8,128)(2,1)S(1)}, s16[2064,128]{1,0:T(8,128)(2,1)S(1)}, u32[]{:S(2)}, u32[]{:S(2)}) collective-permute-start(s16[2064,128]{1,0:T(8,128)(2,1)S(1)} %get-tuple-element.50.refs_6_), channel_id=1, source_target_pairs={{0,224},{32,0},{64,32},{96,64},{128,96},{160,128},{192,160},{224,1... | collective-permute-start | bytes 1585160 | tf_op jit(solution)/shard_map/ppermute | solution.py:405
  79.2 5.7 %collective-permute-done.21.refs_5_ = s16[2064,128]{1,0:T(8,128)(2,1)S(1)} collective-permute-done((s16[2064,128]{1,0:T(8,128)(2,1)S(1)}, s16[2064,128]{1,0:T(8,128)(2,1)S(1)}, u32[]{:S(2)}, u32[]{:S(2)}) %collective-permute-start.21) | collective-permute-done | bytes 528416 | tf_op jit(solution)/shard_map/ppermute | solution.py:405
  84.9 2.8 %middle11.1 = (s16[2064,128]{1,0:T(8,128)(2,1)S(1)}, s16[2064,128]{1,0:T(8,128)(2,1)S(1)}) custom-call(s32[3]{0:T(128)S(1)} %pad_add_fusion.3.pos.refs_0_, s32[1536]{0:T(1024)S(1)} %reshape.107.tab.refs_1_, bf16[160,128,128]{2,1,0:T(8,128)(2,1)S(1)} %get-tuple-element.41.refs_2_.a, bf16[129,128,128]{2,1,0:T(8,128)(2,1)S(1)} %get-tuple-element.42.refs_3_.b, ...), custom_call_target="tpu_custom_call" | custom-call | flops 3000000000 | bytes 9000000 | tf_op jit(solution)/shard_map/middle11/pallas_call | solution.py:338
  88.4 2.1 %collective-permute-start.24 = (s16[2064,128]{1,0:T(8,128)(2,1)S(1)}, s16[2064,128]{1,0:T(8,128)(2,1)S(1)}, u32[]{:S(2)}, u32[]{:S(2)}) collective-permute-start(s16[2064,128]{1,0:T(8,128)(2,1)S(1)} %get-tuple-element.53.refs_6_), channel_id=1, source_target_pairs={{0,224},{32,0},{64,32},{96,64},{128,96},{160,128},{192,160},{224,1... | collective-permute-start | bytes 1585160 | tf_op jit(solution)/shard_map/ppermute | solution.py:405
  90.5 5.7 %collective-permute-done.19.refs_5_ = s16[2064,128]{1,0:T(8,128)(2,1)S(1)} collective-permute-done((s16[2064,128]{1,0:T(8,128)(2,1)S(1)}, s16[2064,128]{1,0:T(8,128)(2,1)S(1)}, u32[]{:S(2)}, u32[]{:S(2)}) %collective-permute-start.19) | collective-permute-done | bytes 528416 | tf_op jit(solution)/shard_map/ppermute | solution.py:405
  96.2 2.8 %middle20.1 = (s16[2064,128]{1,0:T(8,128)(2,1)S(1)}, s16[2064,128]{1,0:T(8,128)(2,1)S(1)}) custom-call(s32[3]{0:T(128)S(1)} %pad_add_fusion.3.pos.refs_0_, s32[1536]{0:T(1024)S(1)} %reshape.107.tab.refs_1_, bf16[160,128,128]{2,1,0:T(8,128)(2,1)S(1)} %get-tuple-element.41.refs_2_.a, bf16[129,128,128]{2,1,0:T(8,128)(2,1)S(1)} %get-tuple-element.42.refs_3_.b, ...), custom_call_target="tpu_custom_call" | custom-call | flops 3000000000 | bytes 9000000 | tf_op jit(solution)/shard_map/middle20/pallas_call | solution.py:338
  99.7 2.1 %collective-permute-start.22 = (s16[2064,128]{1,0:T(8,128)(2,1)S(1)}, s16[2064,128]{1,0:T(8,128)(2,1)S(1)}, u32[]{:S(2)}, u32[]{:S(2)}) collective-permute-start(s16[2064,128]{1,0:T(8,128)(2,1)S(1)} %get-tuple-element.54.unused), channel_id=1, source_target_pairs={{0,224},{32,0},{64,32},{96,64},{128,96},{160,128},{192,160},{224,1... | collective-permute-start | bytes 1585160 | tf_op jit(solution)/shard_map/ppermute | solution.py:405
  101.8 2.6 %own.1.refs_6_ = f32[32,128,128]{2,1,0:T(8,128)S(1)} custom-call(s32[3]{0:T(128)S(1)} %pad_add_fusion.3.pos.refs_0_, s32[1536]{0:T(1024)S(1)} %reshape.107.tab.refs_1_, bf16[160,128,128]{2,1,0:T(8,128)(2,1)S(1)} %get-tuple-element.41.refs_2_.a, bf16[129,128,128]{2,1,0:T(8,128)(2,1)S(1)} %get-tuple-element.42.refs_3_.b, ...), custom_call_target="tpu_custom_call" | custom-call | flops 3000000000 | bytes 9000000 | tf_op jit(solution)/shard_map/own/pallas_call | solution.py:354
  104.5 3.1 %collective-permute-done.25.refs_5_ = s16[2064,128]{1,0:T(8,128)(2,1)S(1)} collective-permute-done((s16[2064,128]{1,0:T(8,128)(2,1)S(1)}, s16[2064,128]{1,0:T(8,128)(2,1)S(1)}, u32[]{:S(2)}, u32[]{:S(2)}) %collective-permute-start.25) | collective-permute-done | bytes 528416 | tf_op jit(solution)/shard_map/ppermute | solution.py:405
  107.5 2.8 %middle21.1 = (s16[2064,128]{1,0:T(8,128)(2,1)S(1)}, s16[2064,128]{1,0:T(8,128)(2,1)S(1)}) custom-call(s32[3]{0:T(128)S(1)} %pad_add_fusion.3.pos.refs_0_, s32[1536]{0:T(1024)S(1)} %reshape.107.tab.refs_1_, bf16[160,128,128]{2,1,0:T(8,128)(2,1)S(1)} %get-tuple-element.41.refs_2_.a, bf16[129,128,128]{2,1,0:T(8,128)(2,1)S(1)} %get-tuple-element.42.refs_3_.b, ...), custom_call_target="tpu_custom_call" | custom-call | flops 3000000000 | bytes 9000000 | tf_op jit(solution)/shard_map/middle21/pallas_call | solution.py:338
  110.4 0.9 collective-permute-start.29
  111.2 2.1 %collective-permute-start.28 = (s16[2064,128]{1,0:T(8,128)(2,1)S(1)}, s16[2064,128]{1,0:T(8,128)(2,1)S(1)}, u32[]{:S(2)}, u32[]{:S(2)}) collective-permute-start(s16[2064,128]{1,0:T(8,128)(2,1)S(1)} %get-tuple-element.57.unused), channel_id=1, source_target_pairs={{0,224},{32,0},{64,32},{96,64},{128,96},{160,128},{192,160},{224,1... | collective-permute-start | bytes 1585160 | tf_op jit(solution)/shard_map/ppermute | solution.py:405
  113.3 5.5 %collective-permute-done.23.in_l = s16[2064,128]{1,0:T(8,128)(2,1)S(1)} collective-permute-done((s16[2064,128]{1,0:T(8,128)(2,1)S(1)}, s16[2064,128]{1,0:T(8,128)(2,1)S(1)}, u32[]{:S(2)}, u32[]{:S(2)}) %collective-permute-start.23) | collective-permute-done | bytes 528416 | tf_op jit(solution)/shard_map/ppermute | solution.py:405
  119.4 2.7 %collective-permute-start.27 = (s16[2,272,128]{2,1,0:T(8,128)(2,1)S(1)}, s16[2,272,128]{2,1,0:T(8,128)(2,1)S(1)}, u32[]{:S(2)}, u32[]{:S(2)}) collective-permute-start(s16[2,272,128]{2,1,0:T(8,128)(2,1)S(1)} %get-tuple-element.59), channel_id=1, source_target_pairs={{0,6},{1,7},{2,0},{3,1},{4,2},{5,3},{6,4},{7,5},{8,14},{9,15},{10,... | collective-permute-start | bytes 417800 | tf_op jit(solution)/shard_map/ppermute | solution.py:405
  122.1 8.1 %collective-permute-done.29.in_l = s16[2064,128]{1,0:T(8,128)(2,1)S(1)} collective-permute-done((s16[2064,128]{1,0:T(8,128)(2,1)S(1)}, s16[2064,128]{1,0:T(8,128)(2,1)S(1)}, u32[]{:S(2)}, u32[]{:S(2)}) %collective-permute-start.29) | collective-permute-done | bytes 528416 | tf_op jit(solution)/shard_map/ppermute | solution.py:405
  130.7 2.7 %collective-permute-start.32 = (s16[2,272,128]{2,1,0:T(8,128)(2,1)S(1)}, s16[2,272,128]{2,1,0:T(8,128)(2,1)S(1)}, u32[]{:S(2)}, u32[]{:S(2)}) collective-permute-start(s16[2,272,128]{2,1,0:T(8,128)(2,1)S(1)} %get-tuple-element.67), channel_id=1, source_target_pairs={{0,6},{1,7},{2,0},{3,1},{4,2},{5,3},{6,4},{7,5},{8,14},{9,15},{10,... | collective-permute-start | bytes 417800 | tf_op jit(solution)/shard_map/ppermute | solution.py:405
  133.5 2.3 %collective-permute-start.33 = (s16[1072,128]{1,0:T(8,128)(2,1)S(1)}, s16[1072,128]{1,0:T(8,128)(2,1)S(1)}, u32[]{:S(2)}, u32[]{:S(2)}) collective-permute-start(s16[1072,128]{1,0:T(8,128)(2,1)S(1)} %pad_add_fusion), channel_id=1, source_target_pairs={{0,1},{1,0},{2,3},{3,2},{4,5},{5,4},{6,7},{7,6},{8,9},{9,8},{10,11... | collective-permute-start | bytes 823304 | tf_op jit(solution)/shard_map/ppermute | solution.py:420
  135.8 1.5 %deliver0.1.before = f32[32,128,128]{2,1,0:T(8,128)} custom-call(s32[3]{0:T(128)S(1)} %pad_add_fusion.3.pos.refs_0_, s16[2,528,128]{2,1,0:T(8,128)(2,1)S(1)} %collective-permute-done.26.far, s16[2,272,128]{2,1,0:T(8,128)(2,1)S(1)} %collective-permute-done.30.unused.up, s16[2,272,128]{2,1,0:T(8,128)(2,1)S(1)} %collective-permute-done.27.down, ...), custom_call_target="tpu_custom_call" | custom-call | flops 1000000000 | bytes 3000000 | tf_op jit(solution)/shard_map/deliver0/pallas_call | solution.py:383
  137.3 1.4 %collective-permute-start.34 = (s16[544,128]{1,0:T(8,128)(2,1)S(1)}, s16[544,128]{1,0:T(8,128)(2,1)S(1)}, u32[]{:S(2)}, u32[]{:S(2)}) collective-permute-start(s16[544,128]{1,0:T(8,128)(2,1)S(1)} %pad_add_fusion.1), channel_id=1, source_target_pairs={{0,1},{1,0},{2,3},{3,2},{4,5},{5,4},{6,7},{7,6},{8,9},{9,8},{10,11... | collective-permute-start | bytes 417800 | tf_op jit(solution)/shard_map/ppermute | solution.py:420
  138.9 1.4 deliver1.1.before
  140.3 1.5 %deliver2.1 = f32[32,128,128]{2,1,0:T(8,128)} custom-call(s32[3]{0:T(128)S(1)} %pad_add_fusion.3.pos.refs_0_, f32[32,128,128]{2,1,0:T(8,128)} %deliver1.1.before, s16[2,272,128]{2,1,0:T(8,128)(2,1)S(1)} %collective-permute-done.31.up, s16[2,272,128]{2,1,0:T(8,128)(2,1)S(1)} %collective-permute-done.32.down, ...), custom_call_target="tpu_custom_call", output_to_operand_aliasing={{}: (1, {})} | custom-call | flops 1000000000 | bytes 3000000 | tf_op jit(solution)/shard_map/deliver2/pallas_call | solution.py:383
  (69 shorter events, 8.9 us)
Async XLA Ops:
  0.0 5.9 %collective-permute-start.6 = (bf16[128,32,128]{2,1,0:T(8,128)(2,1)}, bf16[128,32,128]{2,1,0:T(8,128)(2,1)}, u32[]{:S(2)}, u32[]{:S(2)}) collective-permute-start(bf16[128,32,128]{2,1,0:T(8,128)(2,1)} %bitcast.21), channel_id=1, source_target_pairs={{0,1},{1,0},{2,3},{3,2},{4,5},{5,4},{6,7},{7,6},{8,9},{9,8},{10,11... | collective-permute-start | bytes 3145736 | tf_op jit(solution)/shard_map/ppermute | solution.py:420
  3.2 18.1 %collective-permute-start.5 = (bf16[128,32,128]{2,1,0:T(8,128)(2,1)}, bf16[128,32,128]{2,1,0:T(8,128)(2,1)S(1)}, u32[]{:S(2)}, u32[]{:S(2)}) collective-permute-start(bf16[128,32,128]{2,1,0:T(8,128)(2,1)} %bitcast.22), channel_id=1, source_target_pairs={{0,8},{1,25},{2,10},{3,27},{4,12},{5,29},{6,14},{7,31},{8,16},{9,1... | collective-permute-start | bytes 3145736 | tf_op jit(solution)/shard_map/ppermute | solution.py:415
  5.9 22.9 %collective-permute-start.7 = (bf16[128,32,128]{2,1,0:T(8,128)(2,1)}, bf16[128,32,128]{2,1,0:T(8,128)(2,1)}, u32[]{:S(2)}, u32[]{:S(2)}) collective-permute-start(bf16[128,32,128]{2,1,0:T(8,128)(2,1)} %collective-permute-done.6), channel_id=1, source_target_pairs={{0,8},{1,25},{2,10},{3,27},{4,12},{5,29},{6,14},{7,31},{8,16},{9,1... | collective-permute-start | bytes 3145736 | tf_op jit(solution)/shard_map/ppermute | solution.py:415
  6.9 10.3 %collective-permute-start.1 = (bf16[160,16,128]{2,1,0:T(8,128)(2,1)}, bf16[160,16,128]{2,1,0:T(8,128)(2,1)}, u32[]{:S(2)}, u32[]{:S(2)}) collective-permute-start(bf16[160,16,128]{2,1,0:T(8,128)(2,1)} %bitcast.24), channel_id=1, source_target_pairs={{0,2},{1,7},{2,4},{3,1},{4,6},{5,3},{6,0},{7,5},{8,10},{9,15},{10,... | collective-permute-start | bytes 1966088 | tf_op jit(solution)/shard_map/ppermute | solution.py:408
  9.3 11.3 %collective-permute-start = (bf16[160,16,128]{2,1,0:T(8,128)(2,1)}, bf16[160,16,128]{2,1,0:T(8,128)(2,1)}, u32[]{:S(2)}, u32[]{:S(2)}) collective-permute-start(bf16[160,16,128]{2,1,0:T(8,128)(2,1)} %bitcast.25), channel_id=1, source_target_pairs={{0,1},{1,0},{2,3},{3,2},{4,5},{5,4},{6,7},{7,6},{8,9},{9,8},{10,11... | collective-permute-start | bytes 1966088 | tf_op jit(solution)/shard_map/ppermute | solution.py:420
  17.2 15.8 %collective-permute-start.3 = (bf16[160,16,128]{2,1,0:T(8,128)(2,1)}, bf16[160,16,128]{2,1,0:T(8,128)(2,1)}, u32[]{:S(2)}, u32[]{:S(2)}) collective-permute-start(bf16[160,16,128]{2,1,0:T(8,128)(2,1)} %collective-permute-done.1.p1), channel_id=1, source_target_pairs={{0,2},{1,7},{2,4},{3,1},{4,6},{5,3},{6,0},{7,5},{8,10},{9,15},{10,... | collective-permute-start | bytes 1966088 | tf_op jit(solution)/shard_map/ppermute | solution.py:408
  20.6 14.9 %collective-permute-start.2 = (bf16[160,16,128]{2,1,0:T(8,128)(2,1)}, bf16[160,16,128]{2,1,0:T(8,128)(2,1)}, u32[]{:S(2)}, u32[]{:S(2)}) collective-permute-start(bf16[160,16,128]{2,1,0:T(8,128)(2,1)} %collective-permute-done.ap), channel_id=1, source_target_pairs={{0,2},{1,7},{2,4},{3,1},{4,6},{5,3},{6,0},{7,5},{8,10},{9,15},{10,... | collective-permute-start | bytes 1966088 | tf_op jit(solution)/shard_map/ppermute | solution.py:408
  21.4 20.0 %collective-permute-start.11 = (bf16[128,32,128]{2,1,0:T(8,128)(2,1)S(1)}, bf16[128,32,128]{2,1,0:T(8,128)(2,1)S(1)}, u32[]{:S(2)}, u32[]{:S(2)}) collective-permute-start(bf16[128,32,128]{2,1,0:T(8,128)(2,1)S(1)} %collective-permute-done.5.q1), channel_id=1, source_target_pairs={{0,8},{1,25},{2,10},{3,27},{4,12},{5,29},{6,14},{7,31},{8,16},{9,1... | collective-permute-start | bytes 3145736 | tf_op jit(solution)/shard_map/ppermute | solution.py:415
  28.7 9.5 %collective-permute-start.8 = (bf16[128,32,128]{2,1,0:T(8,128)(2,1)}, bf16[128,32,128]{2,1,0:T(8,128)(2,1)S(1)}, u32[]{:S(2)}, u32[]{:S(2)}) collective-permute-start(bf16[128,32,128]{2,1,0:T(8,128)(2,1)} %collective-permute-done.7), channel_id=1, source_target_pairs={{0,1},{1,0},{2,3},{3,2},{4,5},{5,4},{6,7},{7,6},{8,9},{9,8},{10,11... | collective-permute-start | bytes 3145736 | tf_op jit(solution)/shard_map/ppermute | solution.py:420
  32.9 5.4 %collective-permute-start.4 = (bf16[160,16,128]{2,1,0:T(8,128)(2,1)}, bf16[160,16,128]{2,1,0:T(8,128)(2,1)}, u32[]{:S(2)}, u32[]{:S(2)}) collective-permute-start(bf16[160,16,128]{2,1,0:T(8,128)(2,1)} %collective-permute-done.1.p1), channel_id=1, source_target_pairs={{0,1},{1,0},{2,3},{3,2},{4,5},{5,4},{6,7},{7,6},{8,9},{9,8},{10,11... | collective-permute-start | bytes 1966088 | tf_op jit(solution)/shard_map/ppermute | solution.py:420
  33.0 8.4 %collective-permute-start.10 = (bf16[160,16,128]{2,1,0:T(8,128)(2,1)}, bf16[160,16,128]{2,1,0:T(8,128)(2,1)}, u32[]{:S(2)}, u32[]{:S(2)}) collective-permute-start(bf16[160,16,128]{2,1,0:T(8,128)(2,1)} %collective-permute-done.3.p3), channel_id=1, source_target_pairs={{0,1},{1,0},{2,3},{3,2},{4,5},{5,4},{6,7},{7,6},{8,9},{9,8},{10,11... | collective-permute-start | bytes 1966088 | tf_op jit(solution)/shard_map/ppermute | solution.py:420
  35.5 5.9 %collective-permute-start.9 = (bf16[160,16,128]{2,1,0:T(8,128)(2,1)}, bf16[160,16,128]{2,1,0:T(8,128)(2,1)}, u32[]{:S(2)}, u32[]{:S(2)}) collective-permute-start(bf16[160,16,128]{2,1,0:T(8,128)(2,1)} %collective-permute-done.2.p2), channel_id=1, source_target_pairs={{0,1},{1,0},{2,3},{3,2},{4,5},{5,4},{6,7},{7,6},{8,9},{9,8},{10,11... | collective-permute-start | bytes 1966088 | tf_op jit(solution)/shard_map/ppermute | solution.py:420
  44.4 12.3 %collective-permute-start.13 = (s16[1040,128]{1,0:T(8,128)(2,1)S(1)}, s16[1040,128]{1,0:T(8,128)(2,1)S(1)}, u32[]{:S(2)}, u32[]{:S(2)}) collective-permute-start(s16[1040,128]{1,0:T(8,128)(2,1)S(1)} %get-tuple-element.44), channel_id=1, source_target_pairs={{0,32},{32,64},{64,96},{96,128},{128,160},{160,192},{192,224},{224... | collective-permute-start | bytes 798728 | tf_op jit(solution)/shard_map/ppermute | solution.py:405
  46.0 10.7 %collective-permute-start.12 = (s16[1040,128]{1,0:T(8,128)(2,1)S(1)}, s16[1040,128]{1,0:T(8,128)(2,1)S(1)}, u32[]{:S(2)}, u32[]{:S(2)}) collective-permute-start(s16[1040,128]{1,0:T(8,128)(2,1)S(1)} %get-tuple-element.43.refs_4_), channel_id=1, source_target_pairs={{0,224},{32,0},{64,32},{96,64},{128,96},{160,128},{192,160},{224,1... | collective-permute-start | bytes 798728 | tf_op jit(solution)/shard_map/ppermute | solution.py:405
  51.7 10.7 %collective-permute-start.17 = (s16[1040,128]{1,0:T(8,128)(2,1)S(1)}, s16[1040,128]{1,0:T(8,128)(2,1)S(1)}, u32[]{:S(2)}, u32[]{:S(2)}) collective-permute-start(s16[1040,128]{1,0:T(8,128)(2,1)S(1)} %get-tuple-element.48), channel_id=1, source_target_pairs={{0,32},{32,64},{64,96},{96,128},{128,160},{160,192},{192,224},{224... | collective-permute-start | bytes 798728 | tf_op jit(solution)/shard_map/ppermute | solution.py:405
  52.0 10.4 %collective-permute-start.16 = (s16[1040,128]{1,0:T(8,128)(2,1)S(1)}, s16[1040,128]{1,0:T(8,128)(2,1)S(1)}, u32[]{:S(2)}, u32[]{:S(2)}) collective-permute-start(s16[1040,128]{1,0:T(8,128)(2,1)S(1)} %get-tuple-element.45.refs_6_), channel_id=1, source_target_pairs={{0,224},{32,0},{64,32},{96,64},{128,96},{160,128},{192,160},{224,1... | collective-permute-start | bytes 798728 | tf_op jit(solution)/shard_map/ppermute | solution.py:405
  59.5 14.1 %collective-permute-start.15 = (s16[2064,128]{1,0:T(8,128)(2,1)S(1)}, s16[2064,128]{1,0:T(8,128)(2,1)S(1)}, u32[]{:S(2)}, u32[]{:S(2)}) collective-permute-start(s16[2064,128]{1,0:T(8,128)(2,1)S(1)} %get-tuple-element.47), channel_id=1, source_target_pairs={{0,32},{32,64},{64,96},{96,128},{128,160},{160,192},{192,224},{224... | collective-permute-start | bytes 1585160 | tf_op jit(solution)/shard_map/ppermute | solution.py:405
  59.6 14.0 %collective-permute-start.14 = (s16[2064,128]{1,0:T(8,128)(2,1)S(1)}, s16[2064,128]{1,0:T(8,128)(2,1)S(1)}, u32[]{:S(2)}, u32[]{:S(2)}) collective-permute-start(s16[2064,128]{1,0:T(8,128)(2,1)S(1)} %get-tuple-element.46.refs_6_), channel_id=1, source_target_pairs={{0,224},{32,0},{64,32},{96,64},{128,96},{160,128},{192,160},{224,1... | collective-permute-start | bytes 1585160 | tf_op jit(solution)/shard_map/ppermute | solution.py:405
  65.2 19.7 %collective-permute-start.21 = (s16[2064,128]{1,0:T(8,128)(2,1)S(1)}, s16[2064,128]{1,0:T(8,128)(2,1)S(1)}, u32[]{:S(2)}, u32[]{:S(2)}) collective-permute-start(s16[2064,128]{1,0:T(8,128)(2,1)S(1)} %get-tuple-element.52), channel_id=1, source_target_pairs={{0,32},{32,64},{64,96},{96,128},{128,160},{160,192},{192,224},{224... | collective-permute-start | bytes 1585160 | tf_op jit(solution)/shard_map/ppermute | solution.py:405
  65.3 19.6 %collective-permute-start.20 = (s16[2064,128]{1,0:T(8,128)(2,1)S(1)}, s16[2064,128]{1,0:T(8,128)(2,1)S(1)}, u32[]{:S(2)}, u32[]{:S(2)}) collective-permute-start(s16[2064,128]{1,0:T(8,128)(2,1)S(1)} %get-tuple-element.49.refs_6_), channel_id=1, source_target_pairs={{0,224},{32,0},{64,32},{96,64},{128,96},{160,128},{192,160},{224,1... | collective-permute-start | bytes 1585160 | tf_op jit(solution)/shard_map/ppermute | solution.py:405
  76.4 19.8 %collective-permute-start.19 = (s16[2064,128]{1,0:T(8,128)(2,1)S(1)}, s16[2064,128]{1,0:T(8,128)(2,1)S(1)}, u32[]{:S(2)}, u32[]{:S(2)}) collective-permute-start(s16[2064,128]{1,0:T(8,128)(2,1)S(1)} %get-tuple-element.51), channel_id=1, source_target_pairs={{0,32},{32,64},{64,96},{96,128},{128,160},{160,192},{192,224},{224... | collective-permute-start | bytes 1585160 | tf_op jit(solution)/shard_map/ppermute | solution.py:405
  77.1 19.1 %collective-permute-start.18 = (s16[2064,128]{1,0:T(8,128)(2,1)S(1)}, s16[2064,128]{1,0:T(8,128)(2,1)S(1)}, u32[]{:S(2)}, u32[]{:S(2)}) collective-permute-start(s16[2064,128]{1,0:T(8,128)(2,1)S(1)} %get-tuple-element.50.refs_6_), channel_id=1, source_target_pairs={{0,224},{32,0},{64,32},{96,64},{128,96},{160,128},{192,160},{224,1... | collective-permute-start | bytes 1585160 | tf_op jit(solution)/shard_map/ppermute | solution.py:405
  87.7 19.8 %collective-permute-start.25 = (s16[2064,128]{1,0:T(8,128)(2,1)S(1)}, s16[2064,128]{1,0:T(8,128)(2,1)S(1)}, u32[]{:S(2)}, u32[]{:S(2)}) collective-permute-start(s16[2064,128]{1,0:T(8,128)(2,1)S(1)} %get-tuple-element.56), channel_id=1, source_target_pairs={{0,32},{32,64},{64,96},{96,128},{128,160},{160,192},{192,224},{224... | collective-permute-start | bytes 1585160 | tf_op jit(solution)/shard_map/ppermute | solution.py:405
  88.4 19.2 %collective-permute-start.24 = (s16[2064,128]{1,0:T(8,128)(2,1)S(1)}, s16[2064,128]{1,0:T(8,128)(2,1)S(1)}, u32[]{:S(2)}, u32[]{:S(2)}) collective-permute-start(s16[2064,128]{1,0:T(8,128)(2,1)S(1)} %get-tuple-element.53.refs_6_), channel_id=1, source_target_pairs={{0,224},{32,0},{64,32},{96,64},{128,96},{160,128},{192,160},{224,1... | collective-permute-start | bytes 1585160 | tf_op jit(solution)/shard_map/ppermute | solution.py:405
  99.1 19.8 %collective-permute-start.23 = (s16[2064,128]{1,0:T(8,128)(2,1)S(1)}, s16[2064,128]{1,0:T(8,128)(2,1)S(1)}, u32[]{:S(2)}, u32[]{:S(2)}) collective-permute-start(s16[2064,128]{1,0:T(8,128)(2,1)S(1)} %get-tuple-element.55), channel_id=1, source_target_pairs={{0,32},{32,64},{64,96},{96,128},{128,160},{160,192},{192,224},{224... | collective-permute-start | bytes 1585160 | tf_op jit(solution)/shard_map/ppermute | solution.py:405
  99.7 19.1 %collective-permute-start.22 = (s16[2064,128]{1,0:T(8,128)(2,1)S(1)}, s16[2064,128]{1,0:T(8,128)(2,1)S(1)}, u32[]{:S(2)}, u32[]{:S(2)}) collective-permute-start(s16[2064,128]{1,0:T(8,128)(2,1)S(1)} %get-tuple-element.54.unused), channel_id=1, source_target_pairs={{0,224},{32,0},{64,32},{96,64},{128,96},{160,128},{192,160},{224,1... | collective-permute-start | bytes 1585160 | tf_op jit(solution)/shard_map/ppermute | solution.py:405
  110.4 19.8 %collective-permute-start.29 = (s16[2064,128]{1,0:T(8,128)(2,1)S(1)}, s16[2064,128]{1,0:T(8,128)(2,1)S(1)}, u32[]{:S(2)}, u32[]{:S(2)}) collective-permute-start(s16[2064,128]{1,0:T(8,128)(2,1)S(1)} %get-tuple-element.60), channel_id=1, source_target_pairs={{0,32},{32,64},{64,96},{96,128},{128,160},{160,192},{192,224},{224... | collective-permute-start | bytes 1585160 | tf_op jit(solution)/shard_map/ppermute | solution.py:405
  111.2 18.9 %collective-permute-start.28 = (s16[2064,128]{1,0:T(8,128)(2,1)S(1)}, s16[2064,128]{1,0:T(8,128)(2,1)S(1)}, u32[]{:S(2)}, u32[]{:S(2)}) collective-permute-start(s16[2064,128]{1,0:T(8,128)(2,1)S(1)} %get-tuple-element.57.unused), channel_id=1, source_target_pairs={{0,224},{32,0},{64,32},{96,64},{128,96},{160,128},{192,160},{224,1... | collective-permute-start | bytes 1585160 | tf_op jit(solution)/shard_map/ppermute | solution.py:405
  119.3 10.8 %collective-permute-start.30 = (s16[2,272,128]{2,1,0:T(8,128)(2,1)S(1)}, s16[2,272,128]{2,1,0:T(8,128)(2,1)S(1)}, u32[]{:S(2)}, u32[]{:S(2)}) collective-permute-start(s16[2,272,128]{2,1,0:T(8,128)(2,1)S(1)} %get-tuple-element.61), channel_id=1, source_target_pairs={{0,2},{1,3},{2,4},{3,5},{4,6},{5,7},{6,0},{7,1},{8,10},{9,11},{10,... | collective-permute-start | bytes 417800 | tf_op jit(solution)/shard_map/ppermute | solution.py:405
  119.4 14.0 %collective-permute-start.27 = (s16[2,272,128]{2,1,0:T(8,128)(2,1)S(1)}, s16[2,272,128]{2,1,0:T(8,128)(2,1)S(1)}, u32[]{:S(2)}, u32[]{:S(2)}) collective-permute-start(s16[2,272,128]{2,1,0:T(8,128)(2,1)S(1)} %get-tuple-element.59), channel_id=1, source_target_pairs={{0,6},{1,7},{2,0},{3,1},{4,2},{5,3},{6,4},{7,5},{8,14},{9,15},{10,... | collective-permute-start | bytes 417800 | tf_op jit(solution)/shard_map/ppermute | solution.py:405
  122.1 11.3 %collective-permute-start.26 = (s16[2,528,128]{2,1,0:T(8,128)(2,1)S(1)}, s16[2,528,128]{2,1,0:T(8,128)(2,1)S(1)}, u32[]{:S(2)}, u32[]{:S(2)}) collective-permute-start(s16[2,528,128]{2,1,0:T(8,128)(2,1)S(1)} %get-tuple-element.58), channel_id=1, source_target_pairs={{0,4},{1,5},{2,6},{3,7},{4,0},{5,1},{6,2},{7,3},{8,12},{9,13},{10,... | collective-permute-start | bytes 811016 | tf_op jit(solution)/shard_map/ppermute | solution.py:405
  130.6 6.6 %collective-permute-start.31 = (s16[2,272,128]{2,1,0:T(8,128)(2,1)S(1)}, s16[2,272,128]{2,1,0:T(8,128)(2,1)S(1)}, u32[]{:S(2)}, u32[]{:S(2)}) collective-permute-start(s16[2,272,128]{2,1,0:T(8,128)(2,1)S(1)} %get-tuple-element.66), channel_id=1, source_target_pairs={{0,2},{1,3},{2,4},{3,5},{4,6},{5,7},{6,0},{7,1},{8,10},{9,11},{10,... | collective-permute-start | bytes 417800 | tf_op jit(solution)/shard_map/ppermute | solution.py:405
  130.7 6.5 %collective-permute-start.32 = (s16[2,272,128]{2,1,0:T(8,128)(2,1)S(1)}, s16[2,272,128]{2,1,0:T(8,128)(2,1)S(1)}, u32[]{:S(2)}, u32[]{:S(2)}) collective-permute-start(s16[2,272,128]{2,1,0:T(8,128)(2,1)S(1)} %get-tuple-element.67), channel_id=1, source_target_pairs={{0,6},{1,7},{2,0},{3,1},{4,2},{5,3},{6,4},{7,5},{8,14},{9,15},{10,... | collective-permute-start | bytes 417800 | tf_op jit(solution)/shard_map/ppermute | solution.py:405
  133.5 5.4 %collective-permute-start.33 = (s16[1072,128]{1,0:T(8,128)(2,1)S(1)}, s16[1072,128]{1,0:T(8,128)(2,1)S(1)}, u32[]{:S(2)}, u32[]{:S(2)}) collective-permute-start(s16[1072,128]{1,0:T(8,128)(2,1)S(1)} %pad_add_fusion), channel_id=1, source_target_pairs={{0,1},{1,0},{2,3},{3,2},{4,5},{5,4},{6,7},{7,6},{8,9},{9,8},{10,11... | collective-permute-start | bytes 823304 | tf_op jit(solution)/shard_map/ppermute | solution.py:420
  137.3 3.0 %collective-permute-start.34 = (s16[544,128]{1,0:T(8,128)(2,1)S(1)}, s16[544,128]{1,0:T(8,128)(2,1)S(1)}, u32[]{:S(2)}, u32[]{:S(2)}) collective-permute-start(s16[544,128]{1,0:T(8,128)(2,1)S(1)} %pad_add_fusion.1), channel_id=1, source_target_pairs={{0,1},{1,0},{2,3},{3,2},{4,5},{5,4},{6,7},{7,6},{8,9},{9,8},{10,11... | collective-permute-start | bytes 417800 | tf_op jit(solution)/shard_map/ppermute | solution.py:420
  138.8 1.5 %collective-permute-start.35 = (s16[528,128]{1,0:T(8,128)(2,1)S(1)}, s16[528,128]{1,0:T(8,128)(2,1)S(1)}, u32[]{:S(2)}, u32[]{:S(2)}) collective-permute-start(s16[528,128]{1,0:T(8,128)(2,1)S(1)} %get-tuple-element.72), channel_id=1, source_target_pairs={{0,1},{1,0},{2,3},{3,2},{4,5},{5,4},{6,7},{7,6},{8,9},{9,8},{10,11... | collective-permute-start | bytes 405512 | tf_op jit(solution)/shard_map/ppermute | solution.py:420
